TPU v7x, 32 devices: a whole 2x2x4 slice. The times are simulated.
32 devices in a mesh: grp: 2 (over y), ka: 4 (over z), pb: 4 (over x, core).
Axes of the slice: x: 2, y: 2, z: 4, core: 2. Of those that a mesh axis runs over, the one named last changes fastest.
Arguments:
- kpoint_coords: float32 [3, 128], P(None, ('grp', 'ka')), parts along dimension 1, may hold values from 0 to 1
- g_wannier: bfloat16 [8, 8, 192000], P(('grp', 'pb'), None, 'ka'), parts along dimension 0, may hold values from -0.0234375 to 0.0234375
- mode_vectors: bfloat16 [8, 2, 60, 60], P(('grp', 'pb')), parts along dimension 0, may hold values from -0.5 to 0.5
- frequencies: float32 [8, 60], P(('grp', 'pb')), parts along dimension 0, may hold values from 0.02 to 0.2
- rotations: bfloat16 [128, 3200], P(('grp', 'ka')), parts along dimension 0, may hold values from -0.625 to 0.625
- energies: bfloat16 [128, 40], P(('grp', 'ka')), parts along dimension 0, may hold values from -0.29882812 to 0.29882812
- band_window: int32 [2, 128], P(None, ('grp', 'ka')), parts along dimension 1, may hold values from 0 to 40, as said below
- target_owner: int32 [8, 64, 1], P(('grp', 'pb'), 'ka'), parts along dimension 0, may hold values from 0 to 3; in each aligned block of 16 rows (0 to 15, 16 to 31, ..., all dimensions but the last counted through in order) at most 8 rows name the same one
- target_row: int32 [8, 64], P(('grp', 'pb'), 'ka'), parts along dimension 0, may hold values from 0 to 15
Outputs:
- electron_width: float32 [128, 40], P(('grp', 'ka')), parts along dimension 0
- phonon_width: float32 [8, 60], P(('grp', 'pb')), parts along dimension 0
There are 2 independent parts, one for each index of `grp`. A program takes and returns all parts, laid end to end along the dimension named above; each array names one. Nothing has to cross between parts.
Inputs may be any that keep to these rules, and one draw needn't show every extreme that they name: `target_owner`: among the 16 pairs of one device (one q point, one block of k points), no owner index is named more than 8 times; in every draw some device's pairs name one owner exactly 8 times. `band_window`: row 0 is the first band of a k point's window and row 1 one past its last; every window holds at least half of the bands, and some k point's window holds all of them.
All inputs are finite; a program needn't handle non-finite values.
Results may differ from a plain program's by a relative error of at most 0.0014.
Values may be sent and summed in bfloat16 or wider, within the bound.
A program may use at most 256 MiB of HBM per device.

v0:
```python
import math

import jax
import jax.numpy as jnp
from jax import lax
from jax.sharding import PartitionSpec as P

THERMAL_KELVIN = 0.1
SMEARING_WIDTH = 0.05


def window_mask(band_window, bands):
    energy_levels = jnp.arange(bands, dtype=jnp.int32)
    inside = (energy_levels[None, :] >= band_window[0][:, None]) & (
        energy_levels[None, :] < band_window[1][:, None]
    )
    return inside.astype(jnp.float32)


def phases_of(coords, vectors):
    index = jnp.arange(vectors, dtype=jnp.int32)
    first = (index % 2).astype(jnp.float32)
    second = (index // 2 % 2).astype(jnp.float32)
    third = (index // 4 % 2).astype(jnp.float32)
    angle = coords[0][:, None] * first[None, :] + coords[1][:, None] * second[None, :]
    angle = 2.0 * math.pi * (angle + coords[2][:, None] * third[None, :])
    return jnp.concatenate([jnp.cos(angle), jnp.sin(angle)], 0).astype(jnp.bfloat16)


def lorentz(value):
    return SMEARING_WIDTH / math.pi / (value * value + SMEARING_WIDTH * SMEARING_WIDTH)


def occupation(energy_value):
    return 1.0 / (1.0 + jnp.exp(energy_value / THERMAL_KELVIN))


def pair_terms(
    fourier_sum,
    mode_pair,
    phonon_frequency,
    rot_here,
    eps_here,
    mask_here,
    rot_there,
    eps_there,
    mask_there,
    count_q,
    count_k,
):
    real_part = fourier_sum[0, :, 0] - fourier_sum[1, :, 1]
    imag_part = fourier_sum[1, :, 0] + fourier_sum[0, :, 1]
    wannier = jnp.stack([real_part, imag_part]).astype(jnp.bfloat16)
    mode_re = mode_pair[0]
    mode_im = mode_pair[1]
    mode_block = jnp.stack([jnp.stack([mode_re, mode_im], -1), jnp.stack([-mode_im, mode_re], -1)])
    modal = jnp.einsum(
        "ckmab,cmvd->dkvab", wannier, mode_block, preferred_element_type=jnp.float32
    ).astype(jnp.bfloat16)
    right_re = rot_here[:, 0]
    right_im = rot_here[:, 1]
    right = jnp.stack(
        [jnp.stack([right_re, right_im], -1), jnp.stack([-right_im, right_re], -1)], 1
    )
    half = jnp.einsum(
        "ckvab,kcbnd->dkvan", modal, right, preferred_element_type=jnp.float32
    ).astype(jnp.bfloat16)
    left_re = rot_there[:, 0]
    left_im = rot_there[:, 1]
    left = jnp.stack([jnp.stack([left_re, -left_im], -1), jnp.stack([left_im, left_re], -1)], 1)
    coupling = jnp.einsum("ckvan,kcamd->dkvmn", half, left, preferred_element_type=jnp.float32)
    strength = coupling[0] * coupling[0] + coupling[1] * coupling[1]
    e_here = eps_here.astype(jnp.float32)
    e_there = eps_there.astype(jnp.float32)
    gap = e_here[:, None, :] - e_there[:, :, None]
    bose_einstein_factor = 1.0 / (jnp.exp(phonon_frequency / THERMAL_KELVIN) - 1.0)
    occ_here = occupation(e_here)
    occ_there = occupation(e_there)
    shifted = phonon_frequency[None, :, None, None]
    upward = lorentz(gap[:, None] + shifted)
    descending_transition = lorentz(gap[:, None] - shifted)
    bose_wide = bose_einstein_factor[None, :, None, None]
    occ_wide = occ_there[:, None, :, None]
    emission = (bose_wide + occ_wide) * upward + (
        bose_wide + 1.0 - occ_wide
    ) * descending_transition
    weighted = strength * (mask_here[:, None, :] * mask_there[:, :, None])[:, None]
    self_part = jnp.sum(weighted * emission, axis=(1, 2)) / count_q
    change = occ_here[:, None, None, :] - occ_wide
    width_part = 2.0 * math.pi / count_k * jnp.sum(weighted * change * upward, axis=(0, 2, 3))
    return (self_part, width_part)


def grouped_terms(
    fourier_sum,
    mode_pair,
    phonon_frequency,
    rot_here,
    eps_here,
    mask_here,
    rot_there,
    eps_there,
    mask_there,
    count_q,
    count_k,
):
    local_k = rot_here.shape[0]
    group = 16
    groups = local_k // group
    fourier_groups = jnp.moveaxis(
        fourier_sum.reshape((2, groups, group) + fourier_sum.shape[2:]), 1, 0
    )

    def split(array):
        return array.reshape((groups, group) + array.shape[1:])

    def one_group(items):
        return pair_terms(
            items[0],
            mode_pair,
            phonon_frequency,
            items[1],
            items[2],
            items[3],
            items[4],
            items[5],
            items[6],
            count_q,
            count_k,
        )

    self_part, width_part = lax.map(
        one_group,
        (
            fourier_groups,
            split(rot_here),
            split(eps_here),
            split(mask_here),
            split(rot_there),
            split(eps_there),
            split(mask_there),
        ),
    )
    return (self_part.reshape(local_k, -1), jnp.sum(width_part, 0))


def shards(
    kpoint_coords,
    g_wannier,
    mode_vectors,
    frequencies,
    rotations,
    energies,
    band_window,
    target_owner,
    target_row,
):
    local_k = rotations.shape[0]
    bands = energies.shape[1]
    modes = frequencies.shape[1]
    ka_size = lax.axis_size("ka")
    pb_size = lax.axis_size("pb")
    total_k = local_k * ka_size
    phases = phases_of(kpoint_coords, g_wannier.shape[1])
    fourier_sum = jnp.dot(
        phases,
        lax.all_gather(g_wannier, "ka", axis=2, tiled=True)[0],
        preferred_element_type=jnp.float32,
    )
    fourier_sum = fourier_sum.reshape(2, local_k, 2, modes, bands, bands)
    mask_here = window_mask(band_window, bands)
    outgoing_mask = mask_here.astype(jnp.bfloat16)
    owner = target_owner[0, :, 0]
    row_of = target_row[0]
    gathered = (
        lax.all_gather(rotations, "ka", axis=0, tiled=True),
        lax.all_gather(energies, "ka", axis=0, tiled=True),
        lax.all_gather(outgoing_mask, "ka", axis=0, tiled=True),
    )
    wanted = owner * local_k + row_of
    choose = (wanted[:, None] == jnp.arange(total_k, dtype=jnp.int32)[None, :]).astype(jnp.bfloat16)
    fetched = [
        jnp.dot(choose, member, preferred_element_type=jnp.float32).astype(jnp.bfloat16)
        for member in gathered
    ]
    rot_here = rotations.reshape(local_k, 2, bands, bands)
    rot_there = fetched[0].reshape(local_k, 2, bands, bands)
    eps_there = fetched[1]
    mask_there = fetched[2].astype(jnp.float32)
    self_part, width_part = grouped_terms(
        fourier_sum,
        mode_vectors[0],
        frequencies[0],
        rot_here,
        energies,
        mask_here,
        rot_there,
        eps_there,
        mask_there,
        pb_size,
        total_k,
    )
    electron_width = lax.psum(self_part, "pb")
    phonon_width = lax.psum(width_part, "ka")
    return (electron_width, phonon_width[None, :])


def solution(mesh):
    in_specs = (
        P(None, ("grp", "ka")),
        P(("grp", "pb"), None, "ka"),
        P(("grp", "pb"), None, None, None),
        P(("grp", "pb"), None),
        P(("grp", "ka"), None),
        P(("grp", "ka"), None),
        P(None, ("grp", "ka")),
        P(("grp", "pb"), "ka", None),
        P(("grp", "pb"), "ka"),
    )
    out_specs = (P(("grp", "ka"), None), P(("grp", "pb"), None))
    return jax.shard_map(shards, mesh=mesh, in_specs=in_specs, out_specs=out_specs, check_vma=False)
```

profile of v0, /device:TPU:0, one launch (start us, length us, event | category | flops | bytes accessed | tf_op | source)
XLA Modules:
  0.0 244.1 jit_solution(2349405333442330942)
XLA Ops:
  7.2 0.0 all-gather.2.cloned.1.call-start
  7.2 0.7 all-gather.2.cloned.1.call-update
  7.9 0.8 slice_bitcast_fusion.4
  8.7 0.1 cosine_convert_fusion
  8.8 0.1 pad_maximum_fusion.1
  8.9 0.1 convert_element_type.87
  9.0 0.9 fusion.50
  9.9 1.4 squeeze.84
  11.3 0.1 copy.68
  11.5 0.1 copy.67
  11.6 20.2 %all_gather.12 = bf16[64,3200]{1,0:T(8,128)(2,1)S(1)} all-gather(bf16[16,3200]{1,0:T(8,128)(2,1)} %param.13), channel_id=1, replica_groups=mesh['grp'=2,'ka'=4,'pb'=4] {'ka'}, dimensions={0}, use_global_device_ids=true | all-gather | bytes 512000 | tf_op jit(solution)/shard_map/all_gather | solution.py:176
  31.9 0.7 bitcast_add_fusion
  32.5 0.2 convolution_convert_fusion
  32.8 0.5 squeeze.81
  33.3 0.1 copy.66
  33.4 0.1 copy.65
  33.6 0.7 convert_element_type.98
  34.3 13.5 %all_gather.15 = bf16[64,40]{1,0:T(8,128)(2,1)S(1)} all-gather(bf16[16,40]{1,0:T(8,128)(2,1)} %param.14), channel_id=1, replica_groups=mesh['grp'=2,'ka'=4,'pb'=4] {'ka'}, dimensions={0}, use_global_device_ids=true | all-gather | bytes 6400 | tf_op jit(solution)/shard_map/all_gather | solution.py:177
  47.8 0.8 slice_bitcast_fusion.1
  48.6 0.1 fusion.33
  48.6 13.4 %all_gather.14 = bf16[64,40]{1,0:T(8,128)(2,1)S(1)} all-gather(bf16[16,40]{1,0:T(8,128)(2,1)S(1)} %get-tuple-element.69), channel_id=1, replica_groups=mesh['grp'=2,'ka'=4,'pb'=4] {'ka'}, dimensions={0}, use_global_device_ids=true | all-gather | bytes 6400 | tf_op jit(solution)/shard_map/all_gather | solution.py:178
  62.1 0.9 maximum_bitcast_fusion.6
  63.0 1.0 maximum_bitcast_fusion.4
  64.0 0.7 broadcast_add_fusion.1
  64.6 0.7 add_divide_fusion.1
  65.3 0.2 fusion.25
  65.5 0.2 add_divide_fusion.2
  65.7 0.9 broadcast_multiply_fusion
  66.6 1.0 broadcast_add_fusion
  67.6 1.1 broadcast_subtract_fusion
  68.8 8.9 %all-gather.2.cloned.1.call-done = bf16[1,8,192000]{2,1,0:T(8,128)(2,1)} async-done(((bf16[1,8,48000]{2,1,0:T(8,128)(2,1)}), bf16[1,8,192000]{2,1,0:T(8,128)(2,1)}) %all-gather.2.cloned.1.call-update) | async-done | bytes 3072016 | tf_op jit(solution)/shard_map/all_gather | solution.py:167
  77.7 6.4 %reshape.245 = bf16[1536000]{0:T(1024)(128)(2,1)S(1)} reshape(bf16[8,192000]{1,0:T(8,128)(2,1)} %bitcast.120) | data formatting | bytes 6144000
  84.1 15.8 %reshape.246 = bf16[8,2,60,40,40]{4,3,2,1,0:T(8,128)(2,1)} reshape(bf16[1536000]{0:T(1024)(128)(2,1)S(1)} %reshape.245) | data formatting | bytes 6144000
  99.9 13.0 %copy.46 = bf16[2,60,40,40,8]{1,4,3,2,0:T(8,128)(2,1)} copy(bf16[2,60,40,40,8]{3,2,1,0,4:T(8,128)(2,1)} %bitcast.119) | data formatting | bytes 6144000 | tf_op jit(solution)/shard_map/dot_general | solution.py:165
  112.8 20.4 %fusion.22 = f32[2,16,2,60,40,40]{3,1,5,4,2,0:T(8,128)} fusion(bf16[2,60,40,40,8]{1,4,3,2,0:T(8,128)(2,1)} %copy.46, bf16[2,16,8,1,1,1]{1,0,2,5,4,3:T(2,128)(2,1)S(1)} %bitcast.126), kind=kOutput, calls=%fused_computation.26 | convolution fusion | flops 98304000 | bytes 27648512 | tf_op jit(solution)/shard_map/dot_general | solution.py:165
  133.2 17.2 %fusion.20 = (bf16[1,16,60,40,40]{2,1,4,3,0:T(8,128)(2,1)S(1)}, bf16[1,16,60,40,40]{2,1,4,3,0:T(8,128)(2,1)S(1)}) fusion(f32[2,16,2,60,40,40]{3,1,5,4,2,0:T(8,128)} %fusion.22), kind=kLoop, calls=%fused_computation.24 | loop fusion | flops 6144000 | bytes 30720000 | tf_op jit(solution)/shard_map/while/body/eval_jaxpr/sub | solution.py:51
  150.4 7.0 %pad_maximum_fusion = bf16[2,16,60,40,40]{2,1,4,3,0:T(8,128)(2,1)} fusion(bf16[1,16,60,40,40]{2,1,4,3,0:T(8,128)(2,1)S(1)} %get-tuple-element.35, bf16[1,16,60,40,40]{2,1,4,3,0:T(8,128)(2,1)S(1)} %get-tuple-element.34), kind=kLoop, calls=%fused_computation.12 | loop fusion | flops 3072000 | bytes 12288000 | tf_op jit(solution)/shard_map/while/body/eval_jaxpr/stack | solution.py:53
  157.4 0.0 copy-start
  157.4 11.9 %fusion.15 = bf16[2,16,60,40,40,1]{2,4,3,1,0,5:T(8,128)(2,1)} fusion(bf16[2,16,60,40,40]{2,1,4,3,0:T(8,128)(2,1)} %pad_maximum_fusion, bf16[1,60,60,2]{2,1,0,3:T(8,128)(2,1)S(1)} %get-tuple-element.60, bf16[1,60,60,2]{2,1,0,3:T(8,128)(2,1)S(1)} %get-tuple-element.59), kind=kOutput, calls=%fused_computation.23 | convolution fusion | flops 740409600 | bytes 12316800 | tf_op jit(solution)/shard_map/while/body/eval_jaxpr/ckmab,cmvd->dkvab/dot_general | solution.py:57
  169.3 0.0 copy-done
  169.3 0.0 copy-start.1
  169.3 0.0 copy-start.2
  169.3 9.6 %fusion = bf16[2,16,60,40,40,1]{2,4,3,0,1,5:T(8,128)(2,1)} fusion(bf16[2,16,60,40,40,1]{2,4,3,1,0,5:T(8,128)(2,1)} %fusion.15, bf16[16,1,40,40,2]{2,3,1,4,0:T(8,128)(2,1)S(1)} %copy-done, bf16[16,1,40,40,2]{2,3,1,4,0:T(8,128)(2,1)S(1)} %get-tuple-element.55), kind=kOutput, calls=%fused_computation.2 | convolution fusion | flops 495001600 | bytes 12492800 | tf_op jit(solution)/shard_map/while/body/eval_jaxpr/ckvab,kcbnd->dkvan/dot_general | solution.py:65
  178.9 0.0 copy-done.1
  178.9 0.0 copy-done.2
  178.9 0.0 copy-start.3
  178.9 0.0 copy-start.4
  178.9 0.0 copy-start.5
  178.9 0.0 copy-start.6
  178.9 0.0 copy-start.7
  178.9 0.0 copy-start.8
  178.9 17.1 %fusion.12 = f32[2,16,60,40,40]{2,3,4,0,1:T(8,128)} fusion(bf16[2,16,60,40,40,1]{2,4,3,0,1,5:T(8,128)(2,1)} %fusion, bf16[16,1,40,40,2]{2,3,1,4,0:T(8,128)(2,1)S(1)} %copy-done.2, bf16[16,1,40,40,2]{2,3,1,4,0:T(8,128)(2,1)S(1)} %copy-done.1), kind=kOutput, calls=%fused_computation.22 | convolution fusion | flops 491929600 | bytes 18636800 | tf_op jit(solution)/shard_map/while/body/eval_jaxpr/ckvan,kcamd->dkvmn/dot_general | solution.py:71
  196.0 0.0 copy-done.3
  196.0 0.0 copy-done.4
  196.0 0.0 copy-done.5
  196.0 0.0 copy-done.6
  196.0 0.0 copy-done.7
  196.1 0.0 copy-done.8
  196.1 23.5 %multiply_reduce_fusion = (f32[60]{0:T(128)S(1)}, f32[16,40]{1,0:T(8,128)S(1)}) fusion(f32[16,40,40]{1,2,0:T(8,128)S(1)} %copy-done.4, f32[60]{0:T(128)S(1)} %bitcast.127, f32[16,40,40]{1,2,0:T(8,128)S(1)} %copy-done.5, f32[16,40,40]{1,2,0:T(8,128)S(1)} %copy-done.3, f32[2,16,60,40,40]{2,3,4,0,1:T(8,128)} %fusion.12, f32[16,60,40]{1,2,0:T(8,128)S(1)} %copy-done.7, ...), kind=kLoop, calls=%fused_computation.19 | loop fusion | flops 30719300 | bytes 12905440 | tf_op jit(solution)/shard_map/while/body/eval_jaxpr/reduce_sum | solution.py:90
  219.6 7.5 %psum.14 = f32[16,40]{1,0:T(8,128)} all-reduce(f32[16,40]{1,0:T(8,128)S(1)} %broadcast_multiply_fusion.1), channel_id=1, replica_groups=mesh['grp'=2,'ka'=4,'pb'=4] {'pb'}, use_global_device_ids=true, to_apply=%region_1.2 | all-reduce | flops 640 | bytes 5120 | tf_op jit(solution)/shard_map/psum | solution.py:203
  227.1 10.1 %psum.15 = f32[1,60]{1,0:T(1,128)} all-reduce(f32[1,60]{1,0:T(1,128)S(1)} %multiply_bitcast_fusion), channel_id=1, replica_groups=mesh['grp'=2,'ka'=4,'pb'=4] {'ka'}, use_global_device_ids=true, to_apply=%region_3.4 | all-reduce | flops 60 | bytes 480 | tf_op jit(solution)/shard_map/psum | solution.py:204
  (11 shorter events, 0.2 us)
Async XLA Ops:
  7.2 70.5 %all-gather.2.cloned.1.call-start = ((), (), s32[]{:S(2)}) async-start(), calls=%async_computation | async-start | bytes 3840000 | tf_op jit(solution)/shard_map/all_gather | solution.py:167
  157.4 11.9 %copy-start = (bf16[16,1,40,40,2]{2,3,1,4,0:T(8,128)(2,1)S(1)}, bf16[16,1,40,40,2]{2,3,1,4,0:T(8,128)(2,1)}, u32[]{:S(2)}) copy-start(bf16[16,1,40,40,2]{2,3,1,4,0:T(8,128)(2,1)} %get-tuple-element.56) | copy-start | bytes 307204
  169.3 9.6 %copy-start.1 = (bf16[16,1,40,40,2]{2,3,1,4,0:T(8,128)(2,1)S(1)}, bf16[16,1,40,40,2]{2,3,1,4,0:T(8,128)(2,1)}, u32[]{:S(2)}) copy-start(bf16[16,1,40,40,2]{2,3,1,4,0:T(8,128)(2,1)} %get-tuple-element.53) | copy-start | bytes 307204
  169.3 9.6 %copy-start.2 = (bf16[16,1,40,40,2]{2,3,1,4,0:T(8,128)(2,1)S(1)}, bf16[16,1,40,40,2]{2,3,1,4,0:T(8,128)(2,1)}, u32[]{:S(2)}) copy-start(bf16[16,1,40,40,2]{2,3,1,4,0:T(8,128)(2,1)} %get-tuple-element.54) | copy-start | bytes 307204
  178.9 17.2 %copy-start.3 = (f32[16,40,40]{1,2,0:T(8,128)S(1)}, f32[16,40,40]{1,2,0:T(8,128)}, u32[]{:S(2)}) copy-start(f32[16,40,40]{1,2,0:T(8,128)} %broadcast_multiply_fusion) | copy-start | bytes 307204
  178.9 17.2 %copy-start.4 = (f32[16,40,40]{1,2,0:T(8,128)S(1)}, f32[16,40,40]{1,2,0:T(8,128)}, u32[]{:S(2)}) copy-start(f32[16,40,40]{1,2,0:T(8,128)} %get-tuple-element.74) | copy-start | bytes 307204
  178.9 17.2 %copy-start.5 = (f32[16,40,40]{1,2,0:T(8,128)S(1)}, f32[16,40,40]{1,2,0:T(8,128)}, u32[]{:S(2)}) copy-start(f32[16,40,40]{1,2,0:T(8,128)} %get-tuple-element.75) | copy-start | bytes 307204
  178.9 17.2 %copy-start.6 = (f32[16,60,40]{1,2,0:T(8,128)S(1)}, f32[16,60,40]{1,2,0:T(8,128)}, u32[]{:S(2)}) copy-start(f32[16,60,40]{1,2,0:T(8,128)} %get-tuple-element.61) | copy-start | bytes 460804
  178.9 17.2 %copy-start.7 = (f32[16,60,40]{1,2,0:T(8,128)S(1)}, f32[16,60,40]{1,2,0:T(8,128)}, u32[]{:S(2)}) copy-start(f32[16,60,40]{1,2,0:T(8,128)} %get-tuple-element.62) | copy-start | bytes 460804
  178.9 17.2 %copy-start.8 = (f32[1,60]{1,0:T(1,128)S(1)}, f32[1,60]{1,0:T(1,128)}, u32[]{:S(2)}) copy-start(f32[1,60]{1,0:T(1,128)} %param.12) | copy-start | bytes 724
Sparse Core Ops, SparseCore 0:
  9.6 68.0 all-gather.1
where the time goes:
time: 245 us; the launch traced here: 244 us
  blocking collectives  64.8 us (26%)
  matrix products  59.5 us (24%)
  other arithmetic  55.6 us (23%)
  local copies, waits for them, and re-layouts  40.2 us (16%)
  between operations  14.2 us (6%)
  waiting for transfers between devices  9.58 us (4%)
    reduce_sum x1, other arithmetic, pair_terms(): jnp.sum(weighted * change * upward, axis=(0, 2, 3))  23.5 us
    unnamed x25, local copies, waits for them, and re-layouts  22.8 us
    dot_general x1, matrix products, shards(): jnp.dot(phases, lax.all_gather(g_wannier, 'ka', axis=2, tiled=True)[0], p...  20.4 us
    all_gather x1, blocking collectives, shards(): lax.all_gather(rotations, 'ka', axis=0, tiled=True)  20.2 us
    sub x1, other arithmetic, pair_terms(): real_part = fourier_sum[0, :, 0] - fourier_sum[1, :, 1]  17.2 us
    dot_general x1, matrix products, pair_terms(): jnp.einsum('ckvan,kcamd->dkvmn', half, left, preferred_element_type=jnp.f...  17.1 us
    all_gather x1, blocking collectives, shards(): lax.all_gather(energies, 'ka', axis=0, tiled=True)  13.5 us
    all_gather x1, blocking collectives, shards(): lax.all_gather(outgoing_mask, 'ka', axis=0, tiled=True)  13.4 us
  transfers between devices with their start and end apart: 1, of which 1 were waited for; matrix products, arithmetic and copies ran while one was open for 6% of the time, Pallas kernels for 0%

commit v1 on v0

v1 whole, which is shorter than its diff:
```python
import functools
import math

import jax
import jax.numpy as jnp
from jax import lax
from jax.experimental import pallas as pl
from jax.experimental.pallas import tpu as pltpu
from jax.sharding import PartitionSpec as P

THERMAL_KELVIN = 0.1
SMEARING_WIDTH = 0.05
LANES = 128
HALF = 64


def window_mask(band_window, bands):
    energy_levels = jnp.arange(bands, dtype=jnp.int32)
    inside = (energy_levels[None, :] >= band_window[0][:, None]) & (
        energy_levels[None, :] < band_window[1][:, None]
    )
    return inside.astype(jnp.float32)


def phases_of(coords, vectors):
    index = jnp.arange(vectors, dtype=jnp.int32)
    first = (index % 2).astype(jnp.float32)
    second = (index // 2 % 2).astype(jnp.float32)
    third = (index // 4 % 2).astype(jnp.float32)
    angle = coords[0][:, None] * first[None, :] + coords[1][:, None] * second[None, :]
    angle = 2.0 * math.pi * (angle + coords[2][:, None] * third[None, :])
    return jnp.concatenate([jnp.cos(angle), jnp.sin(angle)], 0).astype(jnp.bfloat16)


def occupation(energy_value):
    return 1.0 / (1.0 + jnp.exp(energy_value / THERMAL_KELVIN))


def pair_kernel(
    g_ref, w_ref, right_ref, left_ref, e_ref, up_ref, mask_ref, shift_ref, gain_ref, occ_ref, keep_ref,
    self_ref, width_ref, turned, modal, half, *, modes, bands
):
    area = bands * bands
    vectors = g_ref.shape[0]
    blocks = 2 * area // LANES
    per = LANES // vectors
    step = pl.program_id(0)

    @pl.when(step == 0)
    def _():
        width_ref[...] = jnp.zeros_like(width_ref)

        def turn(j, carry):
            for group in range(turned.shape[1] // LANES):
                rows = []
                for p in range(group * per, group * per + per):
                    if p < modes:
                        at = pl.multiple_of(p * 2 * area + j * LANES, LANES)
                        rows.append(g_ref[:, pl.ds(at, LANES)].astype(jnp.float32))
                    else:
                        rows.append(jnp.zeros((vectors, LANES), jnp.float32))
                tile = jnp.concatenate(rows, 0).T
                spot = pl.ds(pl.multiple_of(j * LANES, LANES), LANES)
                turned[spot, group * LANES : (group + 1) * LANES] = tile.astype(jnp.bfloat16)
            return carry

        lax.fori_loop(0, blocks, turn, 0)

    chunk = 8 * bands

    for c in range(area // chunk):
        first = c * chunk
        both = jnp.dot(turned[first : first + chunk, :], w_ref[0], preferred_element_type=jnp.float32)
        both += jnp.dot(
            turned[area + first : area + first + chunk, :], w_ref[1], preferred_element_type=jnp.float32
        )
        for kk in range(2):
            modal[kk, first : first + chunk, :] = both[:, kk * LANES : (kk + 1) * LANES]

    lane = lax.broadcasted_iota(jnp.int32, (bands, LANES), 1)
    sign = jnp.where(lane < HALF, -1.0, 1.0)

    def operand(block):
        block = jnp.concatenate([block, pltpu.roll(block, HALF, 1) * sign], 0)
        return block.astype(jnp.bfloat16)

    def one_k(kk, carry):
        k = step * 2 + kk
        right = right_ref[kk]
        for a in range(0, bands, 2):
            pair = [operand(modal[kk, (a + s) * bands : (a + s + 1) * bands, :]) for s in range(2)]
            out = jnp.dot(right, jnp.concatenate(pair, 1), preferred_element_type=jnp.float32)
            for s in range(2):
                half[pl.ds(a + s, bands, stride=bands), :] = out[:, s * LANES : (s + 1) * LANES]
        left = left_ref[kk]
        shift = shift_ref[kk]
        gain = gain_ref[kk]
        occ = occ_ref[kk]
        total = jnp.zeros((bands, LANES), jnp.float32)
        for n in range(0, bands, 2):
            pair = [operand(half[(n + s) * bands : (n + s + 1) * bands, :]) for s in range(2)]
            out = jnp.dot(left, jnp.concatenate(pair, 1), preferred_element_type=jnp.float32)
            for s in range(2):
                coupling = out[:, s * LANES : (s + 1) * LANES]
                square = coupling * coupling
                strength = square + pltpu.roll(square, HALF, 1)
                x = shift + e_ref[k, n + s]
                term = strength / (x * x + SMEARING_WIDTH * SMEARING_WIDTH)
                self_ref[kk, n + s : n + s + 1, :] = jnp.sum(term * gain, 0, keepdims=True)
                total += term * (up_ref[k, n + s] - mask_ref[k, n + s] * occ)
        width_ref[...] += total * keep_ref[kk]
        return carry

    lax.fori_loop(0, 2, one_k, 0)


def pair_sums(g, weights, right, left, e_here, up_here, mask_here, shift, gain, occ, keep, modes, bands):
    local_k = right.shape[0]
    depth = weights.shape[1]
    area = bands * bands
    by_k = lambda i: (i, 0, 0)
    table = pl.BlockSpec((2, bands, LANES), by_k)
    return pl.pallas_call(
        functools.partial(pair_kernel, modes=modes, bands=bands),
        grid=(local_k // 2,),
        in_specs=[
            pl.BlockSpec(g.shape, lambda i: (0, 0)),
            pl.BlockSpec((2, depth, 2 * LANES), lambda i: (0, 0, i)),
            pl.BlockSpec((2,) + right.shape[1:], by_k),
            pl.BlockSpec((2,) + left.shape[1:], by_k),
            pl.BlockSpec(memory_space=pltpu.SMEM),
            pl.BlockSpec(memory_space=pltpu.SMEM),
            pl.BlockSpec(memory_space=pltpu.SMEM),
            table,
            table,
            table,
            table,
        ],
        out_specs=[table, pl.BlockSpec((bands, LANES), lambda i: (0, 0))],
        out_shape=[
            jax.ShapeDtypeStruct((local_k, bands, LANES), jnp.float32),
            jax.ShapeDtypeStruct((bands, LANES), jnp.float32),
        ],
        scratch_shapes=[
            pltpu.VMEM((2 * area, depth), jnp.bfloat16),
            pltpu.VMEM((2, area, LANES), jnp.float32),
            pltpu.VMEM((area, LANES), jnp.float32),
        ],
        compiler_params=pltpu.CompilerParams(vmem_limit_bytes=48 * 1024 * 1024),
        name="pairs",
    )(g, weights, right, left, e_here, up_here, mask_here, shift, gain, occ, keep)


def lanes_of(first, second):
    pad = [(0, 0)] * (first.ndim - 1) + [(0, HALF - first.shape[-1])]
    return jnp.concatenate([jnp.pad(first, pad), jnp.pad(second, pad)], -1)


def weights_of(phases, mode_pair):
    _, local_k, vectors = phases.shape
    modes = mode_pair.shape[1]
    wave = phases.astype(jnp.float32)
    vec = mode_pair.astype(jnp.float32).reshape(2, modes // 2, 2, modes)
    vec = jnp.transpose(vec, (0, 2, 1, 3))[:, :, :, None, None, :]
    cos, sin = (jnp.transpose(w)[None, None, :, :, None] for w in (wave[0], wave[1]))
    real = cos * vec[0] - sin * vec[1]
    imag = cos * vec[1] + sin * vec[0]
    both = jnp.stack([lanes_of(real, imag), lanes_of(-imag, real)], 1).astype(jnp.bfloat16)
    both = both.reshape(2, modes * vectors, local_k * LANES)
    depth = -(-modes * vectors // LANES) * LANES
    return jnp.pad(both, ((0, 0), (0, depth - modes * vectors), (0, 0)))


def shards(
    kpoint_coords,
    g_wannier,
    mode_vectors,
    frequencies,
    rotations,
    energies,
    band_window,
    target_owner,
    target_row,
):
    local_k = rotations.shape[0]
    bands = energies.shape[1]
    modes = frequencies.shape[1]
    vectors = g_wannier.shape[1]
    total_k = local_k * lax.axis_size("ka")
    g = lax.all_gather(g_wannier, "ka", axis=2, tiled=True)[0]
    mask_here = window_mask(band_window, bands)
    packed = jnp.concatenate([rotations, energies, mask_here.astype(jnp.bfloat16)], 1)
    gathered = lax.all_gather(packed, "ka", axis=0, tiled=True)
    wanted = target_owner[0, :, 0] * local_k + target_row[0]
    choose = (wanted[:, None] == jnp.arange(total_k, dtype=jnp.int32)[None, :]).astype(jnp.bfloat16)
    fetched = jnp.dot(choose, gathered, preferred_element_type=jnp.float32)
    size = 2 * bands * bands
    rot_there = fetched[:, :size].astype(jnp.bfloat16).reshape(local_k, 2, bands, bands)
    e_there = fetched[:, size : size + bands]
    mask_there = fetched[:, size + bands :]

    weights = weights_of(
        phases_of(kpoint_coords, vectors).reshape(2, local_k, vectors), mode_vectors[0]
    )
    rot_here = rotations.reshape(local_k, 2, bands, bands)
    right = jnp.transpose(rot_here, (0, 3, 1, 2)).reshape(local_k, bands, 2 * bands)
    left = jnp.stack([rot_there[:, 0], -rot_there[:, 1]], 1)
    left = jnp.transpose(left, (0, 3, 1, 2)).reshape(local_k, bands, 2 * bands)

    e_here = energies.astype(jnp.float32)
    occ_here = occupation(e_here)
    occ_there = jnp.broadcast_to(occupation(e_there)[:, :, None], (local_k, bands, LANES))
    keep = jnp.broadcast_to(mask_there[:, :, None], (local_k, bands, LANES))
    frequency = frequencies[0]
    bose = 1.0 / (jnp.exp(frequency / THERMAL_KELVIN) - 1.0)
    ones = jnp.ones_like(bose)
    shift = lanes_of(frequency, -frequency)[None, None, :] - e_there[:, :, None]
    gain = keep * (lanes_of(bose, bose + 1.0) + lanes_of(ones, -ones) * occ_there)
    self_lanes, width_lanes = pair_sums(
        g, weights, right, left, e_here, occ_here * mask_here, mask_here, shift, gain, occ_there, keep, modes, bands
    )
    scale = SMEARING_WIDTH / math.pi
    self_part = jnp.sum(self_lanes, 2) * mask_here * (scale / lax.axis_size("pb"))
    width_part = jnp.sum(width_lanes, 0)[:modes] * (2.0 * math.pi / total_k * scale)
    electron_width = lax.psum(self_part, "pb")
    phonon_width = lax.psum(width_part, "ka")
    return (electron_width, phonon_width[None, :])


def solution(mesh):
    in_specs = (
        P(None, ("grp", "ka")),
        P(("grp", "pb"), None, "ka"),
        P(("grp", "pb"), None, None, None),
        P(("grp", "pb"), None),
        P(("grp", "ka"), None),
        P(("grp", "ka"), None),
        P(None, ("grp", "ka")),
        P(("grp", "pb"), "ka", None),
        P(("grp", "pb"), "ka"),
    )
    out_specs = (P(("grp", "ka"), None), P(("grp", "pb"), None))
    return jax.shard_map(shards, mesh=mesh, in_specs=in_specs, out_specs=out_specs, check_vma=False)
```

time: 245 us -> 136 us (0.56)
  matrix products: 59.5 us -> 0.23 us
  other arithmetic: 55.6 us -> 9.44 us
  Pallas kernels: 0 us -> 29.5 us
  local copies, waits for them, and re-layouts: 40.2 us -> 10.9 us
  blocking collectives: 64.8 us -> 40.3 us
  waiting for transfers between devices: 9.58 us -> 30.9 us
    dot_general x7 -> x1, matrix products: 59.5 us -> 0.23 us  [shards(): fetched = jnp.dot(choose, gathered, preferred_element_type=jnp.float32)]
    pallas_call x0 -> x1, Pallas kernels: none -> 29.5 us  [pair_sums(): pl.pallas_call(functools.partial(pair_kernel, modes=modes, bands=bands),...]
    all_gather x3 -> x1, blocking collectives: 47.2 us -> 21.7 us  [shards(): gathered = lax.all_gather(packed, 'ka', axis=0, tiled=True)]
    reduce_sum x1 -> x2, other arithmetic: 23.5 us -> 0.18 us  [the longest x1 0.16 us: shards(): jnp.sum(self_lanes, 2) * mask_here * (scale / lax.axis_size('pb'))]
    all_gather x1, waiting for transfers between devices: 8.9 us -> 30.3 us  [shards(): g = lax.all_gather(g_wannier, 'ka', axis=2, tiled=True)[0]]
    unnamed x25 -> x8, local copies, waits for them, and re-layouts: 22.8 us -> 2.27 us
    sub x2 -> x1, other arithmetic: 18.3 us -> 0.74 us  [weights_of(): real = cos * vec[0] - sin * vec[1]]
    dot_general x1 -> x0, local copies, waits for them, and re-layouts: 13 us -> none  [shards(): jnp.dot(phases, lax.all_gather(g_wannier, 'ka', axis=2, tiled=True)[0], p...]
  transfers between devices with their start and end apart: 1 -> 1, of which waited for: 1 -> 1; matrix products, arithmetic and copies ran while one was open for 6% -> 13% of each run, Pallas kernels for 0% -> 0%
where the time goes in v1:
time: 136 us
  blocking collectives  40.3 us (30%)
  waiting for transfers between devices  30.9 us (23%)
  Pallas kernels  29.5 us (22%)
  between operations  14.3 us (11%)
  local copies, waits for them, and re-layouts  10.9 us (8%)
  other arithmetic  9.44 us (7%)
    all_gather x1, waiting for transfers between devices, shards(): g = lax.all_gather(g_wannier, 'ka', axis=2, tiled=True)[0]  30.3 us
    pallas_call x1, Pallas kernels, pair_sums(): pl.pallas_call(functools.partial(pair_kernel, modes=modes, bands=bands),...  29.5 us
    all_gather x1, blocking collectives, shards(): gathered = lax.all_gather(packed, 'ka', axis=0, tiled=True)  21.7 us
    psum x1, blocking collectives, shards(): phonon_width = lax.psum(width_part, 'ka')  11.1 us
    psum x1, blocking collectives, shards(): electron_width = lax.psum(self_part, 'pb')  7.55 us
    another operation x2, other arithmetic, weights_of(): jnp.stack([lanes_of(real, imag), lanes_of(-imag, real)], 1)  2.82 us
  transfers between devices with their start and end apart: 1, of which 1 were waited for; matrix products, arithmetic and copies ran while one was open for 13% of the time, Pallas kernels for 0%

profile of v1, /device:TPU:0, one launch (start us, length us, event | category | flops | bytes accessed | tf_op | source)
XLA Modules:
  0.0 135.6 jit_solution(3238847160370115458)
XLA Ops:
  7.2 0.0 all-gather.2.cloned.1.call-start
  7.2 0.7 all-gather.2.cloned.1.call-update
  7.9 0.8 slice_bitcast_fusion.4
  8.7 0.1 cosine_convert_fusion
  8.8 0.1 maximum_convert_fusion
  8.9 0.1 slice_bitcast_fusion.1
  9.0 0.1 copy.17
  9.1 0.1 copy.19
  9.1 0.8 convert_bitcast_fusion
  10.0 1.4 %reshape.120 = bf16[16,2,40,40]{3,2,1,0:T(8,128)(2,1)S(1)} reshape(bf16[16,3200]{1,0:T(8,128)(2,1)} %param.13) | data formatting | bytes 204800 | tf_op jit(solution)/shard_map/reshape | solution.py:205
  11.4 0.7 convert_element_type.71.e_ref
  12.1 0.8 slice_bitcast_fusion.6
  12.8 0.1 fusion.9
  12.9 1.0 concatenate.27
  13.9 21.7 %all_gather.7 = bf16[64,3280]{1,0:T(8,128)(2,1)S(1)} all-gather(bf16[16,3280]{1,0:T(8,128)(2,1)S(1)} %concatenate.27), channel_id=1, replica_groups=mesh['grp'=2,'ka'=4,'pb'=4] {'ka'}, dimensions={0}, use_global_device_ids=true | all-gather | bytes 524800 | tf_op jit(solution)/shard_map/all_gather | solution.py:193
  35.6 0.7 bitcast_add_fusion
  36.3 0.2 fusion.8
  36.6 0.5 reshape.122
  37.1 0.2 copy.26
  37.3 0.3 neg.12
  37.6 0.2 copy.25
  37.8 0.9 maximum_bitcast_fusion
  38.7 0.2 reshape.123.left_ref
  38.9 0.3 copy.22
  39.2 0.2 reshape.121.right_ref
  39.4 0.7 multiply_subtract_fusion
  40.2 0.7 pad_convert_fusion
  40.9 1.3 fusion
  42.1 2.5 %fusion.6 = (bf16[2,1,30,8,16,128]{5,3,4,2,1,0:T(8,128)(2,1)S(1)}, bf16[2,1,30,8,16,128]{5,3,4,2,1,0:T(8,128)(2,1)S(1)}) fusion(bf16[2,30,8,16,60]{4,2,3,1,0:T(8,128)(2,1)S(1)} %get-tuple-element.15, bf16[2,30,8,16,64]{4,2,3,1,0:T(8,128)(2,1)S(1)} %pad_convert_fusion, bf16[2,30,8,16,60]{4,2,3,1,0:T(8,128)(2,1)S(1)} %get-tuple-element.16), kind=kLoop, calls=%fused_computation.13 | loop fusion | flops 11796480 | bytes 6758400 | tf_op jit(solution)/shard_map/stack | solution.py:168
  44.6 0.4 pad_maximum_fusion
  45.0 0.0 copy-start.2
  45.0 0.0 copy-start.1
  45.0 2.3 %pad.39.w_ref = bf16[2,512,2048]{2,1,0:T(8,128)(2,1)} pad(bf16[2,480,2048]{2,1,0:T(8,128)(2,1)S(1)} %bitcast.43, bf16[]{:T(256)} %constant.73.clone.1), padding=0_0x0_32x0_0 | pad | bytes 8126466 | tf_op jit(solution)/shard_map/jit(_pad)/pad | solution.py:171
  47.2 0.0 copy-done.2
  47.3 0.1 select_maximum_fusion.1
  47.3 0.1 select_maximum_fusion.2
  47.4 0.1 select_maximum_fusion
  47.5 0.0 copy-done.1
  47.5 0.1 divide_select_fusion.up_ref
  47.6 0.1 fusion.18
  47.6 0.3 add_multiply_fusion
  48.0 30.3 %all-gather.2.cloned.1.call-done = bf16[1,8,192000]{2,1,0:T(8,128)(2,1)} async-done(((bf16[1,8,48000]{2,1,0:T(8,128)(2,1)}), bf16[1,8,192000]{2,1,0:T(8,128)(2,1)}) %all-gather.2.cloned.1.call-update) | async-done | bytes 3072016 | tf_op jit(solution)/shard_map/all_gather | solution.py:190
  78.2 0.1 broadcast_in_dim.6.keep_ref
  78.4 0.1 broadcast_in_dim.7.occ_ref
  78.5 0.0 copy-start
  78.6 1.9 %copy-done = bf16[1,8,192000]{2,1,0:T(8,128)(2,1)S(1)} copy-done((bf16[1,8,192000]{2,1,0:T(8,128)(2,1)S(1)}, bf16[1,8,192000]{2,1,0:T(8,128)(2,1)}, u32[]{:S(2)}) %copy-start) | copy-done | bytes 3072024
  80.4 29.5 %pairs.1 = (f32[16,40,128]{2,1,0:T(8,128)S(1)}, f32[40,128]{1,0:T(8,128)S(1)}) custom-call(bf16[8,192000]{1,0:T(8,128)(2,1)S(1)} %bitcast.42, bf16[2,512,2048]{2,1,0:T(8,128)(2,1)} %pad.39.w_ref, bf16[16,40,80]{2,1,0:T(8,128)(2,1)S(1)} %reshape.121.right_ref, bf16[16,40,80]{2,1,0:T(8,128)(2,1)S(1)} %reshape.123.left_ref, ...), custom_call_target="tpu_custom_call" | custom-call | tf_op jit(solution)/shard_map/pairs/pallas_call | solution.py:123
  109.9 0.2 reduce_sum.18
  110.1 0.1 select_multiply_fusion
  110.2 7.5 %psum.14 = f32[16,40]{1,0:T(8,128)} all-reduce(f32[16,40]{1,0:T(8,128)S(1)} %select_multiply_fusion), channel_id=1, replica_groups=mesh['grp'=2,'ka'=4,'pb'=4] {'pb'}, use_global_device_ids=true, to_apply=%region_1.2 | all-reduce | flops 640 | bytes 5120 | tf_op jit(solution)/shard_map/psum | solution.py:225
  117.7 11.1 %psum.15 = f32[1,60]{1,0:T(1,128)} all-reduce(f32[1,60]{1,0:T(1,128)S(1)} %multiply_bitcast_fusion), channel_id=1, replica_groups=mesh['grp'=2,'ka'=4,'pb'=4] {'ka'}, use_global_device_ids=true, to_apply=%region_3.4 | all-reduce | flops 60 | bytes 480 | tf_op jit(solution)/shard_map/psum | solution.py:226
  (12 shorter events, 0.2 us)
Async XLA Ops:
  7.2 71.1 %all-gather.2.cloned.1.call-start = ((), (), s32[]{:S(2)}) async-start(), calls=%async_computation | async-start | bytes 3840000 | tf_op jit(solution)/shard_map/all_gather | solution.py:190
  45.0 2.3 %copy-start.2 = (f32[1,60]{1,0:T(1,128)S(1)}, f32[1,60]{1,0:T(1,128)}, u32[]{:S(2)}) copy-start(f32[1,60]{1,0:T(1,128)} %param.12) | copy-start | bytes 724
  45.0 2.5 %copy-start.1 = (bf16[16,40]{1,0:T(8,128)(2,1)S(1)}, bf16[16,40]{1,0:T(8,128)(2,1)}, u32[]{:S(2)}) copy-start(bf16[16,40]{1,0:T(8,128)(2,1)} %param.14) | copy-start | bytes 3844
  78.5 1.9 %copy-start = (bf16[1,8,192000]{2,1,0:T(8,128)(2,1)S(1)}, bf16[1,8,192000]{2,1,0:T(8,128)(2,1)}, u32[]{:S(2)}) copy-start(bf16[1,8,192000]{2,1,0:T(8,128)(2,1)} %all-gather.2.cloned.1.call-done) | copy-start | bytes 9216004
Sparse Core Ops, SparseCore 0:
  9.6 68.6 all-gather.1

commit v2 on v1

--- a/solution.py
+++ b/solution.py
@@ -151,6 +151,57 @@
     )(g, weights, right, left, e_here, up_here, mask_here, shift, gain, occ, keep)
 
 
+def sum_kernel(sizes, self_ref, width_ref, self_out, width_out, self_slots, width_slots, sends, receives):
+    kinds = (("pb", sizes[0], self_ref, self_slots), ("ka", sizes[1], width_ref, width_slots))
+    barrier = pltpu.get_barrier_semaphore()
+    for axis, size, _, _ in kinds:
+        for hop in range(1, size):
+            peer = lax.rem(lax.axis_index(axis) + hop, size)
+            pl.semaphore_signal(barrier, inc=1, device_id={axis: peer}, device_id_type=pl.DeviceIdType.MESH)
+    pl.semaphore_wait(barrier, sizes[0] + sizes[1] - 2)
+    copies = []
+    for axis, size, source, slots in kinds:
+        me = lax.axis_index(axis)
+        for hop in range(1, size):
+            copy = pltpu.make_async_remote_copy(
+                src_ref=source,
+                dst_ref=slots.at[me],
+                send_sem=sends.at[len(copies)],
+                recv_sem=receives.at[len(copies)],
+                device_id={axis: lax.rem(me + hop, size)},
+                device_id_type=pl.DeviceIdType.MESH,
+            )
+            copy.start()
+            copies.append(copy)
+        slots[me] = source[...]
+    for copy in copies:
+        copy.wait()
+    for (_, size, _, slots), out in zip(kinds, (self_out, width_out)):
+        total = slots[0]
+        for s in range(1, size):
+            total += slots[s]
+        out[...] = total
+
+
+def both_sums(self_part, width_part):
+    sizes = (lax.axis_size("pb"), lax.axis_size("ka"))
+    copies = sizes[0] + sizes[1] - 2
+    return pl.pallas_call(
+        functools.partial(sum_kernel, sizes),
+        in_specs=[pl.BlockSpec(memory_space=pltpu.VMEM)] * 2,
+        out_specs=[pl.BlockSpec(memory_space=pltpu.VMEM)] * 2,
+        out_shape=[jax.ShapeDtypeStruct(a.shape, jnp.float32) for a in (self_part, width_part)],
+        scratch_shapes=[
+            pltpu.VMEM((sizes[0],) + self_part.shape, jnp.float32),
+            pltpu.VMEM((sizes[1],) + width_part.shape, jnp.float32),
+            pltpu.SemaphoreType.DMA((copies,)),
+            pltpu.SemaphoreType.DMA((copies,)),
+        ],
+        compiler_params=pltpu.CompilerParams(collective_id=0, has_side_effects=True),
+        name="sums",
+    )(self_part, width_part)
+
+
 def lanes_of(first, second):
     pad = [(0, 0)] * (first.ndim - 1) + [(0, HALF - first.shape[-1])]
     return jnp.concatenate([jnp.pad(first, pad), jnp.pad(second, pad)], -1)
@@ -190,7 +241,9 @@
     g = lax.all_gather(g_wannier, "ka", axis=2, tiled=True)[0]
     mask_here = window_mask(band_window, bands)
     packed = jnp.concatenate([rotations, energies, mask_here.astype(jnp.bfloat16)], 1)
-    gathered = lax.all_gather(packed, "ka", axis=0, tiled=True)
+    share = local_k // lax.axis_size("pb")
+    mine = lax.dynamic_slice_in_dim(packed, lax.axis_index("pb") * share, share, 0)
+    gathered = lax.all_gather(mine, ("ka", "pb"), axis=0, tiled=True)
     wanted = target_owner[0, :, 0] * local_k + target_row[0]
     choose = (wanted[:, None] == jnp.arange(total_k, dtype=jnp.int32)[None, :]).astype(jnp.bfloat16)
     fetched = jnp.dot(choose, gathered, preferred_element_type=jnp.float32)
@@ -222,9 +275,10 @@
     scale = SMEARING_WIDTH / math.pi
     self_part = jnp.sum(self_lanes, 2) * mask_here * (scale / lax.axis_size("pb"))
     width_part = jnp.sum(width_lanes, 0)[:modes] * (2.0 * math.pi / total_k * scale)
-    electron_width = lax.psum(self_part, "pb")
-    phonon_width = lax.psum(width_part, "ka")
-    return (electron_width, phonon_width[None, :])
+    self_part = jnp.pad(self_part, ((0, 0), (0, LANES - bands)))
+    width_part = jnp.broadcast_to(jnp.pad(width_part, (0, LANES - modes))[None, :], (8, LANES))
+    electron_width, phonon_width = both_sums(self_part, width_part)
+    return (electron_width[:, :bands], phonon_width[:1, :modes])
 
 
 def solution(mesh):

time: 136 us -> 125 us (0.919)
  blocking collectives: 40.3 us -> 26.5 us
  waiting for transfers between devices: 30.9 us -> 23.1 us
  Pallas kernels: 29.5 us -> 36.3 us
  local copies, waits for them, and re-layouts: 10.9 us -> 14.8 us
    psum x2 -> x0, blocking collectives: 18.6 us -> none  [the longest x1 11.1 us: shards(): phonon_width = lax.psum(width_part, 'ka')]
    all_gather x1, waiting for transfers between devices: 30.3 us -> 22.4 us  [shards(): g = lax.all_gather(g_wannier, 'ka', axis=2, tiled=True)[0]]
    pallas_call x0 -> x1, Pallas kernels: none -> 6.82 us  [both_sums(): pl.pallas_call(functools.partial(sum_kernel, sizes), in_specs=[pl.BlockSp...]
    all_gather x1, blocking collectives: 21.7 us -> 26.5 us  [shards(): gathered = lax.all_gather(mine, ('ka', 'pb'), axis=0, tiled=True)]
    unnamed x8 -> x11, local copies, waits for them, and re-layouts: 2.27 us -> 3.75 us
  transfers between devices with their start and end apart: 1 -> 1, of which waited for: 1 -> 1; matrix products, arithmetic and copies ran while one was open for 13% -> 15% of each run, Pallas kernels for 0% -> 0%
where the time goes in v2:
time: 125 us
  Pallas kernels  36.3 us (29%)
  blocking collectives  26.5 us (21%)
  waiting for transfers between devices  23.1 us (18%)
  local copies, waits for them, and re-layouts  14.8 us (12%)
  between operations  14.3 us (11%)
  other arithmetic  9.44 us (8%)
    pallas_call x1, Pallas kernels, pair_sums(): pl.pallas_call(functools.partial(pair_kernel, modes=modes, bands=bands),...  29.5 us
    all_gather x1, blocking collectives, shards(): gathered = lax.all_gather(mine, ('ka', 'pb'), axis=0, tiled=True)  26.5 us
    all_gather x1, waiting for transfers between devices, shards(): g = lax.all_gather(g_wannier, 'ka', axis=2, tiled=True)[0]  22.4 us
    pallas_call x1, Pallas kernels, both_sums(): pl.pallas_call(functools.partial(sum_kernel, sizes), in_specs=[pl.BlockSp...  6.82 us
    unnamed x11, local copies, waits for them, and re-layouts  3.75 us
    another operation x2, other arithmetic, weights_of(): jnp.stack([lanes_of(real, imag), lanes_of(-imag, real)], 1)  2.82 us
  transfers between devices with their start and end apart: 1, of which 1 were waited for; matrix products, arithmetic and copies ran while one was open for 15% of the time, Pallas kernels for 0%

profile of v2, /device:TPU:0, one launch (start us, length us, event | category | flops | bytes accessed | tf_op | source)
XLA Modules:
  0.0 124.7 jit_solution(4408652314456755961)
XLA Ops:
  7.2 0.0 all-gather.3.cloned.1.call-start
  7.2 0.7 all-gather.3.cloned.1.call-update
  7.9 0.8 slice_bitcast_fusion.4
  8.7 0.1 cosine_convert_fusion
  8.8 0.1 maximum_convert_fusion
  8.9 0.1 slice_bitcast_fusion.1
  9.0 0.1 copy.17
  9.1 0.1 copy.19
  9.1 0.8 convert_bitcast_fusion
  10.0 1.4 %reshape.121 = bf16[16,2,40,40]{3,2,1,0:T(8,128)(2,1)S(1)} reshape(bf16[16,3200]{1,0:T(8,128)(2,1)} %param.13) | data formatting | bytes 204800 | tf_op jit(solution)/shard_map/reshape | solution.py:258
  11.4 0.7 convert_element_type.75.e_ref
  12.1 0.8 slice_bitcast_fusion.6
  12.8 0.1 fusion.9
  12.9 1.0 concatenate.27
  13.9 26.5 %all-gather = bf16[16,4,3280]{2,1,0:T(4,128)(2,1)S(1)} all-gather(bf16[1,4,3280]{2,1,0:T(4,128)(2,1)S(1)} %dynamic-slice_bitcast_fusion), channel_id=1, replica_groups=mesh['grp'=2,'ka'=4,'pb'=4] {'ka','pb'}, dimensions={0}, use_global_device_ids=true | all-gather | bytes 446080 | tf_op jit(solution)/shard_map/all_gather | solution.py:246
  40.4 0.2 reshape.127
  40.6 0.7 bitcast_add_fusion
  41.3 0.2 fusion.8
  41.5 0.5 reshape.123
  42.0 0.2 copy.26
  42.2 0.3 neg.12
  42.6 0.2 copy.25
  42.8 0.9 maximum_bitcast_fusion
  43.7 0.2 reshape.124.left_ref
  43.8 0.3 copy.22
  44.2 0.2 reshape.122.right_ref
  44.4 0.7 multiply_subtract_fusion
  45.1 0.7 pad_convert_fusion
  45.8 1.3 %fusion = (bf16[2,30,8,16,60]{4,2,3,1,0:T(8,128)(2,1)S(1)}, bf16[2,30,8,16,60]{4,2,3,1,0:T(8,128)(2,1)S(1)}) fusion(f32[2,30,60]{2,1,0:T(8,128)S(1)} %copy.20, f32[8,16]{0,1:T(8,128)S(1)} %copy.19, f32[2,30,60]{2,1,0:T(8,128)S(1)} %copy.18, f32[8,16]{0,1:T(8,128)S(1)} %copy.17), kind=kLoop, calls=%fused_computation.5 | loop fusion | flops 2764800 | bytes 1873024 | tf_op jit(solution)/shard_map/convert.13
  47.1 2.5 %fusion.6 = (bf16[2,1,30,8,16,128]{5,3,4,2,1,0:T(8,128)(2,1)S(1)}, bf16[2,1,30,8,16,128]{5,3,4,2,1,0:T(8,128)(2,1)S(1)}) fusion(bf16[2,30,8,16,60]{4,2,3,1,0:T(8,128)(2,1)S(1)} %get-tuple-element.19, bf16[2,30,8,16,64]{4,2,3,1,0:T(8,128)(2,1)S(1)} %pad_convert_fusion, bf16[2,30,8,16,60]{4,2,3,1,0:T(8,128)(2,1)S(1)} %get-tuple-element.20), kind=kLoop, calls=%fused_computation.13 | loop fusion | flops 11796480 | bytes 6758400 | tf_op jit(solution)/shard_map/stack | solution.py:219
  49.6 0.4 pad_maximum_fusion
  49.9 0.0 copy-start.2
  49.9 0.0 copy-start.1
  49.9 2.3 %pad.47.w_ref = bf16[2,512,2048]{2,1,0:T(8,128)(2,1)} pad(bf16[2,480,2048]{2,1,0:T(8,128)(2,1)S(1)} %bitcast.44, bf16[]{:T(256)} %constant.77.clone.1), padding=0_0x0_32x0_0 | pad | bytes 8126466 | tf_op jit(solution)/shard_map/jit(_pad)/pad | solution.py:222
  52.2 0.0 copy-done.2
  52.2 0.1 select_maximum_fusion.1
  52.3 0.1 select_maximum_fusion.2
  52.4 0.1 select_maximum_fusion
  52.5 0.0 copy-done.1
  52.5 0.1 divide_select_fusion.up_ref
  52.5 0.1 fusion.18
  52.6 0.3 add_multiply_fusion
  53.0 22.4 %all-gather.3.cloned.1.call-done = bf16[1,8,192000]{2,1,0:T(8,128)(2,1)} async-done(((bf16[1,8,48000]{2,1,0:T(8,128)(2,1)}), bf16[1,8,192000]{2,1,0:T(8,128)(2,1)}) %all-gather.3.cloned.1.call-update) | async-done | bytes 3072016 | tf_op jit(solution)/shard_map/all_gather | solution.py:241
  75.4 0.1 broadcast_in_dim.6.keep_ref
  75.5 0.1 broadcast_in_dim.7.occ_ref
  75.6 0.0 copy-start
  75.7 1.9 %copy-done = bf16[1,8,192000]{2,1,0:T(8,128)(2,1)S(1)} copy-done((bf16[1,8,192000]{2,1,0:T(8,128)(2,1)S(1)}, bf16[1,8,192000]{2,1,0:T(8,128)(2,1)}, u32[]{:S(2)}) %copy-start) | copy-done | bytes 3072024
  77.5 29.5 %pairs.1 = (f32[16,40,128]{2,1,0:T(8,128)S(1)}, f32[40,128]{1,0:T(8,128)S(1)}) custom-call(bf16[8,192000]{1,0:T(8,128)(2,1)S(1)} %bitcast.43, bf16[2,512,2048]{2,1,0:T(8,128)(2,1)} %pad.47.w_ref, bf16[16,40,80]{2,1,0:T(8,128)(2,1)S(1)} %reshape.122.right_ref, bf16[16,40,80]{2,1,0:T(8,128)(2,1)S(1)} %reshape.124.left_ref, ...), custom_call_target="tpu_custom_call" | custom-call | tf_op jit(solution)/shard_map/pairs/pallas_call | solution.py:123
  107.0 0.2 reduce_sum.18
  107.2 0.1 select_multiply_fusion
  107.3 0.6 pad.54.self_ref
  107.9 0.6 broadcast_in_dim.8.width_ref
  108.5 6.8 %sums.1 = (f32[16,128]{1,0:T(8,128)}, f32[8,128]{1,0:T(8,128)}) custom-call(f32[16,128]{1,0:T(8,128)} %pad.54.self_ref, f32[8,128]{1,0:T(8,128)} %broadcast_in_dim.8.width_ref), custom_call_target="tpu_custom_call" | custom-call | tf_op jit(solution)/shard_map/sums/pallas_call | solution.py:189
  115.3 1.2 slice.74
  116.5 1.3 %copy.28 = f32[16,40]{1,0:T(8,128)} copy(f32[16,40]{1,0:T(8,128)} %bitcast.49) | data formatting | bytes 5120
  (14 shorter events, 0.2 us)
Async XLA Ops:
  7.2 68.2 %all-gather.3.cloned.1.call-start = ((), (), s32[]{:S(2)}) async-start(), calls=%async_computation | async-start | bytes 3840000 | tf_op jit(solution)/shard_map/all_gather | solution.py:241
  49.9 2.3 %copy-start.2 = (f32[1,60]{1,0:T(1,128)S(1)}, f32[1,60]{1,0:T(1,128)}, u32[]{:S(2)}) copy-start(f32[1,60]{1,0:T(1,128)} %param.12) | copy-start | bytes 724
  49.9 2.5 %copy-start.1 = (bf16[16,40]{1,0:T(8,128)(2,1)S(1)}, bf16[16,40]{1,0:T(8,128)(2,1)}, u32[]{:S(2)}) copy-start(bf16[16,40]{1,0:T(8,128)(2,1)} %param.14) | copy-start | bytes 3844
  75.6 1.9 %copy-start = (bf16[1,8,192000]{2,1,0:T(8,128)(2,1)S(1)}, bf16[1,8,192000]{2,1,0:T(8,128)(2,1)}, u32[]{:S(2)}) copy-start(bf16[1,8,192000]{2,1,0:T(8,128)(2,1)} %all-gather.3.cloned.1.call-done) | copy-start | bytes 9216004
Sparse Core Ops, SparseCore 0:
  9.6 65.7 all-gather.2

commit v3 on v2

--- a/solution.py
+++ b/solution.py
@@ -36,43 +36,92 @@
     return 1.0 / (1.0 + jnp.exp(energy_value / THERMAL_KELVIN))
 
 
+def turn_part(g_ref, turned, area):
+    vectors, length = g_ref.shape
+    pairs = length // (2 * area)
+    fill = jnp.zeros((LANES - pairs * vectors, LANES), jnp.float32)
+
+    def turn(j, carry):
+        rows = [
+            g_ref[:, pl.ds(pl.multiple_of(p * 2 * area + j * LANES, LANES), LANES)].astype(jnp.float32)
+            for p in range(pairs)
+        ]
+        tile = jnp.concatenate(rows + [fill], 0).T.astype(jnp.bfloat16)
+        spot = pl.multiple_of(j * LANES, LANES)
+        for half in range(LANES // HALF):
+            first = spot + half * HALF
+
+            @pl.when(first < area)
+            def _():
+                turned[pl.ds(pl.multiple_of(first, HALF), HALF), :LANES] = tile[half * HALF : (half + 1) * HALF]
+
+            @pl.when(first >= area)
+            def _():
+                later = pl.multiple_of(first - area, HALF)
+                turned[pl.ds(later, HALF), LANES:] = tile[half * HALF : (half + 1) * HALF]
+
+        return carry
+
+    lax.fori_loop(0, 2 * area // LANES, turn, 0)
+
+
+def early_kernel(*refs, area):
+    order_ref, parts, w_ref, out_ref, turned = refs[0], refs[1:-3], refs[-3], refs[-2], refs[-1]
+
+    @pl.when(pl.program_id(0) == 0)
+    def _():
+        for s, g_ref in enumerate(parts):
+            turn_part(g_ref, turned.at[s], area)
+
+    chunk = area // 5
+    for c in range(5):
+        rows = slice(c * chunk, (c + 1) * chunk)
+        total = 0.0
+        for s in range(len(parts)):
+            total += jnp.dot(turned[s, rows, :], w_ref[order_ref[s]], preferred_element_type=jnp.float32)
+        out_ref[rows, :] = total
+
+
+def early_sums(order, parts, weights, area):
+    count, depth, width = weights.shape
+    return pl.pallas_call(
+        functools.partial(early_kernel, area=area),
+        grid=(width // (2 * LANES),),
+        in_specs=[pl.BlockSpec(memory_space=pltpu.SMEM)]
+        + [pl.BlockSpec(g.shape, lambda i: (0, 0)) for g in parts]
+        + [pl.BlockSpec((count, depth, 2 * LANES), lambda i: (0, 0, i))],
+        out_specs=pl.BlockSpec((area, 2 * LANES), lambda i: (0, i)),
+        out_shape=jax.ShapeDtypeStruct((area, width), jnp.float32),
+        scratch_shapes=[pltpu.VMEM((len(parts), area, depth), jnp.bfloat16)],
+        compiler_params=pltpu.CompilerParams(vmem_limit_bytes=48 * 1024 * 1024),
+        cost_estimate=pl.CostEstimate(
+            flops=2 * len(parts) * area * depth * width,
+            bytes_accessed=4 * area * width + 2 * weights.size,
+            transcendentals=0,
+        ),
+        name="early",
+    )(order, *parts, weights)
+
+
 def pair_kernel(
-    g_ref, w_ref, right_ref, left_ref, e_ref, up_ref, mask_ref, shift_ref, gain_ref, occ_ref, keep_ref,
-    self_ref, width_ref, turned, modal, half, *, modes, bands
+    order_ref, g_ref, w_ref, early_ref, right_ref, left_ref, e_ref, up_ref, mask_ref,
+    shift_ref, gain_ref, occ_ref, keep_ref, self_ref, width_ref, turned, modal, half, *, bands
 ):
     area = bands * bands
-    vectors = g_ref.shape[0]
-    blocks = 2 * area // LANES
-    per = LANES // vectors
     step = pl.program_id(0)
 
     @pl.when(step == 0)
     def _():
         width_ref[...] = jnp.zeros_like(width_ref)
-
-        def turn(j, carry):
-            for group in range(turned.shape[1] // LANES):
-                rows = []
-                for p in range(group * per, group * per + per):
-                    if p < modes:
-                        at = pl.multiple_of(p * 2 * area + j * LANES, LANES)
-                        rows.append(g_ref[:, pl.ds(at, LANES)].astype(jnp.float32))
-                    else:
-                        rows.append(jnp.zeros((vectors, LANES), jnp.float32))
-                tile = jnp.concatenate(rows, 0).T
-                spot = pl.ds(pl.multiple_of(j * LANES, LANES), LANES)
-                turned[spot, group * LANES : (group + 1) * LANES] = tile.astype(jnp.bfloat16)
-            return carry
-
-        lax.fori_loop(0, blocks, turn, 0)
+        turn_part(g_ref, turned, area)
 
     chunk = 8 * bands
+    weight = w_ref[order_ref[w_ref.shape[0] - 1]]
 
     for c in range(area // chunk):
         first = c * chunk
-        both = jnp.dot(turned[first : first + chunk, :], w_ref[0], preferred_element_type=jnp.float32)
-        both += jnp.dot(
-            turned[area + first : area + first + chunk, :], w_ref[1], preferred_element_type=jnp.float32
+        both = early_ref[first : first + chunk, :] + jnp.dot(
+            turned[first : first + chunk, :], weight, preferred_element_type=jnp.float32
         )
         for kk in range(2):
             modal[kk, first : first + chunk, :] = both[:, kk * LANES : (kk + 1) * LANES]
@@ -114,18 +163,20 @@
     lax.fori_loop(0, 2, one_k, 0)
 
 
-def pair_sums(g, weights, right, left, e_here, up_here, mask_here, shift, gain, occ, keep, modes, bands):
+def pair_sums(order, g, weights, early, right, left, e_here, up_here, mask_here, shift, gain, occ, keep, bands):
     local_k = right.shape[0]
-    depth = weights.shape[1]
+    count, depth, _ = weights.shape
     area = bands * bands
     by_k = lambda i: (i, 0, 0)
     table = pl.BlockSpec((2, bands, LANES), by_k)
     return pl.pallas_call(
-        functools.partial(pair_kernel, modes=modes, bands=bands),
+        functools.partial(pair_kernel, bands=bands),
         grid=(local_k // 2,),
         in_specs=[
+            pl.BlockSpec(memory_space=pltpu.SMEM),
             pl.BlockSpec(g.shape, lambda i: (0, 0)),
-            pl.BlockSpec((2, depth, 2 * LANES), lambda i: (0, 0, i)),
+            pl.BlockSpec((count, depth, 2 * LANES), lambda i: (0, 0, i)),
+            pl.BlockSpec((area, 2 * LANES), lambda i: (0, i)),
             pl.BlockSpec((2,) + right.shape[1:], by_k),
             pl.BlockSpec((2,) + left.shape[1:], by_k),
             pl.BlockSpec(memory_space=pltpu.SMEM),
@@ -142,13 +193,13 @@
             jax.ShapeDtypeStruct((bands, LANES), jnp.float32),
         ],
         scratch_shapes=[
-            pltpu.VMEM((2 * area, depth), jnp.bfloat16),
+            pltpu.VMEM((area, depth), jnp.bfloat16),
             pltpu.VMEM((2, area, LANES), jnp.float32),
             pltpu.VMEM((area, LANES), jnp.float32),
         ],
         compiler_params=pltpu.CompilerParams(vmem_limit_bytes=48 * 1024 * 1024),
         name="pairs",
-    )(g, weights, right, left, e_here, up_here, mask_here, shift, gain, occ, keep)
+    )(order, g, weights, early, right, left, e_here, up_here, mask_here, shift, gain, occ, keep)
 
 
 def sum_kernel(sizes, self_ref, width_ref, self_out, width_out, self_slots, width_slots, sends, receives):
@@ -207,19 +258,34 @@
     return jnp.concatenate([jnp.pad(first, pad), jnp.pad(second, pad)], -1)
 
 
-def weights_of(phases, mode_pair):
+def weights_of(phases, mode_pair, pairs):
     _, local_k, vectors = phases.shape
     modes = mode_pair.shape[1]
     wave = phases.astype(jnp.float32)
-    vec = mode_pair.astype(jnp.float32).reshape(2, modes // 2, 2, modes)
-    vec = jnp.transpose(vec, (0, 2, 1, 3))[:, :, :, None, None, :]
-    cos, sin = (jnp.transpose(w)[None, None, :, :, None] for w in (wave[0], wave[1]))
+    vec = mode_pair.astype(jnp.float32).reshape(2, modes // 2 // pairs, pairs, 2, modes)
+    vec = jnp.transpose(vec, (0, 1, 3, 2, 4))[..., None, None, :]
+    cos, sin = (jnp.transpose(w)[None, None, None, :, :, None] for w in (wave[0], wave[1]))
     real = cos * vec[0] - sin * vec[1]
     imag = cos * vec[1] + sin * vec[0]
-    both = jnp.stack([lanes_of(real, imag), lanes_of(-imag, real)], 1).astype(jnp.bfloat16)
-    both = both.reshape(2, modes * vectors, local_k * LANES)
-    depth = -(-modes * vectors // LANES) * LANES
-    return jnp.pad(both, ((0, 0), (0, depth - modes * vectors), (0, 0)))
+    both = jnp.stack([lanes_of(real, imag), lanes_of(-imag, real)]).astype(jnp.bfloat16)
+    both = both.reshape(modes // pairs, 2, pairs * vectors, local_k * LANES)
+    both = jnp.pad(both, ((0, 0), (0, 0), (0, LANES - pairs * vectors), (0, 0)))
+    return both.reshape(modes // pairs, 2 * LANES, local_k * LANES)
+
+
+def ring_of(array, axis):
+    size = lax.axis_size(axis)
+    held = [array]
+    for _ in range(size - 1):
+        held.append(lax.ppermute(held[-1], axis, [(i, (i + 1) % size) for i in range(size)]))
+    return held
+
+
+def from_each(array, axis):
+    size = lax.axis_size(axis)
+    return [array] + [
+        lax.ppermute(array, axis, [(i, (i + hop) % size) for i in range(size)]) for hop in range(1, size)
+    ]
 
 
 def shards(
@@ -237,24 +303,38 @@
     bands = energies.shape[1]
     modes = frequencies.shape[1]
     vectors = g_wannier.shape[1]
-    total_k = local_k * lax.axis_size("ka")
-    g = lax.all_gather(g_wannier, "ka", axis=2, tiled=True)[0]
+    ka_size, pb_size = lax.axis_size("ka"), lax.axis_size("pb")
+    ka, pb = lax.axis_index("ka"), lax.axis_index("pb")
+    total_k = local_k * ka_size
+    area = bands * bands
+    pairs = max(n for n in range(1, LANES // vectors + 1) if modes // 2 % n == 0)
+    count = modes // pairs
     mask_here = window_mask(band_window, bands)
     packed = jnp.concatenate([rotations, energies, mask_here.astype(jnp.bfloat16)], 1)
-    share = local_k // lax.axis_size("pb")
-    mine = lax.dynamic_slice_in_dim(packed, lax.axis_index("pb") * share, share, 0)
-    gathered = lax.all_gather(mine, ("ka", "pb"), axis=0, tiled=True)
-    wanted = target_owner[0, :, 0] * local_k + target_row[0]
+    share = local_k // pb_size
+    mine = lax.dynamic_slice_in_dim(packed, pb * share, share, 0)
+    mine = jnp.concatenate(from_each(mine, "ka"), 0)
+    gathered = jnp.concatenate(from_each(mine, "pb"), 0)
+    if ka_size == count:
+        parts = ring_of(g_wannier[0], "ka")
+        order = (ka - jnp.arange(count, dtype=jnp.int32)) % count
+    else:
+        whole = lax.all_gather(g_wannier, "ka", axis=2, tiled=True)[0]
+        parts = jnp.split(whole, count, 1)
+        order = jnp.arange(count, dtype=jnp.int32)
+    owner, row = target_owner[0, :, 0], target_row[0]
+    wanted = ((pb - row // share) % pb_size * ka_size + (ka - owner) % ka_size) * share + row % share
     choose = (wanted[:, None] == jnp.arange(total_k, dtype=jnp.int32)[None, :]).astype(jnp.bfloat16)
     fetched = jnp.dot(choose, gathered, preferred_element_type=jnp.float32)
-    size = 2 * bands * bands
+    size = 2 * area
     rot_there = fetched[:, :size].astype(jnp.bfloat16).reshape(local_k, 2, bands, bands)
     e_there = fetched[:, size : size + bands]
     mask_there = fetched[:, size + bands :]
 
     weights = weights_of(
-        phases_of(kpoint_coords, vectors).reshape(2, local_k, vectors), mode_vectors[0]
+        phases_of(kpoint_coords, vectors).reshape(2, local_k, vectors), mode_vectors[0], pairs
     )
+    early = early_sums(order, parts[:-1], weights, area)
     rot_here = rotations.reshape(local_k, 2, bands, bands)
     right = jnp.transpose(rot_here, (0, 3, 1, 2)).reshape(local_k, bands, 2 * bands)
     left = jnp.stack([rot_there[:, 0], -rot_there[:, 1]], 1)
@@ -270,10 +350,11 @@
     shift = lanes_of(frequency, -frequency)[None, None, :] - e_there[:, :, None]
     gain = keep * (lanes_of(bose, bose + 1.0) + lanes_of(ones, -ones) * occ_there)
     self_lanes, width_lanes = pair_sums(
-        g, weights, right, left, e_here, occ_here * mask_here, mask_here, shift, gain, occ_there, keep, modes, bands
+        order, parts[-1], weights, early, right, left, e_here, occ_here * mask_here, mask_here,
+        shift, gain, occ_there, keep, bands,
     )
     scale = SMEARING_WIDTH / math.pi
-    self_part = jnp.sum(self_lanes, 2) * mask_here * (scale / lax.axis_size("pb"))
+    self_part = jnp.sum(self_lanes, 2) * mask_here * (scale / pb_size)
     width_part = jnp.sum(width_lanes, 0)[:modes] * (2.0 * math.pi / total_k * scale)
     self_part = jnp.pad(self_part, ((0, 0), (0, LANES - bands)))
     width_part = jnp.broadcast_to(jnp.pad(width_part, (0, LANES - modes))[None, :], (8, LANES))

time: 125 us -> 114 us (0.912)
  blocking collectives: 26.5 us -> 0 us
  Pallas kernels: 36.3 us -> 52.1 us
  between operations: 14.3 us -> 0.92 us
  starting transfers between devices: 0.04 us -> 10.9 us
  waiting for transfers between devices: 23.1 us -> 16.6 us
  other arithmetic: 9.44 us -> 14.8 us
  local copies, waits for them, and re-layouts: 14.8 us -> 17.6 us
    all_gather x1 -> x0, blocking collectives: 26.5 us -> none  [shards(): gathered = lax.all_gather(mine, ('ka', 'pb'), axis=0, tiled=True)]
    all_gather x1 -> x0, waiting for transfers between devices: 22.4 us -> none  [shards(): g = lax.all_gather(g_wannier, 'ka', axis=2, tiled=True)[0]]
    ppermute x0 -> x9, waiting for transfers between devices: none -> 16.6 us  [the longest x3 13.2 us: ring_of(): lax.ppermute(held[-1], axis, [(i, (i + 1) % size) for i in range(size)])]
    pallas_call x1 -> x2, Pallas kernels: 29.5 us -> 43.9 us  [the longest x1 24.5 us: pair_sums(): pl.pallas_call(functools.partial(pair_kernel, bands=bands), grid=(local_k...]
    ppermute x0 -> x9, starting transfers between devices: none -> 10.9 us  [the longest x6 10 us: from_each(): lax.ppermute(array, axis, [(i, (i + hop) % size) for i in range(size)])]
    another operation x4, other arithmetic: 4.19 us -> 7.02 us  [the longest x2 4.65 us: weights_of(): jnp.stack([lanes_of(real, imag), lanes_of(-imag, real)])]
    pad x1, local copies, waits for them, and re-layouts: 2.27 us -> 4.61 us  [weights_of(): both = jnp.pad(both, ((0, 0), (0, 0), (0, LANES - pairs * vectors), (0, 0)))]
    transpose x1, other arithmetic: 0.88 us -> 2.66 us  [shards(): left = jnp.transpose(left, (0, 3, 1, 2)).reshape(local_k, bands, 2 * bands)]
  transfers between devices with their start and end apart: 1 -> 9, of which waited for: 1 -> 4; matrix products, arithmetic and copies ran while one was open for 15% -> 23% of each run, Pallas kernels for 0% -> 17%
where the time goes in v3:
time: 114 us; the launch traced here: 113 us
  Pallas kernels  52.1 us (46%)
  local copies, waits for them, and re-layouts  17.6 us (15%)
  waiting for transfers between devices  16.6 us (15%)
  other arithmetic  14.8 us (13%)
  starting transfers between devices  10.9 us (10%)
    pallas_call x1, Pallas kernels, pair_sums(): pl.pallas_call(functools.partial(pair_kernel, bands=bands), grid=(local_k...  24.5 us
    pallas_call x1, Pallas kernels, early_sums(): pl.pallas_call(functools.partial(early_kernel, area=area), grid=(width //...  19.4 us
    ppermute x3, waiting for transfers between devices, ring_of(): lax.ppermute(held[-1], axis, [(i, (i + 1) % size) for i in range(size)])  13.2 us
    ppermute x6, starting transfers between devices, from_each(): lax.ppermute(array, axis, [(i, (i + hop) % size) for i in range(size)])  10 us
    pallas_call x1, Pallas kernels, both_sums(): pl.pallas_call(functools.partial(sum_kernel, sizes), in_specs=[pl.BlockSp...  8.15 us
    another operation x2, other arithmetic, weights_of(): jnp.stack([lanes_of(real, imag), lanes_of(-imag, real)])  4.65 us
    pad x1, local copies, waits for them, and re-layouts, weights_of(): both = jnp.pad(both, ((0, 0), (0, 0), (0, LANES - pairs * vectors), (0, 0)))  4.61 us
    ppermute x6, waiting for transfers between devices, from_each(): lax.ppermute(array, axis, [(i, (i + hop) % size) for i in range(size)])  3.31 us
  transfers between devices with their start and end apart: 9, of which 4 were waited for; matrix products, arithmetic and copies ran while one was open for 23% of the time, Pallas kernels for 17%

profile of v3, /device:TPU:0, one launch (start us, length us, event | category | flops | bytes accessed | tf_op | source)
XLA Modules:
  0.0 113.0 jit_solution(7982983440294942407)
XLA Ops:
  0.6 0.0 copy-start.3
  0.6 0.8 slice_bitcast_fusion.6
  1.4 0.1 fusion.9
  1.5 1.0 concatenate.34
  2.5 3.1 %collective-permute-start.3 = (bf16[4,3280]{1,0:T(4,128)(2,1)S(1)}, bf16[4,3280]{1,0:T(4,128)(2,1)S(1)}, u32[]{:S(2)}, u32[]{:S(2)}) collective-permute-start(bf16[4,3280]{1,0:T(4,128)(2,1)S(1)} %constant_dynamic-slice_fusion), channel_id=1, source_target_pairs={{0,4},{4,8},{8,12},{12,0},{1,5},{5,9},{9,13},{13,1},{2,6},{6,10},{... | collective-permute-start | bytes 78728 | tf_op jit(solution)/shard_map/ppermute | solution.py:287
  5.6 2.6 %collective-permute-start.4 = (bf16[4,3280]{1,0:T(4,128)(2,1)S(1)}, bf16[4,3280]{1,0:T(4,128)(2,1)S(1)}, u32[]{:S(2)}, u32[]{:S(2)}) collective-permute-start(bf16[4,3280]{1,0:T(4,128)(2,1)S(1)} %constant_dynamic-slice_fusion), channel_id=1, source_target_pairs={{0,8},{4,12},{8,0},{12,4},{1,9},{5,13},{9,1},{13,5},{2,10},{6,14},... | collective-permute-start | bytes 78728 | tf_op jit(solution)/shard_map/ppermute | solution.py:287
  8.1 1.3 %collective-permute-start.5 = (bf16[4,3280]{1,0:T(4,128)(2,1)S(1)}, bf16[4,3280]{1,0:T(4,128)(2,1)S(1)}, u32[]{:S(2)}, u32[]{:S(2)}) collective-permute-start(bf16[4,3280]{1,0:T(4,128)(2,1)S(1)} %constant_dynamic-slice_fusion), channel_id=1, source_target_pairs={{0,12},{4,0},{8,4},{12,8},{1,13},{5,1},{9,5},{13,9},{2,14},{6,2},{... | collective-permute-start | bytes 78728 | tf_op jit(solution)/shard_map/ppermute | solution.py:287
  9.5 0.7 collective-permute-start
  10.2 0.8 convert_bitcast_fusion
  11.0 0.8 slice_bitcast_fusion.4
  11.8 0.1 cosine_convert_fusion
  11.9 0.1 maximum_convert_fusion
  12.0 0.1 slice_bitcast_fusion.1
  12.1 0.1 copy.18
  12.2 0.1 copy.16
  12.3 2.3 %fusion = (bf16[2,2,15,8,16,60]{5,3,4,2,1,0:T(8,128)(2,1)S(1)}, bf16[2,2,15,8,16,60]{5,3,4,2,1,0:T(8,128)(2,1)}) fusion(f32[2,2,15,60]{3,2,1,0:T(8,128)S(1)} %copy.19, f32[8,16]{0,1:T(8,128)S(1)} %copy.18, f32[2,2,15,60]{3,2,1,0:T(8,128)S(1)} %copy.17, f32[8,16]{0,1:T(8,128)S(1)} %copy.16), kind=kLoop, calls=%fused_computation.5 | loop fusion | flops 2764800 | bytes 1873024 | tf_op jit(solution)/shard_map/convert.13
  14.5 2.0 %multiply_subtract_fusion = bf16[2,2,15,8,16,60]{5,3,4,2,1,0:T(8,128)(2,1)} fusion(f32[2,2,15,60]{3,2,1,0:T(8,128)S(1)} %copy.19, f32[8,16]{0,1:T(8,128)S(1)} %copy.18, f32[2,2,15,60]{3,2,1,0:T(8,128)S(1)} %copy.17, f32[8,16]{0,1:T(8,128)S(1)} %copy.16), kind=kLoop, calls=%fused_computation.7 | loop fusion | flops 1843200 | bytes 951424 | tf_op jit(solution)/shard_map/sub | solution.py:268
  16.5 0.1 divide_select_fusion.up_ref
  16.6 2.2 %pad_convert_fusion = bf16[2,2,15,8,16,64]{5,3,4,2,1,0:T(8,128)(2,1)S(1)} fusion(bf16[2,2,15,8,16,60]{5,3,4,2,1,0:T(8,128)(2,1)} %multiply_subtract_fusion), kind=kLoop, calls=%fused_computation.6 | loop fusion | bytes 1904640 | tf_op jit(solution)/shard_map/convert.11
  18.9 0.1 select_maximum_fusion
  19.0 2.4 %fusion.6 = (bf16[1,2,2,15,8,16,128]{6,4,5,3,2,1,0:T(8,128)(2,1)S(1)}, bf16[1,2,2,15,8,16,128]{6,4,5,3,2,1,0:T(8,128)(2,1)S(1)}) fusion(bf16[2,2,15,8,16,60]{5,3,4,2,1,0:T(8,128)(2,1)S(1)} %get-tuple-element.19, bf16[2,2,15,8,16,64]{5,3,4,2,1,0:T(8,128)(2,1)S(1)} %pad_convert_fusion, bf16[2,2,15,8,16,60]{5,3,4,2,1,0:T(8,128)(2,1)S(1)} %copy-done.1), kind=kLoop, calls=%fused_computation.13 | loop fusion | flops 11796480 | bytes 6758400 | tf_op jit(solution)/shard_map/stack | solution.py:270
  21.5 0.0 copy-start.2
  21.5 2.2 %pad_maximum_fusion = bf16[2,2,2,15,8,16,128]{6,4,5,3,2,1,0:T(8,128)(2,1)} fusion(bf16[1,2,2,15,8,16,128]{6,4,5,3,2,1,0:T(8,128)(2,1)S(1)} %get-tuple-element.13, bf16[1,2,2,15,8,16,128]{6,4,5,3,2,1,0:T(8,128)(2,1)S(1)} %get-tuple-element.12), kind=kLoop, calls=%fused_computation.2 | loop fusion | flops 1966080 | bytes 7864320 | tf_op jit(solution)/shard_map/stack | solution.py:270
  23.7 0.1 select_maximum_fusion.1
  23.8 0.5 reshape.195
  24.3 0.3 copy.20
  24.6 0.2 reshape.196.right_ref
  24.8 4.6 %pad.47 = bf16[4,2,128,2048]{3,2,1,0:T(8,128)(2,1)} pad(bf16[4,2,120,2048]{3,2,1,0:T(8,128)(2,1)} %bitcast.57, bf16[]{:T(256)} %constant.120.clone.1), padding=0_0x0_0x0_8x0_0 | pad | bytes 8126466 | tf_op jit(solution)/shard_map/jit(_pad)/pad | solution.py:272
  29.4 0.0 collective-permute-done.3
  29.4 0.0 collective-permute-done.4
  29.4 0.0 collective-permute-done.5
  29.4 0.1 pad_maximum_fusion.1
  29.5 0.1 collective-permute-start.6
  29.6 1.6 %collective-permute-start.7 = (bf16[16,3280]{1,0:T(8,128)(2,1)S(1)}, bf16[16,3280]{1,0:T(8,128)(2,1)S(1)}, u32[]{:S(2)}, u32[]{:S(2)}) collective-permute-start(bf16[16,3280]{1,0:T(8,128)(2,1)S(1)} %pad_maximum_fusion.1), channel_id=1, source_target_pairs={{0,2},{1,3},{2,0},{3,1},{4,6},{5,7},{6,4},{7,5},{8,10},{9,11},{10,... | collective-permute-start | bytes 314888 | tf_op jit(solution)/shard_map/ppermute | solution.py:287
  31.1 1.4 %collective-permute-start.8 = (bf16[16,3280]{1,0:T(8,128)(2,1)S(1)}, bf16[16,3280]{1,0:T(8,128)(2,1)S(1)}, u32[]{:S(2)}, u32[]{:S(2)}) collective-permute-start(bf16[16,3280]{1,0:T(8,128)(2,1)S(1)} %pad_maximum_fusion.1), channel_id=1, source_target_pairs={{0,3},{1,0},{2,1},{3,2},{4,7},{5,4},{6,5},{7,6},{8,11},{9,8},{10,9... | collective-permute-start | bytes 314888 | tf_op jit(solution)/shard_map/ppermute | solution.py:287
  32.5 0.0 collective-permute-done.refs_2_
  32.5 0.2 collective-permute-start.1
  32.7 0.1 select_maximum_fusion.2
  32.8 1.4 %collective-permute-done.6 = bf16[16,3280]{1,0:T(8,128)(2,1)S(1)} collective-permute-done((bf16[16,3280]{1,0:T(8,128)(2,1)S(1)}, bf16[16,3280]{1,0:T(8,128)(2,1)S(1)}, u32[]{:S(2)}, u32[]{:S(2)}) %collective-permute-start.6) | collective-permute-done | bytes 104992 | tf_op jit(solution)/shard_map/ppermute | solution.py:287
  34.2 1.2 %collective-permute-done.7 = bf16[16,3280]{1,0:T(8,128)(2,1)S(1)} collective-permute-done((bf16[16,3280]{1,0:T(8,128)(2,1)S(1)}, bf16[16,3280]{1,0:T(8,128)(2,1)S(1)}, u32[]{:S(2)}, u32[]{:S(2)}) %collective-permute-start.7) | collective-permute-done | bytes 104992 | tf_op jit(solution)/shard_map/ppermute | solution.py:287
  35.4 0.7 collective-permute-done.8
  36.1 0.1 concatenate.36
  36.2 0.2 fusion.8
  36.5 0.5 reshape.197
  37.0 0.2 copy.24
  37.2 1.1 neg.12
  38.3 0.9 copy.23
  39.2 0.1 fusion.24
  39.3 13.2 %collective-permute-done.1.refs_3_ = bf16[8,48000]{1,0:T(8,128)(2,1)S(1)} collective-permute-done((bf16[8,48000]{1,0:T(8,128)(2,1)S(1)}, bf16[8,48000]{1,0:T(8,128)(2,1)S(1)}, u32[]{:S(2)}, u32[]{:S(2)}) %collective-permute-start.1) | collective-permute-done | bytes 768032 | tf_op jit(solution)/shard_map/ppermute | solution.py:280
  52.5 0.0 collective-permute-start.2
  52.5 2.7 %maximum_bitcast_fusion = bf16[16,40,2,40]{3,2,1,0:T(2,128)(2,1)} fusion(bf16[16,1,40,40]{2,1,3,0:T(2,128)(2,1)} %neg.12, bf16[16,1,40,40]{2,1,3,0:T(2,128)(2,1)} %copy.23), kind=kLoop, calls=%fused_computation.14 | loop fusion | flops 204800 | bytes 204800 | tf_op jit(solution)/shard_map/transpose | solution.py:341
  55.2 1.2 %reshape.198.left_ref = bf16[16,40,80]{2,1,0:T(8,128)(2,1)S(1)} reshape(bf16[16,40,2,40]{3,2,1,0:T(2,128)(2,1)} %maximum_bitcast_fusion) | data formatting | bytes 204800 | tf_op jit(solution)/shard_map/reshape | solution.py:341
  56.3 0.3 add_multiply_fusion
  56.7 19.4 %early.1.early_ref = f32[1600,2048]{1,0:T(8,128)} custom-call(s32[4]{0:T(128)S(1)} %and_select_fusion.9.refs_0_.order_ref, bf16[8,48000]{1,0:T(8,128)(2,1)S(1)} %bitcast.54, bf16[8,48000]{1,0:T(8,128)(2,1)S(1)} %collective-permute-done.refs_2_, bf16[8,48000]{1,0:T(8,128)(2,1)S(1)} %collective-permute-done.1.refs_3_, bf16[4,256,2048]{2,1,0:T(8,128)(2,1)} %bitcast.55), custom_call_target="tpu_custom_call" | custom-call | flops 5033164800 | bytes 17301504 | tf_op jit(solution)/shard_map/early/pallas_call | solution.py:87
  76.1 0.1 broadcast_in_dim.7.occ_ref
  76.3 0.1 broadcast_in_dim.6.keep_ref
  76.4 24.5 %pairs.1 = (f32[16,40,128]{2,1,0:T(8,128)S(1)}, f32[40,128]{1,0:T(8,128)S(1)}) custom-call(s32[4]{0:T(128)S(1)} %and_select_fusion.9.refs_0_.order_ref, bf16[8,48000]{1,0:T(8,128)(2,1)S(1)} %collective-permute-done.2.g_ref, bf16[4,256,2048]{2,1,0:T(8,128)(2,1)} %bitcast.56, f32[1600,2048]{1,0:T(8,128)} %early.1.early_ref, ...), custom_call_target="tpu_custom_call" | custom-call | tf_op jit(solution)/shard_map/pairs/pallas_call | solution.py:172
  100.9 0.2 reduce_sum.18
  101.1 0.1 select_multiply_fusion
  101.2 0.6 pad.54.self_ref
  101.8 0.6 broadcast_in_dim.8.width_ref
  102.4 8.1 %sums.1 = (f32[16,128]{1,0:T(8,128)}, f32[8,128]{1,0:T(8,128)}) custom-call(f32[16,128]{1,0:T(8,128)} %pad.54.self_ref, f32[8,128]{1,0:T(8,128)} %broadcast_in_dim.8.width_ref), custom_call_target="tpu_custom_call" | custom-call | tf_op jit(solution)/shard_map/sums/pallas_call | solution.py:240
  110.6 1.2 %slice.74 = f32[1,60]{1,0:T(1,128)} slice(f32[8,128]{1,0:T(8,128)} %get-tuple-element.9), slice={[0:1], [0:60]} | slice | bytes 480 | tf_op jit(solution)/shard_map/slice | solution.py:362
  111.7 1.3 %copy.26 = f32[16,40]{1,0:T(8,128)} copy(f32[16,40]{1,0:T(8,128)} %bitcast.62) | data formatting | bytes 5120
  (30 shorter events, 0.3 us)
Async XLA Ops:
  0.6 15.9 %copy-start.3 = (bf16[16,40]{1,0:T(8,128)(2,1)S(1)}, bf16[16,40]{1,0:T(8,128)(2,1)}, u32[]{:S(2)}) copy-start(bf16[16,40]{1,0:T(8,128)(2,1)} %param.14) | copy-start | bytes 3844
  2.5 26.9 %collective-permute-start.3 = (bf16[4,3280]{1,0:T(4,128)(2,1)S(1)}, bf16[4,3280]{1,0:T(4,128)(2,1)S(1)}, u32[]{:S(2)}, u32[]{:S(2)}) collective-permute-start(bf16[4,3280]{1,0:T(4,128)(2,1)S(1)} %constant_dynamic-slice_fusion), channel_id=1, source_target_pairs={{0,4},{4,8},{8,12},{12,0},{1,5},{5,9},{9,13},{13,1},{2,6},{6,10},{... | collective-permute-start | bytes 78728 | tf_op jit(solution)/shard_map/ppermute | solution.py:287
  5.6 23.9 %collective-permute-start.4 = (bf16[4,3280]{1,0:T(4,128)(2,1)S(1)}, bf16[4,3280]{1,0:T(4,128)(2,1)S(1)}, u32[]{:S(2)}, u32[]{:S(2)}) collective-permute-start(bf16[4,3280]{1,0:T(4,128)(2,1)S(1)} %constant_dynamic-slice_fusion), channel_id=1, source_target_pairs={{0,8},{4,12},{8,0},{12,4},{1,9},{5,13},{9,1},{13,5},{2,10},{6,14},... | collective-permute-start | bytes 78728 | tf_op jit(solution)/shard_map/ppermute | solution.py:287
  8.1 21.3 %collective-permute-start.5 = (bf16[4,3280]{1,0:T(4,128)(2,1)S(1)}, bf16[4,3280]{1,0:T(4,128)(2,1)S(1)}, u32[]{:S(2)}, u32[]{:S(2)}) collective-permute-start(bf16[4,3280]{1,0:T(4,128)(2,1)S(1)} %constant_dynamic-slice_fusion), channel_id=1, source_target_pairs={{0,12},{4,0},{8,4},{12,8},{1,13},{5,1},{9,5},{13,9},{2,14},{6,2},{... | collective-permute-start | bytes 78728 | tf_op jit(solution)/shard_map/ppermute | solution.py:287
  9.5 23.0 %collective-permute-start = (bf16[8,48000]{1,0:T(8,128)(2,1)}, bf16[8,48000]{1,0:T(8,128)(2,1)S(1)}, u32[]{:S(2)}, u32[]{:S(2)}) collective-permute-start(bf16[8,48000]{1,0:T(8,128)(2,1)} %bitcast.53), channel_id=1, source_target_pairs={{0,4},{4,8},{8,12},{12,0},{1,5},{5,9},{9,13},{13,1},{2,6},{6,10},{... | collective-permute-start | bytes 2304008 | tf_op jit(solution)/shard_map/ppermute | solution.py:280
  14.5 4.3 %copy-start.6 = (f32[1,60]{1,0:T(1,128)S(1)}, f32[1,60]{1,0:T(1,128)}, u32[]{:S(2)}) copy-start(f32[1,60]{1,0:T(1,128)} %param.12) | copy-start | bytes 724
  14.5 4.4 %copy-start.4 = (s32[1,16,1]{1,2,0:T(1,128)S(1)}, s32[1,16,1]{1,2,0:T(1,128)}, u32[]{:S(2)}) copy-start(s32[1,16,1]{1,2,0:T(1,128)} %param.16) | copy-start | bytes 196
  14.5 4.4 %copy-start.5 = (s32[1,16]{1,0:T(1,128)S(1)}, s32[1,16]{1,0:T(1,128)}, u32[]{:S(2)}) copy-start(s32[1,16]{1,0:T(1,128)} %param.17) | copy-start | bytes 196
  16.6 2.4 %copy-start.1 = (bf16[2,2,15,8,16,60]{5,3,4,2,1,0:T(8,128)(2,1)S(1)}, bf16[2,2,15,8,16,60]{5,3,4,2,1,0:T(8,128)(2,1)}, u32[]{:S(2)}) copy-start(bf16[2,2,15,8,16,60]{5,3,4,2,1,0:T(8,128)(2,1)} %get-tuple-element.20) | copy-start | bytes 2764804
  21.5 2.3 %copy-start.2 = (bf16[16,3200]{1,0:T(8,128)(2,1)S(1)}, bf16[16,3200]{1,0:T(8,128)(2,1)}, u32[]{:S(2)}) copy-start(bf16[16,3200]{1,0:T(8,128)(2,1)} %param.13) | copy-start | bytes 307204
  29.4 27.3 %copy-start = (bf16[1,8,48000]{2,1,0:T(8,128)(2,1)S(1)}, bf16[1,8,48000]{2,1,0:T(8,128)(2,1)}, u32[]{:S(2)}) copy-start(bf16[1,8,48000]{2,1,0:T(8,128)(2,1)} %param.10) | copy-start | bytes 2304004
  29.5 4.7 %collective-permute-start.6 = (bf16[16,3280]{1,0:T(8,128)(2,1)S(1)}, bf16[16,3280]{1,0:T(8,128)(2,1)S(1)}, u32[]{:S(2)}, u32[]{:S(2)}) collective-permute-start(bf16[16,3280]{1,0:T(8,128)(2,1)S(1)} %pad_maximum_fusion.1), channel_id=1, source_target_pairs={{0,1},{1,2},{2,3},{3,0},{4,5},{5,6},{6,7},{7,4},{8,9},{9,10},{10,1... | collective-permute-start | bytes 314888 | tf_op jit(solution)/shard_map/ppermute | solution.py:287
  29.6 5.9 %collective-permute-start.7 = (bf16[16,3280]{1,0:T(8,128)(2,1)S(1)}, bf16[16,3280]{1,0:T(8,128)(2,1)S(1)}, u32[]{:S(2)}, u32[]{:S(2)}) collective-permute-start(bf16[16,3280]{1,0:T(8,128)(2,1)S(1)} %pad_maximum_fusion.1), channel_id=1, source_target_pairs={{0,2},{1,3},{2,0},{3,1},{4,6},{5,7},{6,4},{7,5},{8,10},{9,11},{10,... | collective-permute-start | bytes 314888 | tf_op jit(solution)/shard_map/ppermute | solution.py:287
  31.1 5.0 %collective-permute-start.8 = (bf16[16,3280]{1,0:T(8,128)(2,1)S(1)}, bf16[16,3280]{1,0:T(8,128)(2,1)S(1)}, u32[]{:S(2)}, u32[]{:S(2)}) collective-permute-start(bf16[16,3280]{1,0:T(8,128)(2,1)S(1)} %pad_maximum_fusion.1), channel_id=1, source_target_pairs={{0,3},{1,0},{2,1},{3,2},{4,7},{5,4},{6,5},{7,6},{8,11},{9,8},{10,9... | collective-permute-start | bytes 314888 | tf_op jit(solution)/shard_map/ppermute | solution.py:287
  32.5 20.0 %collective-permute-start.1 = (bf16[8,48000]{1,0:T(8,128)(2,1)S(1)}, bf16[8,48000]{1,0:T(8,128)(2,1)S(1)}, u32[]{:S(2)}, u32[]{:S(2)}) collective-permute-start(bf16[8,48000]{1,0:T(8,128)(2,1)S(1)} %collective-permute-done.refs_2_), channel_id=1, source_target_pairs={{0,4},{4,8},{8,12},{12,0},{1,5},{5,9},{9,13},{13,1},{2,6},{6,10},{... | collective-permute-start | bytes 2304008 | tf_op jit(solution)/shard_map/ppermute | solution.py:280
  52.5 23.6 %collective-permute-start.2 = (bf16[8,48000]{1,0:T(8,128)(2,1)S(1)}, bf16[8,48000]{1,0:T(8,128)(2,1)S(1)}, u32[]{:S(2)}, u32[]{:S(2)}) collective-permute-start(bf16[8,48000]{1,0:T(8,128)(2,1)S(1)} %collective-permute-done.1.refs_3_), channel_id=1, source_target_pairs={{0,4},{4,8},{8,12},{12,0},{1,5},{5,9},{9,13},{13,1},{2,6},{6,10},{... | collective-permute-start | bytes 2304008 | tf_op jit(solution)/shard_map/ppermute | solution.py:280

commit v4 on v3

v4 whole, which is shorter than its diff:
```python
import functools
import math

import jax
import jax.numpy as jnp
from jax import lax
from jax.experimental import pallas as pl
from jax.experimental.pallas import tpu as pltpu
from jax.sharding import PartitionSpec as P

THERMAL_KELVIN = 0.1
SMEARING_WIDTH = 0.05
LANES = 128
HALF = 64
VMEM_LIMIT = 32 * 1024 * 1024


def window_mask(band_window, bands):
    energy_levels = jnp.arange(bands, dtype=jnp.int32)
    inside = (energy_levels[None, :] >= band_window[0][:, None]) & (
        energy_levels[None, :] < band_window[1][:, None]
    )
    return inside.astype(jnp.float32)


def phases_of(coords, vectors):
    index = jnp.arange(vectors, dtype=jnp.int32)
    first = (index % 2).astype(jnp.float32)
    second = (index // 2 % 2).astype(jnp.float32)
    third = (index // 4 % 2).astype(jnp.float32)
    angle = coords[0][:, None] * first[None, :] + coords[1][:, None] * second[None, :]
    angle = 2.0 * math.pi * (angle + coords[2][:, None] * third[None, :])
    return jnp.concatenate([jnp.cos(angle), jnp.sin(angle)], 0).astype(jnp.bfloat16)


def occupation(energy_value):
    return 1.0 / (1.0 + jnp.exp(energy_value / THERMAL_KELVIN))


def turn_part(g_ref, turned, area):
    vectors, length = g_ref.shape
    pairs = length // (2 * area)
    fill = jnp.zeros((LANES - pairs * vectors, LANES), jnp.float32)

    def tile_of(start):
        rows = [
            g_ref[:, pl.ds(pl.multiple_of(p * 2 * area + start, LANES), LANES)].astype(jnp.float32)
            for p in range(pairs)
        ]
        return jnp.concatenate(rows + [fill], 0).T.astype(jnp.bfloat16)

    whole = area // LANES
    rest = area - whole * LANES

    def even(j, carry):
        spot = pl.multiple_of(j * LANES, LANES)
        turned[pl.ds(spot, LANES), :LANES] = tile_of(spot)
        return carry

    def odd(j, carry):
        spot = pl.multiple_of(j * LANES, LANES)
        turned[pl.ds(pl.multiple_of(spot + LANES - rest, rest), LANES), LANES:] = tile_of(spot + (whole + 1) * LANES)
        return carry

    lax.fori_loop(0, whole, even, 0)
    middle = tile_of(whole * LANES)
    turned[whole * LANES : area, :LANES] = middle[:rest]
    turned[: LANES - rest, LANES:] = middle[rest:]
    lax.fori_loop(0, whole, odd, 0)


def early_kernel(*refs, area):
    order_ref, parts, w_ref, out_ref, turned = refs[0], refs[1:-3], refs[-3], refs[-2], refs[-1]
    for s, g_ref in enumerate(parts):
        turn_part(g_ref, turned.at[s], area)
    chunk = area // 5

    def one_step(step, carry):
        columns = pl.ds(pl.multiple_of(step * 2 * LANES, 2 * LANES), 2 * LANES)
        weights = [w_ref[order_ref[s], :, columns] for s in range(len(parts))]
        for c in range(5):
            rows = slice(c * chunk, (c + 1) * chunk)
            total = 0.0
            for s in range(len(parts)):
                total += jnp.dot(turned[s, rows, :], weights[s], preferred_element_type=jnp.float32)
            out_ref[step, rows, :] = total.astype(out_ref.dtype)
        return carry

    lax.fori_loop(0, out_ref.shape[0], one_step, 0)


def early_sums(order, parts, weights, area):
    count, depth, width = weights.shape
    return pl.pallas_call(
        functools.partial(early_kernel, area=area),
        in_specs=[pl.BlockSpec(memory_space=pltpu.SMEM)]
        + [pl.BlockSpec(memory_space=pltpu.VMEM)] * (len(parts) + 1),
        out_specs=pl.BlockSpec(memory_space=pltpu.VMEM),
        out_shape=jax.ShapeDtypeStruct((width // (2 * LANES), area, 2 * LANES), jnp.bfloat16),
        scratch_shapes=[pltpu.VMEM((len(parts), area, depth), jnp.bfloat16)],
        compiler_params=pltpu.CompilerParams(vmem_limit_bytes=VMEM_LIMIT),
        cost_estimate=pl.CostEstimate(
            flops=2 * len(parts) * area * depth * width,
            bytes_accessed=2 * area * width + 2 * weights.size,
            transcendentals=0,
        ),
        name="early",
    )(order, *parts, weights)


def pair_kernel(
    order_ref, g_ref, w_ref, early_ref, right_ref, left_ref, e_ref, up_ref, mask_ref,
    shift_ref, gain_ref, occ_ref, keep_ref, self_ref, width_ref, turned, modal, half, *, bands
):
    area = bands * bands
    width_ref[...] = jnp.zeros_like(width_ref)
    turn_part(g_ref, turned, area)
    chunk = 8 * bands
    lane = lax.broadcasted_iota(jnp.int32, (bands, LANES), 1)
    sign = jnp.where(lane < HALF, -1.0, 1.0)

    def operand(block):
        block = jnp.concatenate([block, pltpu.roll(block, HALF, 1) * sign], 0)
        return block.astype(jnp.bfloat16)

    def one_k(kk, step):
        k = step * 2 + kk
        right = right_ref[k]
        for a in range(0, bands, 2):
            pair = [operand(modal[kk, (a + s) * bands : (a + s + 1) * bands, :]) for s in range(2)]
            out = jnp.dot(right, jnp.concatenate(pair, 1), preferred_element_type=jnp.float32)
            for s in range(2):
                half[pl.ds(a + s, bands, stride=bands), :] = out[:, s * LANES : (s + 1) * LANES]
        left = left_ref[k]
        shift = shift_ref[k]
        gain = gain_ref[k]
        occ = occ_ref[k]
        total = jnp.zeros((bands, LANES), jnp.float32)
        for n in range(0, bands, 2):
            pair = [operand(half[(n + s) * bands : (n + s + 1) * bands, :]) for s in range(2)]
            out = jnp.dot(left, jnp.concatenate(pair, 1), preferred_element_type=jnp.float32)
            for s in range(2):
                coupling = out[:, s * LANES : (s + 1) * LANES]
                square = coupling * coupling
                strength = square + pltpu.roll(square, HALF, 1)
                x = shift + e_ref[k, n + s]
                term = strength / (x * x + SMEARING_WIDTH * SMEARING_WIDTH)
                self_ref[k, n + s : n + s + 1, :] = jnp.sum(term * gain, 0, keepdims=True)
                total += term * (up_ref[k, n + s] - mask_ref[k, n + s] * occ)
        width_ref[...] += total * keep_ref[k]
        return step

    def one_step(step, carry):
        columns = pl.ds(pl.multiple_of(step * 2 * LANES, 2 * LANES), 2 * LANES)
        weight = w_ref[order_ref[w_ref.shape[0] - 1], :, columns]
        for c in range(area // chunk):
            rows = slice(c * chunk, (c + 1) * chunk)
            both = early_ref[step, rows, :].astype(jnp.float32) + jnp.dot(
                turned[rows, :], weight, preferred_element_type=jnp.float32
            )
            for kk in range(2):
                modal[kk, rows, :] = both[:, kk * LANES : (kk + 1) * LANES]
        lax.fori_loop(0, 2, one_k, step)
        return carry

    lax.fori_loop(0, right_ref.shape[0] // 2, one_step, 0)


def pair_sums(order, g, weights, early, right, left, e_here, up_here, mask_here, shift, gain, occ, keep, bands):
    local_k = right.shape[0]
    depth = weights.shape[1]
    area = bands * bands
    vmem = pl.BlockSpec(memory_space=pltpu.VMEM)
    smem = pl.BlockSpec(memory_space=pltpu.SMEM)
    return pl.pallas_call(
        functools.partial(pair_kernel, bands=bands),
        in_specs=[smem] + [vmem] * 5 + [smem] * 3 + [vmem] * 4,
        out_specs=[vmem, vmem],
        out_shape=[
            jax.ShapeDtypeStruct((local_k, bands, LANES), jnp.float32),
            jax.ShapeDtypeStruct((bands, LANES), jnp.float32),
        ],
        scratch_shapes=[
            pltpu.VMEM((area, depth), jnp.bfloat16),
            pltpu.VMEM((2, area, LANES), jnp.float32),
            pltpu.VMEM((area, LANES), jnp.float32),
        ],
        compiler_params=pltpu.CompilerParams(vmem_limit_bytes=VMEM_LIMIT),
        name="pairs",
    )(order, g, weights, early, right, left, e_here, up_here, mask_here, shift, gain, occ, keep)


def greet(axes):
    barrier = pltpu.get_barrier_semaphore()
    for axis, size in axes:
        for hop in range(1, size):
            peer = lax.rem(lax.axis_index(axis) + hop, size)
            pl.semaphore_signal(barrier, inc=1, device_id={axis: peer}, device_id_type=pl.DeviceIdType.MESH)
    pl.semaphore_wait(barrier, sum(size - 1 for _, size in axes))


def send_all(axis, size, source, slots, sends, receives, first):
    me = lax.axis_index(axis)
    copies = []
    for hop in range(1, size):
        copy = pltpu.make_async_remote_copy(
            src_ref=source,
            dst_ref=slots.at[me],
            send_sem=sends.at[first + hop - 1],
            recv_sem=receives.at[first + hop - 1],
            device_id={axis: lax.rem(me + hop, size)},
            device_id_type=pl.DeviceIdType.MESH,
        )
        copy.start()
        copies.append(copy)
    slots[me] = source[...]
    return copies


def sum_kernel(
    sizes, scales, self_ref, mask_ref, width_ref, self_out, width_out,
    self_mine, width_mine, self_slots, width_slots, sends, receives
):
    self_mine[...] = jnp.sum(self_ref[...], 2) * mask_ref[...] * scales[0]
    width = jnp.sum(width_ref[...], 0, keepdims=True) * scales[1]
    width_mine[...] = jnp.broadcast_to(width, width_mine.shape)
    greet((("pb", sizes[0]), ("ka", sizes[1])))
    copies = send_all("pb", sizes[0], self_mine, self_slots, sends, receives, 0)
    copies += send_all("ka", sizes[1], width_mine, width_slots, sends, receives, sizes[0] - 1)
    for copy in copies:
        copy.wait()
    for size, slots, out in ((sizes[0], self_slots, self_out), (sizes[1], width_slots, width_out)):
        total = slots[0]
        for s in range(1, size):
            total += slots[s]
        out[...] = total[: out.shape[0], : out.shape[1]]


def both_sums(self_lanes, mask_here, width_lanes, modes, scales):
    sizes = (lax.axis_size("pb"), lax.axis_size("ka"))
    copies = sizes[0] + sizes[1] - 2
    return pl.pallas_call(
        functools.partial(sum_kernel, sizes, scales),
        in_specs=[pl.BlockSpec(memory_space=pltpu.VMEM)] * 3,
        out_specs=[pl.BlockSpec(memory_space=pltpu.VMEM)] * 2,
        out_shape=[
            jax.ShapeDtypeStruct(mask_here.shape, jnp.float32),
            jax.ShapeDtypeStruct((1, modes), jnp.float32),
        ],
        scratch_shapes=[
            pltpu.VMEM(mask_here.shape, jnp.float32),
            pltpu.VMEM((8, LANES), jnp.float32),
            pltpu.VMEM((sizes[0],) + mask_here.shape, jnp.float32),
            pltpu.VMEM((sizes[1], 8, LANES), jnp.float32),
            pltpu.SemaphoreType.DMA((copies,)),
            pltpu.SemaphoreType.DMA((copies,)),
        ],
        compiler_params=pltpu.CompilerParams(collective_id=0, has_side_effects=True),
        name="sums",
    )(self_lanes, mask_here, width_lanes)


def rows_kernel(sizes, mine_ref, out_ref, ka_slots, pb_slots, sends, receives):
    greet((("ka", sizes[1]), ("pb", sizes[0])))
    for copy in send_all("ka", sizes[1], mine_ref, ka_slots, sends, receives, 0):
        copy.wait()
    for copy in send_all("pb", sizes[0], ka_slots, pb_slots, sends, receives, sizes[1] - 1):
        copy.wait()
    rows, columns = mine_ref.shape
    for source in range(sizes[0]):
        for owner in range(sizes[1]):
            place = slice(owner * rows, (owner + 1) * rows), slice(source * columns, (source + 1) * columns)
            out_ref[place] = pb_slots[source, owner]


def gather_rows(packed):
    sizes = (lax.axis_size("pb"), lax.axis_size("ka"))
    rows, width = packed.shape
    columns = -(-width // (sizes[0] * LANES)) * LANES
    packed = jnp.pad(packed, ((0, 0), (0, columns * sizes[0] - width)))
    mine = lax.dynamic_slice_in_dim(packed, lax.axis_index("pb") * columns, columns, 1)
    copies = sizes[0] + sizes[1] - 2
    return pl.pallas_call(
        functools.partial(rows_kernel, sizes),
        in_specs=[pl.BlockSpec(memory_space=pltpu.VMEM)],
        out_specs=pl.BlockSpec(memory_space=pltpu.VMEM),
        out_shape=jax.ShapeDtypeStruct((sizes[1] * rows, sizes[0] * columns), packed.dtype),
        scratch_shapes=[
            pltpu.VMEM((sizes[1], rows, columns), packed.dtype),
            pltpu.VMEM((sizes[0], sizes[1], rows, columns), packed.dtype),
            pltpu.SemaphoreType.DMA((copies,)),
            pltpu.SemaphoreType.DMA((copies,)),
        ],
        compiler_params=pltpu.CompilerParams(collective_id=1, has_side_effects=True),
        name="rows",
    )(mine)


def lanes_of(first, second):
    pad = [(0, 0)] * (first.ndim - 1) + [(0, HALF - first.shape[-1])]
    return jnp.concatenate([jnp.pad(first, pad), jnp.pad(second, pad)], -1)


def weights_of(phases, mode_pair, pairs):
    _, local_k, vectors = phases.shape
    modes = mode_pair.shape[1]
    wave = phases.astype(jnp.float32)
    vec = mode_pair.astype(jnp.float32).reshape(2, modes // 2 // pairs, pairs, 2, modes)
    vec = jnp.transpose(vec, (0, 1, 3, 2, 4))[..., None, None, :]
    cos, sin = (jnp.transpose(w)[None, None, None, :, :, None] for w in (wave[0], wave[1]))
    real = cos * vec[0] - sin * vec[1]
    imag = cos * vec[1] + sin * vec[0]
    both = jnp.stack([lanes_of(real, imag), lanes_of(-imag, real)]).astype(jnp.bfloat16)
    both = both.reshape(modes // pairs, 2, pairs * vectors, local_k * LANES)
    both = jnp.pad(both, ((0, 0), (0, 0), (0, LANES - pairs * vectors), (0, 0)))
    return both.reshape(modes // pairs, 2 * LANES, local_k * LANES)


def ring_of(array, axis):
    size = lax.axis_size(axis)
    held = [array]
    for _ in range(size - 1):
        held.append(lax.ppermute(held[-1], axis, [(i, (i + 1) % size) for i in range(size)]))
    return held


def shards(
    kpoint_coords,
    g_wannier,
    mode_vectors,
    frequencies,
    rotations,
    energies,
    band_window,
    target_owner,
    target_row,
):
    local_k = rotations.shape[0]
    bands = energies.shape[1]
    modes = frequencies.shape[1]
    vectors = g_wannier.shape[1]
    ka_size, pb_size = lax.axis_size("ka"), lax.axis_size("pb")
    ka = lax.axis_index("ka")
    total_k = local_k * ka_size
    area = bands * bands
    pairs = max(n for n in range(1, LANES // vectors + 1) if modes // 2 % n == 0)
    count = modes // pairs
    mask_here = window_mask(band_window, bands)
    packed = jnp.concatenate([rotations, energies, mask_here.astype(jnp.bfloat16)], 1)
    gathered = gather_rows(packed)
    if ka_size == count:
        parts = ring_of(g_wannier[0], "ka")
        order = (ka - jnp.arange(count, dtype=jnp.int32)) % count
    else:
        whole = lax.all_gather(g_wannier, "ka", axis=2, tiled=True)[0]
        parts = jnp.split(whole, count, 1)
        order = jnp.arange(count, dtype=jnp.int32)
    wanted = target_owner[0, :, 0] * local_k + target_row[0]
    choose = (wanted[:, None] == jnp.arange(total_k, dtype=jnp.int32)[None, :]).astype(jnp.bfloat16)
    fetched = jnp.dot(choose, gathered, preferred_element_type=jnp.float32)
    size = 2 * area
    rot_there = fetched[:, :size].astype(jnp.bfloat16).reshape(local_k, 2, bands, bands)
    e_there = fetched[:, size : size + bands]
    mask_there = fetched[:, size + bands : size + 2 * bands]

    weights = weights_of(
        phases_of(kpoint_coords, vectors).reshape(2, local_k, vectors), mode_vectors[0], pairs
    )
    early = early_sums(order, parts[:-1], weights, area)
    rot_here = rotations.reshape(local_k, 2, bands, bands)
    right = jnp.transpose(rot_here, (0, 3, 1, 2)).reshape(local_k, bands, 2 * bands)
    left = jnp.stack([rot_there[:, 0], -rot_there[:, 1]], 1)
    left = jnp.transpose(left, (0, 3, 1, 2)).reshape(local_k, bands, 2 * bands)

    e_here = energies.astype(jnp.float32)
    occ_here = occupation(e_here)
    occ_there = jnp.broadcast_to(occupation(e_there)[:, :, None], (local_k, bands, LANES))
    keep = jnp.broadcast_to(mask_there[:, :, None], (local_k, bands, LANES))
    frequency = frequencies[0]
    bose = 1.0 / (jnp.exp(frequency / THERMAL_KELVIN) - 1.0)
    ones = jnp.ones_like(bose)
    shift = lanes_of(frequency, -frequency)[None, None, :] - e_there[:, :, None]
    gain = keep * (lanes_of(bose, bose + 1.0) + lanes_of(ones, -ones) * occ_there)
    self_lanes, width_lanes = pair_sums(
        order, parts[-1], weights, early, right, left, e_here, occ_here * mask_here, mask_here,
        shift, gain, occ_there, keep, bands,
    )
    scale = SMEARING_WIDTH / math.pi
    scales = (scale / pb_size, 2.0 * math.pi / total_k * scale)
    return both_sums(self_lanes, mask_here, width_lanes, modes, scales)


def solution(mesh):
    in_specs = (
        P(None, ("grp", "ka")),
        P(("grp", "pb"), None, "ka"),
        P(("grp", "pb"), None, None, None),
        P(("grp", "pb"), None),
        P(("grp", "ka"), None),
        P(("grp", "ka"), None),
        P(None, ("grp", "ka")),
        P(("grp", "pb"), "ka", None),
        P(("grp", "pb"), "ka"),
    )
    out_specs = (P(("grp", "ka"), None), P(("grp", "pb"), None))
    return jax.shard_map(shards, mesh=mesh, in_specs=in_specs, out_specs=out_specs, check_vma=False)
```

time: 114 us -> 122 us (1.070)
  Pallas kernels: 52.1 us -> 67.5 us
  starting transfers between devices: 10.9 us -> 4.26 us
  waiting for transfers between devices: 16.6 us -> 19.4 us
  local copies, waits for them, and re-layouts: 17.6 us -> 15.3 us
  other arithmetic: 14.8 us -> 13 us
    pallas_call x3 -> x4, Pallas kernels: 52.1 us -> 67.5 us  [the longest x1 23.3 us: pair_sums(): pl.pallas_call(functools.partial(pair_kernel, bands=bands), in_specs=[sme...]
    ppermute x6 -> x0, starting transfers between devices: 10 us -> none  [from_each(): lax.ppermute(array, axis, [(i, (i + hop) % size) for i in range(size)])]
    ppermute x3, waiting for transfers between devices: 13.2 us -> 19.4 us  [ring_of(): lax.ppermute(held[-1], axis, [(i, (i + 1) % size) for i in range(size)])]
    unnamed x17 -> x50, local copies, waits for them, and re-layouts: 2.44 us -> 7.79 us
    ppermute x3, starting transfers between devices: 0.9 us -> 4.26 us  [ring_of(): lax.ppermute(held[-1], axis, [(i, (i + 1) % size) for i in range(size)])]
    ppermute x6 -> x0, waiting for transfers between devices: 3.31 us -> none  [from_each(): lax.ppermute(array, axis, [(i, (i + hop) % size) for i in range(size)])]
    pad x1, local copies, waits for them, and re-layouts: 4.61 us -> 2.51 us  [weights_of(): both = jnp.pad(both, ((0, 0), (0, 0), (0, LANES - pairs * vectors), (0, 0)))]
    another operation x3, local copies, waits for them, and re-layouts: 2.23 us -> 0.54 us
  transfers between devices with their start and end apart: 9 -> 3, of which waited for: 4 -> 2; matrix products, arithmetic and copies ran while one was open for 23% -> 19% of each run, Pallas kernels for 17% -> 30%
where the time goes in v4:
time: 122 us
  Pallas kernels  67.5 us (55%)
  waiting for transfers between devices  19.4 us (16%)
  local copies, waits for them, and re-layouts  15.3 us (13%)
  other arithmetic  13 us (11%)
  starting transfers between devices  4.26 us (3%)
  matrix products  1.25 us (1%)
    pallas_call x1, Pallas kernels, pair_sums(): pl.pallas_call(functools.partial(pair_kernel, bands=bands), in_specs=[sme...  23.3 us
    pallas_call x1, Pallas kernels, gather_rows(): pl.pallas_call(functools.partial(rows_kernel, sizes), in_specs=[pl.BlockS...  22.4 us
    ppermute x3, waiting for transfers between devices, ring_of(): lax.ppermute(held[-1], axis, [(i, (i + 1) % size) for i in range(size)])  19.4 us
    pallas_call x1, Pallas kernels, early_sums(): pl.pallas_call(functools.partial(early_kernel, area=area), in_specs=[pl.B...  14.5 us
    unnamed x50, local copies, waits for them, and re-layouts  7.79 us
    pallas_call x1, Pallas kernels, both_sums(): pl.pallas_call(functools.partial(sum_kernel, sizes, scales), in_specs=[pl...  7.32 us
    another operation x2, other arithmetic, weights_of(): jnp.stack([lanes_of(real, imag), lanes_of(-imag, real)])  4.67 us
    ppermute x3, starting transfers between devices, ring_of(): lax.ppermute(held[-1], axis, [(i, (i + 1) % size) for i in range(size)])  4.26 us
  transfers between devices with their start and end apart: 3, of which 2 were waited for; matrix products, arithmetic and copies ran while one was open for 19% of the time, Pallas kernels for 30%

profile of v4, /device:TPU:0, one launch (start us, length us, event | category | flops | bytes accessed | tf_op | source)
XLA Modules:
  0.0 121.9 jit_solution(14104260263665530655)
XLA Ops:
  0.6 0.0 copy-start.14
  0.6 0.0 copy-start.6
  0.7 0.0 copy-start.8
  0.7 3.1 %collective-permute-start = (bf16[8,48000]{1,0:T(8,128)(2,1)}, bf16[8,48000]{1,0:T(8,128)(2,1)S(1)}, u32[]{:S(2)}, u32[]{:S(2)}) collective-permute-start(bf16[8,48000]{1,0:T(8,128)(2,1)} %bitcast.41), channel_id=1, source_target_pairs={{0,4},{4,8},{8,12},{12,0},{1,5},{5,9},{9,13},{13,1},{2,6},{6,10},{... | collective-permute-start | bytes 2304008 | tf_op jit(solution)/shard_map/ppermute | solution.py:323
  3.8 0.8 convert_bitcast_fusion
  4.6 0.8 slice_bitcast_fusion.6
  5.4 0.1 cosine_convert_fusion
  5.5 0.1 maximum_convert_fusion
  5.6 0.1 slice_bitcast_fusion.1
  5.7 0.1 copy.18
  5.8 0.1 copy.16
  5.9 0.5 copy-done.7
  6.4 0.7 multiply_subtract_fusion
  7.1 0.5 pad_convert_fusion
  7.7 0.0 copy-start.12
  7.7 0.1 fusion.9
  7.8 0.4 copy-done.10
  8.3 0.0 copy-done.6
  8.3 0.1 concatenate.27
  8.4 0.6 pad_dynamic-slice_fusion.mine_ref
  9.0 22.4 %rows.1 = bf16[64,3584]{1,0:T(8,128)(2,1)} custom-call(bf16[16,896]{1,0:T(8,128)(2,1)} %pad_dynamic-slice_fusion.mine_ref), custom_call_target="tpu_custom_call" | custom-call | tf_op jit(solution)/shard_map/rows/pallas_call | solution.py:283
  31.4 0.0 copy-done.21
  31.4 0.0 copy-done.22
  31.5 1.3 %fusion.7 = f32[16,3584]{1,0:T(8,128)S(1)} fusion(bf16[64,3584]{1,0:T(8,128)(2,1)} %rows.1, s32[16]{0:T(128)S(1)} %bitcast_add_fusion), kind=kOutput, calls=%fused_computation.25 | convolution fusion | flops 7341056 | bytes 688192 | tf_op jit(solution)/shard_map/dot_general | solution.py:360
  32.7 0.0 copy-start.5
  32.7 0.7 copy-done.5
  33.5 0.5 reshape.126
  33.9 0.8 fusion.18
  34.7 0.6 broadcast_add_fusion
  35.3 0.6 select_maximum_fusion
  35.9 1.1 copy.24
  37.0 0.3 neg.12
  37.4 1.1 copy.23
  38.5 1.6 %maximum_bitcast_fusion = bf16[16,40,2,40]{3,2,1,0:T(2,128)(2,1)} fusion(bf16[16,1,40,40]{2,1,3,0:T(2,128)(2,1)S(1)} %neg.12, bf16[16,1,40,40]{2,1,3,0:T(2,128)(2,1)S(1)} %copy.23), kind=kLoop, calls=%fused_computation.14 | loop fusion | flops 204800 | bytes 204800 | tf_op jit(solution)/shard_map/transpose | solution.py:373
  40.1 2.0 %fusion = (bf16[2,2,15,8,16,60]{5,3,4,2,1,0:T(8,128)(2,1)S(1)}, bf16[2,2,15,8,16,60]{5,3,4,2,1,0:T(8,128)(2,1)S(1)}) fusion(f32[2,2,15,60]{3,2,1,0:T(8,128)S(1)} %copy.19, f32[8,16]{0,1:T(8,128)S(1)} %copy.18, f32[2,2,15,60]{3,2,1,0:T(8,128)} %copy-done.7, f32[8,16]{0,1:T(8,128)S(1)} %copy.16), kind=kLoop, calls=%fused_computation.5 | loop fusion | flops 2764800 | bytes 1873024 | tf_op jit(solution)/shard_map/convert.13
  42.1 0.0 copy-start.19
  42.1 0.0 copy-start.20
  42.1 2.5 %fusion.6 = (bf16[1,2,2,15,8,16,128]{6,4,5,3,2,1,0:T(8,128)(2,1)S(1)}, bf16[1,2,2,15,8,16,128]{6,4,5,3,2,1,0:T(8,128)(2,1)S(1)}) fusion(bf16[2,2,15,8,16,60]{5,3,4,2,1,0:T(8,128)(2,1)S(1)} %get-tuple-element.15, bf16[2,2,15,8,16,64]{5,3,4,2,1,0:T(8,128)(2,1)S(1)} %pad_convert_fusion, bf16[2,2,15,8,16,60]{5,3,4,2,1,0:T(8,128)(2,1)S(1)} %get-tuple-element.16), kind=kLoop, calls=%fused_computation.13 | loop fusion | flops 11796480 | bytes 6758400 | tf_op jit(solution)/shard_map/stack | solution.py:313
  44.6 0.0 collective-permute-done.refs_2_
  44.6 1.2 collective-permute-start.1
  45.8 0.1 select_maximum_fusion.1
  45.9 2.2 %pad_maximum_fusion = bf16[2,2,2,15,8,16,128]{6,4,5,3,2,1,0:T(8,128)(2,1)} fusion(bf16[1,2,2,15,8,16,128]{6,4,5,3,2,1,0:T(8,128)(2,1)S(1)} %get-tuple-element.9, bf16[1,2,2,15,8,16,128]{6,4,5,3,2,1,0:T(8,128)(2,1)S(1)} %get-tuple-element.8), kind=kLoop, calls=%fused_computation.2 | loop fusion | flops 1966080 | bytes 7864320 | tf_op jit(solution)/shard_map/stack | solution.py:313
  48.1 0.1 divide_select_fusion.up_ref
  48.2 0.8 fusion.19
  49.0 16.8 %collective-permute-done.1.refs_3_ = bf16[8,48000]{1,0:T(8,128)(2,1)S(1)} collective-permute-done((bf16[8,48000]{1,0:T(8,128)(2,1)S(1)}, bf16[8,48000]{1,0:T(8,128)(2,1)S(1)}, u32[]{:S(2)}, u32[]{:S(2)}) %collective-permute-start.1) | collective-permute-done | bytes 768032 | tf_op jit(solution)/shard_map/ppermute | solution.py:323
  65.8 0.0 collective-permute-start.2
  65.8 0.1 select_maximum_fusion.2
  65.9 0.5 reshape.124
  66.4 0.3 copy.20
  66.7 0.2 reshape.125.right_ref
  67.0 0.2 reshape.127.left_ref
  67.2 0.0 copy-start.3
  67.2 2.5 %pad.43 = bf16[4,2,128,2048]{3,2,1,0:T(8,128)(2,1)S(1)} pad(bf16[4,2,120,2048]{3,2,1,0:T(8,128)(2,1)} %bitcast.43, bf16[]{:T(256)} %constant.90.clone.1), padding=0_0x0_0x0_8x0_0 | pad | bytes 8126466 | tf_op jit(solution)/shard_map/jit(_pad)/pad | solution.py:315
  69.7 0.3 add_multiply_fusion
  70.0 14.5 %early.1.early_ref = bf16[8,1600,256]{2,1,0:T(8,128)(2,1)S(1)} custom-call(s32[4]{0:T(128)S(1)} %and_select_fusion.5.refs_0_.order_ref, bf16[8,48000]{1,0:T(8,128)(2,1)S(1)} %bitcast.42, bf16[8,48000]{1,0:T(8,128)(2,1)S(1)} %collective-permute-done.refs_2_, bf16[8,48000]{1,0:T(8,128)(2,1)S(1)} %collective-permute-done.1.refs_3_, ...), custom_call_target="tpu_custom_call" | custom-call | flops 5033164800 | bytes 10747904 | tf_op jit(solution)/shard_map/early/pallas_call | solution.py:94
  84.5 2.6 %collective-permute-done.2.g_ref = bf16[8,48000]{1,0:T(8,128)(2,1)S(1)} collective-permute-done((bf16[8,48000]{1,0:T(8,128)(2,1)S(1)}, bf16[8,48000]{1,0:T(8,128)(2,1)S(1)}, u32[]{:S(2)}, u32[]{:S(2)}) %collective-permute-start.2) | collective-permute-done | bytes 768032 | tf_op jit(solution)/shard_map/ppermute | solution.py:323
  87.1 0.1 broadcast_in_dim.5.occ_ref
  87.3 0.1 broadcast_in_dim.4.keep_ref
  87.5 23.3 %pairs.1 = (f32[16,40,128]{2,1,0:T(8,128)S(1)}, f32[40,128]{1,0:T(8,128)S(1)}) custom-call(s32[4]{0:T(128)S(1)} %and_select_fusion.5.refs_0_.order_ref, bf16[8,48000]{1,0:T(8,128)(2,1)S(1)} %collective-permute-done.2.g_ref, bf16[4,256,2048]{2,1,0:T(8,128)(2,1)S(1)} %bitcast.40, bf16[8,1600,256]{2,1,0:T(8,128)(2,1)S(1)} %early.1.early_ref, ...), custom_call_target="tpu_custom_call" | custom-call | tf_op jit(solution)/shard_map/pairs/pallas_call | solution.py:175
  110.7 0.7 copy-done
  111.5 0.6 copy-done.2
  112.1 7.3 %sums.1 = (f32[16,40]{1,0:T(8,128)}, f32[1,60]{1,0:T(1,128)}) custom-call(f32[16,40,128]{2,1,0:T(8,128)} %copy-done, f32[16,40]{1,0:T(8,128)} %copy-done.1, f32[40,128]{1,0:T(8,128)} %copy-done.2), custom_call_target="tpu_custom_call" | custom-call | tf_op jit(solution)/shard_map/sums/pallas_call | solution.py:242
  119.4 1.3 %copy.27 = f32[16,40]{1,0:T(8,128)} copy(f32[16,40]{1,0:T(8,128)} %get-tuple-element.37) | data formatting | bytes 5120
  120.7 1.2 copy.28
  (42 shorter events, 0.2 us)
Async XLA Ops:
  0.6 7.1 %copy-start.14 = (s32[2,16]{1,0:T(2,128)S(1)}, s32[2,16]{1,0:T(2,128)}, u32[]{:S(2)}) copy-start(s32[2,16]{1,0:T(2,128)} %param.15) | copy-start | bytes 388
  0.6 7.6 %copy-start.6 = (bf16[16,3200]{1,0:T(8,128)(2,1)S(1)}, bf16[16,3200]{1,0:T(8,128)(2,1)}, u32[]{:S(2)}) copy-start(bf16[16,3200]{1,0:T(8,128)(2,1)} %param.13) | copy-start | bytes 307204
  0.7 7.6 %copy-start.8 = (bf16[16,40]{1,0:T(8,128)(2,1)S(1)}, bf16[16,40]{1,0:T(8,128)(2,1)}, u32[]{:S(2)}) copy-start(bf16[16,40]{1,0:T(8,128)(2,1)} %param.14) | copy-start | bytes 3844
  0.7 30.8 %copy-start.21 = (s32[1,16]{1,0:T(1,128)S(1)}, s32[1,16]{1,0:T(1,128)}, u32[]{:S(2)}) copy-start(s32[1,16]{1,0:T(1,128)} %param.17) | copy-start | bytes 196
  0.7 30.8 %copy-start.22 = (s32[1,16,1]{1,2,0:T(1,128)S(1)}, s32[1,16,1]{1,2,0:T(1,128)}, u32[]{:S(2)}) copy-start(s32[1,16,1]{1,2,0:T(1,128)} %param.16) | copy-start | bytes 196
  0.7 43.9 %collective-permute-start = (bf16[8,48000]{1,0:T(8,128)(2,1)}, bf16[8,48000]{1,0:T(8,128)(2,1)S(1)}, u32[]{:S(2)}, u32[]{:S(2)}) collective-permute-start(bf16[8,48000]{1,0:T(8,128)(2,1)} %bitcast.41), channel_id=1, source_target_pairs={{0,4},{4,8},{8,12},{12,0},{1,5},{5,9},{9,13},{13,1},{2,6},{6,10},{... | collective-permute-start | bytes 2304008 | tf_op jit(solution)/shard_map/ppermute | solution.py:323
  5.8 0.6 copy-start.7
  6.4 28.3 %copy-start.16 = (f32[1,60]{1,0:T(1,128)S(1)}, f32[1,60]{1,0:T(1,128)}, u32[]{:S(2)}) copy-start(f32[1,60]{1,0:T(1,128)} %param.12) | copy-start | bytes 724
  7.7 0.5 copy-start.10
  7.7 0.5 copy-start.12
  8.3 79.2 %copy-start.1 = (f32[16,40]{1,0:T(8,128)}, f32[16,40]{1,0:T(8,128)S(1)}, u32[]{:S(2)}) copy-start(f32[16,40]{1,0:T(8,128)S(1)} %get-tuple-element.26.mask_ref) | copy-start | bytes 7684
  32.7 0.7 copy-start.5
  42.1 3.7 %copy-start.19 = (f32[60]{0:T(128)S(1)}, f32[60]{0:T(128)}, u32[]{:S(2)}) copy-start(f32[60]{0:T(128)} %get-tuple-element.6) | copy-start | bytes 724
  42.1 3.7 %copy-start.20 = (f32[60]{0:T(128)S(1)}, f32[60]{0:T(128)}, u32[]{:S(2)}) copy-start(f32[60]{0:T(128)} %get-tuple-element.7) | copy-start | bytes 724
  44.6 21.2 %collective-permute-start.1 = (bf16[8,48000]{1,0:T(8,128)(2,1)S(1)}, bf16[8,48000]{1,0:T(8,128)(2,1)S(1)}, u32[]{:S(2)}, u32[]{:S(2)}) collective-permute-start(bf16[8,48000]{1,0:T(8,128)(2,1)S(1)} %collective-permute-done.refs_2_), channel_id=1, source_target_pairs={{0,4},{4,8},{8,12},{12,0},{1,5},{5,9},{9,13},{13,1},{2,6},{6,10},{... | collective-permute-start | bytes 2304008 | tf_op jit(solution)/shard_map/ppermute | solution.py:323
  45.9 2.2 %copy-start.9 = (bf16[16,40]{1,0:T(8,128)(2,1)S(1)}, bf16[16,40]{1,0:T(8,128)(2,1)}, u32[]{:S(2)}) copy-start(bf16[16,40]{1,0:T(8,128)(2,1)} %param.14) | copy-start | bytes 3844
  45.9 2.2 %copy-start.11 = (s32[16]{0:T(128)S(1)}, s32[16]{0:T(128)}, u32[]{:S(2)}) copy-start(s32[16]{0:T(128)} %copy-done.10) | copy-start | bytes 196
  45.9 2.2 %copy-start.13 = (s32[16]{0:T(128)S(1)}, s32[16]{0:T(128)}, u32[]{:S(2)}) copy-start(s32[16]{0:T(128)} %copy-done.12) | copy-start | bytes 196
  45.9 20.0 %copy-start.17 = (f32[1,60]{1,0:T(1,128)S(1)}, f32[1,60]{1,0:T(1,128)}, u32[]{:S(2)}) copy-start(f32[1,60]{1,0:T(1,128)} %param.12) | copy-start | bytes 724
  45.9 20.0 %copy-start.18 = (f32[60]{0:T(128)S(1)}, f32[60]{0:T(128)}, u32[]{:S(2)}) copy-start(f32[60]{0:T(128)} %get-tuple-element.30) | copy-start | bytes 724
  45.9 21.1 %copy-start.4 = (bf16[16,40,2,40]{3,2,1,0:T(2,128)(2,1)S(1)}, bf16[16,40,2,40]{3,2,1,0:T(2,128)(2,1)}, u32[]{:S(2)}) copy-start(bf16[16,40,2,40]{3,2,1,0:T(2,128)(2,1)} %maximum_bitcast_fusion) | copy-start | bytes 307204
  65.8 21.3 %collective-permute-start.2 = (bf16[8,48000]{1,0:T(8,128)(2,1)S(1)}, bf16[8,48000]{1,0:T(8,128)(2,1)S(1)}, u32[]{:S(2)}, u32[]{:S(2)}) collective-permute-start(bf16[8,48000]{1,0:T(8,128)(2,1)S(1)} %collective-permute-done.1.refs_3_), channel_id=1, source_target_pairs={{0,4},{4,8},{8,12},{12,0},{1,5},{5,9},{9,13},{13,1},{2,6},{6,10},{... | collective-permute-start | bytes 2304008 | tf_op jit(solution)/shard_map/ppermute | solution.py:323
  67.2 2.5 %copy-start.15 = (f32[128]{0:T(128)S(1)}, f32[128]{0:T(128)}, u32[]{:S(2)}) copy-start(f32[128]{0:T(128)} %select_maximum_fusion) | copy-start | bytes 1540
  67.2 2.9 %copy-start.3 = (bf16[1,8,48000]{2,1,0:T(8,128)(2,1)S(1)}, bf16[1,8,48000]{2,1,0:T(8,128)(2,1)}, u32[]{:S(2)}) copy-start(bf16[1,8,48000]{2,1,0:T(8,128)(2,1)} %param.10) | copy-start | bytes 2304004
  110.7 0.7 copy-start
  111.4 0.6 copy-start.2

commit v5 on v4

--- a/solution.py
+++ b/solution.py
@@ -110,12 +110,13 @@
 
 def pair_kernel(
     order_ref, g_ref, w_ref, early_ref, right_ref, left_ref, e_ref, up_ref, mask_ref,
-    shift_ref, gain_ref, occ_ref, keep_ref, self_ref, width_ref, turned, modal, half, *, bands
+    shift_ref, gain_ref, occ_ref, keep_ref, self_ref, width_ref, turned, modal_even, modal_odd, half_even, half_odd, *, bands
 ):
     area = bands * bands
+    steps = right_ref.shape[0] // 2
+    modals, halves = (modal_even, modal_odd), (half_even, half_odd)
     width_ref[...] = jnp.zeros_like(width_ref)
     turn_part(g_ref, turned, area)
-    chunk = 8 * bands
     lane = lax.broadcasted_iota(jnp.int32, (bands, LANES), 1)
     sign = jnp.where(lane < HALF, -1.0, 1.0)
 
@@ -123,47 +124,59 @@
         block = jnp.concatenate([block, pltpu.roll(block, HALF, 1) * sign], 0)
         return block.astype(jnp.bfloat16)
 
-    def one_k(kk, step):
-        k = step * 2 + kk
-        right = right_ref[k]
-        for a in range(0, bands, 2):
-            pair = [operand(modal[kk, (a + s) * bands : (a + s + 1) * bands, :]) for s in range(2)]
-            out = jnp.dot(right, jnp.concatenate(pair, 1), preferred_element_type=jnp.float32)
-            for s in range(2):
-                half[pl.ds(a + s, bands, stride=bands), :] = out[:, s * LANES : (s + 1) * LANES]
-        left = left_ref[k]
-        shift = shift_ref[k]
-        gain = gain_ref[k]
-        occ = occ_ref[k]
-        total = jnp.zeros((bands, LANES), jnp.float32)
-        for n in range(0, bands, 2):
-            pair = [operand(half[(n + s) * bands : (n + s + 1) * bands, :]) for s in range(2)]
-            out = jnp.dot(left, jnp.concatenate(pair, 1), preferred_element_type=jnp.float32)
-            for s in range(2):
-                coupling = out[:, s * LANES : (s + 1) * LANES]
-                square = coupling * coupling
-                strength = square + pltpu.roll(square, HALF, 1)
-                x = shift + e_ref[k, n + s]
-                term = strength / (x * x + SMEARING_WIDTH * SMEARING_WIDTH)
-                self_ref[k, n + s : n + s + 1, :] = jnp.sum(term * gain, 0, keepdims=True)
-                total += term * (up_ref[k, n + s] - mask_ref[k, n + s] * occ)
-        width_ref[...] += total * keep_ref[k]
-        return step
-
-    def one_step(step, carry):
-        columns = pl.ds(pl.multiple_of(step * 2 * LANES, 2 * LANES), 2 * LANES)
+    def modal_of(t, modal, c):
+        columns = pl.ds(pl.multiple_of(t * 2 * LANES, 2 * LANES), 2 * LANES)
         weight = w_ref[order_ref[w_ref.shape[0] - 1], :, columns]
-        for c in range(area // chunk):
-            rows = slice(c * chunk, (c + 1) * chunk)
-            both = early_ref[step, rows, :].astype(jnp.float32) + jnp.dot(
-                turned[rows, :], weight, preferred_element_type=jnp.float32
-            )
+        rows = slice(c * 8 * bands, (c + 1) * 8 * bands)
+        both = early_ref[t, rows, :].astype(jnp.float32) + jnp.dot(
+            turned[rows, :], weight, preferred_element_type=jnp.float32
+        )
+        for kk in range(2):
+            modal[kk, rows, :] = both[:, kk * LANES : (kk + 1) * LANES]
+
+    def half_of(k, kk, a, modal, half):
+        pair = [operand(modal[kk, (a + s) * bands : (a + s + 1) * bands, :]) for s in range(2)]
+        out = jnp.dot(right_ref[k], jnp.concatenate(pair, 1), preferred_element_type=jnp.float32)
+        for s in range(2):
+            half[kk, pl.ds(a + s, bands, stride=bands), :] = out[:, s * LANES : (s + 1) * LANES]
+
+    def coupling_of(k, kk, n, half, total):
+        pair = [operand(half[kk, (n + s) * bands : (n + s + 1) * bands, :]) for s in range(2)]
+        out = jnp.dot(left_ref[k], jnp.concatenate(pair, 1), preferred_element_type=jnp.float32)
+        for s in range(2):
+            coupling = out[:, s * LANES : (s + 1) * LANES]
+            square = coupling * coupling
+            strength = square + pltpu.roll(square, HALF, 1)
+            x = shift_ref[k] + e_ref[k, n + s]
+            term = strength / (x * x + SMEARING_WIDTH * SMEARING_WIDTH)
+            self_ref[k, n + s : n + s + 1, :] = jnp.sum(term * gain_ref[k], 0, keepdims=True)
+            total += term * (up_ref[k, n + s] - mask_ref[k, n + s] * occ_ref[k])
+        return total
+
+    def run(t, slot, first, second, third):
+        totals = [jnp.zeros((bands, LANES), jnp.float32)] * 2
+        for i in range(0, bands, 2):
+            if first and i % 8 == 0:
+                modal_of(t, modals[slot], i // 8)
             for kk in range(2):
-                modal[kk, rows, :] = both[:, kk * LANES : (kk + 1) * LANES]
-        lax.fori_loop(0, 2, one_k, step)
+                if second:
+                    half_of((t - 1) * 2 + kk, kk, i, modals[1 - slot], halves[1 - slot])
+                if third:
+                    totals[kk] = coupling_of((t - 2) * 2 + kk, kk, i, halves[slot], totals[kk])
+        if third:
+            for kk in range(2):
+                width_ref[...] += totals[kk] * keep_ref[(t - 2) * 2 + kk]
+
+    def two_steps(u, carry):
+        run(2 * u, 0, True, True, True)
+        run(2 * u + 1, 1, True, True, True)
         return carry
 
-    lax.fori_loop(0, right_ref.shape[0] // 2, one_step, 0)
+    run(0, 0, True, False, False)
+    run(1, 1, True, True, False)
+    lax.fori_loop(1, steps // 2, two_steps, 0)
+    run(steps, 0, False, True, True)
+    run(steps + 1, 1, False, False, True)
 
 
 def pair_sums(order, g, weights, early, right, left, e_here, up_here, mask_here, shift, gain, occ, keep, bands):
@@ -183,7 +196,9 @@
         scratch_shapes=[
             pltpu.VMEM((area, depth), jnp.bfloat16),
             pltpu.VMEM((2, area, LANES), jnp.float32),
-            pltpu.VMEM((area, LANES), jnp.float32),
+            pltpu.VMEM((2, area, LANES), jnp.float32),
+            pltpu.VMEM((2, area, LANES), jnp.float32),
+            pltpu.VMEM((2, area, LANES), jnp.float32),
         ],
         compiler_params=pltpu.CompilerParams(vmem_limit_bytes=VMEM_LIMIT),
         name="pairs",
@@ -316,12 +331,9 @@
     return both.reshape(modes // pairs, 2 * LANES, local_k * LANES)
 
 
-def ring_of(array, axis):
+def ring_step(array, axis):
     size = lax.axis_size(axis)
-    held = [array]
-    for _ in range(size - 1):
-        held.append(lax.ppermute(held[-1], axis, [(i, (i + 1) % size) for i in range(size)]))
-    return held
+    return lax.ppermute(array, axis, [(i, (i + 1) % size) for i in range(size)])
 
 
 def shards(
@@ -347,11 +359,15 @@
     count = modes // pairs
     mask_here = window_mask(band_window, bands)
     packed = jnp.concatenate([rotations, energies, mask_here.astype(jnp.bfloat16)], 1)
-    gathered = gather_rows(packed)
     if ka_size == count:
-        parts = ring_of(g_wannier[0], "ka")
+        parts = [g_wannier[0], ring_step(g_wannier[0], "ka")]
+        packed, second = lax.optimization_barrier((packed, parts[1]))
+        gathered, parts[1] = lax.optimization_barrier((gather_rows(packed), second))
+        while len(parts) < count:
+            parts.append(ring_step(parts[-1], "ka"))
         order = (ka - jnp.arange(count, dtype=jnp.int32)) % count
     else:
+        gathered = gather_rows(packed)
         whole = lax.all_gather(g_wannier, "ka", axis=2, tiled=True)[0]
         parts = jnp.split(whole, count, 1)
         order = jnp.arange(count, dtype=jnp.int32)

time: 122 us -> 154 us (1.26)
  Pallas kernels: 67.5 us -> 96.1 us
  local copies, waits for them, and re-layouts: 15.3 us -> 19.3 us
  waiting for transfers between devices: 19.4 us -> 16.2 us
  other arithmetic: 13 us -> 15.1 us
    pallas_call x1, Pallas kernels: 23.3 us -> 59.7 us  [pair_sums(): pl.pallas_call(functools.partial(pair_kernel, bands=bands), in_specs=[sme...]
    pallas_call x1, Pallas kernels: 22.4 us -> 13.4 us  [gather_rows(): pl.pallas_call(functools.partial(rows_kernel, sizes), in_specs=[pl.BlockS...]
    ppermute x3, waiting for transfers between devices: 19.4 us -> 16.2 us  [ring_step(): return lax.ppermute(array, axis, [(i, (i + 1) % size) for i in range(size)])]
    another operation x3, local copies, waits for them, and re-layouts: 0.54 us -> 3.51 us
    unnamed x50 -> x28, local copies, waits for them, and re-layouts: 7.79 us -> 7.12 us
  transfers between devices with their start and end apart: 3 -> 3, of which waited for: 2 -> 1; matrix products, arithmetic and copies ran while one was open for 19% -> 19% of each run, Pallas kernels for 30% -> 9%
where the time goes in v5:
time: 154 us; the launch traced here: 153 us
  Pallas kernels  96.1 us (62%)
  local copies, waits for them, and re-layouts  19.3 us (13%)
  waiting for transfers between devices  16.2 us (11%)
  other arithmetic  15.1 us (10%)
  starting transfers between devices  4.31 us (3%)
    pallas_call x1, Pallas kernels, pair_sums(): pl.pallas_call(functools.partial(pair_kernel, bands=bands), in_specs=[sme...  59.7 us
    ppermute x3, waiting for transfers between devices, ring_step(): return lax.ppermute(array, axis, [(i, (i + 1) % size) for i in range(size)])  16.2 us
    pallas_call x1, Pallas kernels, early_sums(): pl.pallas_call(functools.partial(early_kernel, area=area), in_specs=[pl.B...  14.5 us
    pallas_call x1, Pallas kernels, gather_rows(): pl.pallas_call(functools.partial(rows_kernel, sizes), in_specs=[pl.BlockS...  13.4 us
    pallas_call x1, Pallas kernels, both_sums(): pl.pallas_call(functools.partial(sum_kernel, sizes, scales), in_specs=[pl...  8.49 us
    unnamed x28, local copies, waits for them, and re-layouts  7.12 us
    another operation x2, other arithmetic, weights_of(): jnp.stack([lanes_of(real, imag), lanes_of(-imag, real)])  4.97 us
    ppermute x3, starting transfers between devices, ring_step(): return lax.ppermute(array, axis, [(i, (i + 1) % size) for i in range(size)])  4.31 us
  transfers between devices with their start and end apart: 3, of which 1 were waited for; matrix products, arithmetic and copies ran while one was open for 19% of the time, Pallas kernels for 9%

profile of v5, /device:TPU:0, one launch (start us, length us, event | category | flops | bytes accessed | tf_op | source)
XLA Modules:
  0.0 153.1 jit_solution(2135800785521704703)
XLA Ops:
  0.6 0.0 copy-start.8
  0.6 0.0 copy-start.6
  0.7 0.0 copy-start.7
  0.7 3.1 %collective-permute-start = (bf16[8,48000]{1,0:T(8,128)(2,1)}, bf16[8,48000]{1,0:T(8,128)(2,1)S(1)}, u32[]{:S(2)}, u32[]{:S(2)}) collective-permute-start(bf16[8,48000]{1,0:T(8,128)(2,1)} %bitcast.41), channel_id=1, source_target_pairs={{0,4},{4,8},{8,12},{12,0},{1,5},{5,9},{9,13},{13,1},{2,6},{6,10},{... | collective-permute-start | bytes 2304008 | tf_op jit(solution)/shard_map/ppermute | solution.py:336
  3.7 0.8 convert_bitcast_fusion
  4.6 0.8 slice_bitcast_fusion.4
  5.4 0.1 cosine_convert_fusion
  5.5 0.1 maximum_convert_fusion
  5.6 0.1 slice_bitcast_fusion.1
  5.7 0.1 copy.18
  5.7 0.1 copy.16
  5.8 2.5 %fusion = (bf16[2,2,15,8,16,60]{5,3,4,2,1,0:T(8,128)(2,1)S(1)}, bf16[2,2,15,8,16,60]{5,3,4,2,1,0:T(8,128)(2,1)}) fusion(f32[2,2,15,60]{3,2,1,0:T(8,128)S(1)} %copy.19, f32[8,16]{0,1:T(8,128)S(1)} %copy.18, f32[2,2,15,60]{3,2,1,0:T(8,128)S(1)} %copy.17, f32[8,16]{0,1:T(8,128)S(1)} %copy.16), kind=kLoop, calls=%fused_computation.5 | loop fusion | flops 2764800 | bytes 1873024 | tf_op jit(solution)/shard_map/convert.13
  8.4 2.0 %multiply_subtract_fusion = bf16[2,2,15,8,16,60]{5,3,4,2,1,0:T(8,128)(2,1)} fusion(f32[2,2,15,60]{3,2,1,0:T(8,128)S(1)} %copy.19, f32[8,16]{0,1:T(8,128)S(1)} %copy.18, f32[2,2,15,60]{3,2,1,0:T(8,128)S(1)} %copy.17, f32[8,16]{0,1:T(8,128)S(1)} %copy.16), kind=kLoop, calls=%fused_computation.7 | loop fusion | flops 1843200 | bytes 951424 | tf_op jit(solution)/shard_map/sub | solution.py:326
  10.4 0.0 copy-done.8
  10.4 0.0 copy-done.6
  10.4 0.5 reshape.124
  10.9 0.0 copy-done.7
  10.9 0.1 fusion.9
  11.0 0.1 concatenate.24
  11.1 3.5 %pad_convert_fusion = bf16[2,2,15,8,16,64]{5,3,4,2,1,0:T(8,128)(2,1)} fusion(bf16[2,2,15,8,16,60]{5,3,4,2,1,0:T(8,128)(2,1)} %multiply_subtract_fusion), kind=kLoop, calls=%fused_computation.6 | loop fusion | bytes 1904640 | tf_op jit(solution)/shard_map/convert.11
  14.6 1.0 copy.20
  15.6 1.2 reshape.125.right_ref
  16.8 4.6 %fusion.6 = (bf16[1,2,2,15,8,16,128]{6,4,5,3,2,1,0:T(8,128)(2,1)S(1)}, bf16[1,2,2,15,8,16,128]{6,4,5,3,2,1,0:T(8,128)(2,1)S(1)}) fusion(bf16[2,2,15,8,16,60]{5,3,4,2,1,0:T(8,128)(2,1)S(1)} %get-tuple-element.23, bf16[2,2,15,8,16,64]{5,3,4,2,1,0:T(8,128)(2,1)} %pad_convert_fusion, bf16[2,2,15,8,16,60]{5,3,4,2,1,0:T(8,128)(2,1)} %get-tuple-element.24), kind=kLoop, calls=%fused_computation.13 | loop fusion | flops 11796480 | bytes 6758400 | tf_op jit(solution)/shard_map/stack | solution.py:328
  21.4 0.4 pad_maximum_fusion
  21.8 0.0 copy-start.9
  21.8 0.0 copy-start.10
  21.8 0.0 copy-start.11
  21.8 2.3 %pad.44 = bf16[4,2,128,2048]{3,2,1,0:T(8,128)(2,1)} pad(bf16[4,2,120,2048]{3,2,1,0:T(8,128)(2,1)S(1)} %bitcast.43, bf16[]{:T(256)} %constant.85.clone.1), padding=0_0x0_0x0_8x0_0 | pad | bytes 8126466 | tf_op jit(solution)/shard_map/jit(_pad)/pad | solution.py:330
  24.1 0.1 select_maximum_fusion
  24.2 0.0 copy-done.9
  24.2 0.1 select_maximum_fusion.1
  24.2 0.0 copy-done.10
  24.2 0.0 copy-done.11
  24.3 0.1 divide_select_fusion.up_ref
  24.3 0.0 collective-permute-done.refs_2_
  24.3 0.6 pad_dynamic-slice_fusion.mine_ref
  25.0 13.4 %rows.1 = bf16[64,3584]{1,0:T(8,128)(2,1)} custom-call(bf16[16,896]{1,0:T(8,128)(2,1)} %pad_dynamic-slice_fusion.mine_ref), custom_call_target="tpu_custom_call" | custom-call | tf_op jit(solution)/shard_map/rows/pallas_call | solution.py:298
  38.4 1.2 collective-permute-start.1
  39.6 0.1 select_maximum_fusion.2
  39.7 1.3 fusion.8
  41.0 0.5 reshape.126
  41.5 0.2 copy.24
  41.7 1.1 neg.12
  42.7 0.9 copy.23
  43.7 0.1 fusion.19
  43.8 16.2 %collective-permute-done.1.refs_3_ = bf16[8,48000]{1,0:T(8,128)(2,1)S(1)} collective-permute-done((bf16[8,48000]{1,0:T(8,128)(2,1)S(1)}, bf16[8,48000]{1,0:T(8,128)(2,1)S(1)}, u32[]{:S(2)}, u32[]{:S(2)}) %collective-permute-start.1) | collective-permute-done | bytes 768032 | tf_op jit(solution)/shard_map/ppermute | solution.py:336
  59.9 0.0 collective-permute-start.2
  59.9 2.7 %maximum_bitcast_fusion = bf16[16,40,2,40]{3,2,1,0:T(2,128)(2,1)} fusion(bf16[16,1,40,40]{2,1,3,0:T(2,128)(2,1)} %neg.12, bf16[16,1,40,40]{2,1,3,0:T(2,128)(2,1)} %copy.23), kind=kLoop, calls=%fused_computation.14 | loop fusion | flops 204800 | bytes 204800 | tf_op jit(solution)/shard_map/transpose | solution.py:389
  62.6 1.2 reshape.127.left_ref
  63.8 0.3 add_multiply_fusion
  64.1 0.0 copy-done.5
  64.1 0.0 copy-start
  64.1 2.2 %copy-done = bf16[4,2,128,2048]{3,2,1,0:T(8,128)(2,1)S(1)} copy-done((bf16[4,2,128,2048]{3,2,1,0:T(8,128)(2,1)S(1)}, bf16[4,2,128,2048]{3,2,1,0:T(8,128)(2,1)}, u32[]{:S(2)}) %copy-start) | copy-done | bytes 4194328
  66.3 14.5 %early.1.early_ref = bf16[8,1600,256]{2,1,0:T(8,128)(2,1)S(1)} custom-call(s32[4]{0:T(128)S(1)} %and_select_fusion.5.refs_0_.order_ref, bf16[8,48000]{1,0:T(8,128)(2,1)S(1)} %bitcast.42, bf16[8,48000]{1,0:T(8,128)(2,1)S(1)} %collective-permute-done.refs_2_, bf16[8,48000]{1,0:T(8,128)(2,1)S(1)} %collective-permute-done.1.refs_3_, ...), custom_call_target="tpu_custom_call" | custom-call | flops 5033164800 | bytes 10747904 | tf_op jit(solution)/shard_map/early/pallas_call | solution.py:94
  80.8 0.0 collective-permute-done.2.g_ref
  80.9 0.1 broadcast_in_dim.5.occ_ref
  81.0 0.1 broadcast_in_dim.4.keep_ref
  81.2 59.7 %pairs.1 = (f32[16,40,128]{2,1,0:T(8,128)S(1)}, f32[40,128]{1,0:T(8,128)S(1)}) custom-call(s32[4]{0:T(128)S(1)} %and_select_fusion.5.refs_0_.order_ref, bf16[8,48000]{1,0:T(8,128)(2,1)S(1)} %collective-permute-done.2.g_ref, bf16[4,256,2048]{2,1,0:T(8,128)(2,1)S(1)} %bitcast.40, bf16[8,1600,256]{2,1,0:T(8,128)(2,1)S(1)} %early.1.early_ref, ...), custom_call_target="tpu_custom_call" | custom-call | tf_op jit(solution)/shard_map/pairs/pallas_call | solution.py:188
  140.9 0.0 copy-start.2
  140.9 0.7 copy-done.2
  141.6 0.6 copy-done.4
  142.2 8.5 %sums.1 = (f32[16,40]{1,0:T(8,128)}, f32[1,60]{1,0:T(1,128)}) custom-call(f32[16,40,128]{2,1,0:T(8,128)} %copy-done.2, f32[16,40]{1,0:T(8,128)} %copy-done.3, f32[40,128]{1,0:T(8,128)} %copy-done.4), custom_call_target="tpu_custom_call" | custom-call | tf_op jit(solution)/shard_map/sums/pallas_call | solution.py:257
  150.7 1.3 copy.27
  152.0 1.2 copy.28
  (20 shorter events, 0.2 us)
Async XLA Ops:
  0.6 9.8 %copy-start.8 = (s32[2,16]{1,0:T(2,128)S(1)}, s32[2,16]{1,0:T(2,128)}, u32[]{:S(2)}) copy-start(s32[2,16]{1,0:T(2,128)} %param.15) | copy-start | bytes 388
  0.6 9.8 %copy-start.6 = (bf16[16,3200]{1,0:T(8,128)(2,1)S(1)}, bf16[16,3200]{1,0:T(8,128)(2,1)}, u32[]{:S(2)}) copy-start(bf16[16,3200]{1,0:T(8,128)(2,1)} %param.13) | copy-start | bytes 307204
  0.7 10.3 %copy-start.7 = (bf16[16,40]{1,0:T(8,128)(2,1)S(1)}, bf16[16,40]{1,0:T(8,128)(2,1)}, u32[]{:S(2)}) copy-start(bf16[16,40]{1,0:T(8,128)(2,1)} %param.14) | copy-start | bytes 3844
  0.7 23.7 %collective-permute-start = (bf16[8,48000]{1,0:T(8,128)(2,1)}, bf16[8,48000]{1,0:T(8,128)(2,1)S(1)}, u32[]{:S(2)}, u32[]{:S(2)}) collective-permute-start(bf16[8,48000]{1,0:T(8,128)(2,1)} %bitcast.41), channel_id=1, source_target_pairs={{0,4},{4,8},{8,12},{12,0},{1,5},{5,9},{9,13},{13,1},{2,6},{6,10},{... | collective-permute-start | bytes 2304008 | tf_op jit(solution)/shard_map/ppermute | solution.py:336
  11.0 70.2 %copy-start.3 = (f32[16,40]{1,0:T(8,128)}, f32[16,40]{1,0:T(8,128)S(1)}, u32[]{:S(2)}) copy-start(f32[16,40]{1,0:T(8,128)S(1)} %get-tuple-element.34.mask_ref) | copy-start | bytes 7684
  21.8 2.4 %copy-start.9 = (f32[1,60]{1,0:T(1,128)S(1)}, f32[1,60]{1,0:T(1,128)}, u32[]{:S(2)}) copy-start(f32[1,60]{1,0:T(1,128)} %param.12) | copy-start | bytes 724
  21.8 2.5 %copy-start.10 = (s32[1,16]{1,0:T(1,128)S(1)}, s32[1,16]{1,0:T(1,128)}, u32[]{:S(2)}) copy-start(s32[1,16]{1,0:T(1,128)} %param.17) | copy-start | bytes 196
  21.8 2.5 %copy-start.11 = (s32[1,16,1]{1,2,0:T(1,128)S(1)}, s32[1,16,1]{1,2,0:T(1,128)}, u32[]{:S(2)}) copy-start(s32[1,16,1]{1,2,0:T(1,128)} %param.16) | copy-start | bytes 196
  24.1 40.1 %copy-start.5 = (bf16[1,8,48000]{2,1,0:T(8,128)(2,1)S(1)}, bf16[1,8,48000]{2,1,0:T(8,128)(2,1)}, u32[]{:S(2)}) copy-start(bf16[1,8,48000]{2,1,0:T(8,128)(2,1)} %param.10) | copy-start | bytes 2304004
  38.4 21.5 %collective-permute-start.1 = (bf16[8,48000]{1,0:T(8,128)(2,1)S(1)}, bf16[8,48000]{1,0:T(8,128)(2,1)S(1)}, u32[]{:S(2)}, u32[]{:S(2)}) collective-permute-start(bf16[8,48000]{1,0:T(8,128)(2,1)S(1)} %collective-permute-done.refs_2_), channel_id=1, source_target_pairs={{0,4},{4,8},{8,12},{12,0},{1,5},{5,9},{9,13},{13,1},{2,6},{6,10},{... | collective-permute-start | bytes 2304008 | tf_op jit(solution)/shard_map/ppermute | solution.py:336
  59.9 20.9 %collective-permute-start.2 = (bf16[8,48000]{1,0:T(8,128)(2,1)S(1)}, bf16[8,48000]{1,0:T(8,128)(2,1)S(1)}, u32[]{:S(2)}, u32[]{:S(2)}) collective-permute-start(bf16[8,48000]{1,0:T(8,128)(2,1)S(1)} %collective-permute-done.1.refs_3_), channel_id=1, source_target_pairs={{0,4},{4,8},{8,12},{12,0},{1,5},{5,9},{9,13},{13,1},{2,6},{6,10},{... | collective-permute-start | bytes 2304008 | tf_op jit(solution)/shard_map/ppermute | solution.py:336
  64.1 2.2 %copy-start = (bf16[4,2,128,2048]{3,2,1,0:T(8,128)(2,1)S(1)}, bf16[4,2,128,2048]{3,2,1,0:T(8,128)(2,1)}, u32[]{:S(2)}) copy-start(bf16[4,2,128,2048]{3,2,1,0:T(8,128)(2,1)} %pad.44) | copy-start | bytes 12582916
  66.3 14.8 %copy-start.1 = (bf16[4,2,128,2048]{3,2,1,0:T(8,128)(2,1)S(1)}, bf16[4,2,128,2048]{3,2,1,0:T(8,128)(2,1)}, u32[]{:S(2)}) copy-start(bf16[4,2,128,2048]{3,2,1,0:T(8,128)(2,1)} %pad.44) | copy-start | bytes 12582916
  140.9 0.7 copy-start.2
  141.6 0.6 copy-start.4

commit v6 on v4

--- a/solution.py
+++ b/solution.py
@@ -260,68 +260,37 @@
     )(self_lanes, mask_here, width_lanes)
 
 
-def rows_kernel(sizes, mine_ref, out_ref, ka_slots, pb_slots, sends, receives):
-    greet((("ka", sizes[1]), ("pb", sizes[0])))
-    for copy in send_all("ka", sizes[1], mine_ref, ka_slots, sends, receives, 0):
-        copy.wait()
-    for copy in send_all("pb", sizes[0], ka_slots, pb_slots, sends, receives, sizes[1] - 1):
-        copy.wait()
-    rows, columns = mine_ref.shape
-    for source in range(sizes[0]):
-        for owner in range(sizes[1]):
-            place = slice(owner * rows, (owner + 1) * rows), slice(source * columns, (source + 1) * columns)
-            out_ref[place] = pb_slots[source, owner]
-
-
-def gather_rows(packed):
-    sizes = (lax.axis_size("pb"), lax.axis_size("ka"))
-    rows, width = packed.shape
-    columns = -(-width // (sizes[0] * LANES)) * LANES
-    packed = jnp.pad(packed, ((0, 0), (0, columns * sizes[0] - width)))
-    mine = lax.dynamic_slice_in_dim(packed, lax.axis_index("pb") * columns, columns, 1)
-    copies = sizes[0] + sizes[1] - 2
-    return pl.pallas_call(
-        functools.partial(rows_kernel, sizes),
-        in_specs=[pl.BlockSpec(memory_space=pltpu.VMEM)],
-        out_specs=pl.BlockSpec(memory_space=pltpu.VMEM),
-        out_shape=jax.ShapeDtypeStruct((sizes[1] * rows, sizes[0] * columns), packed.dtype),
-        scratch_shapes=[
-            pltpu.VMEM((sizes[1], rows, columns), packed.dtype),
-            pltpu.VMEM((sizes[0], sizes[1], rows, columns), packed.dtype),
-            pltpu.SemaphoreType.DMA((copies,)),
-            pltpu.SemaphoreType.DMA((copies,)),
-        ],
-        compiler_params=pltpu.CompilerParams(collective_id=1, has_side_effects=True),
-        name="rows",
-    )(mine)
-
-
 def lanes_of(first, second):
     pad = [(0, 0)] * (first.ndim - 1) + [(0, HALF - first.shape[-1])]
     return jnp.concatenate([jnp.pad(first, pad), jnp.pad(second, pad)], -1)
 
 
-def weights_of(phases, mode_pair, pairs):
+def weights_of(phases, mode_pair, pairs, behind):
     _, local_k, vectors = phases.shape
     modes = mode_pair.shape[1]
     wave = phases.astype(jnp.float32)
     vec = mode_pair.astype(jnp.float32).reshape(2, modes // 2 // pairs, pairs, 2, modes)
     vec = jnp.transpose(vec, (0, 1, 3, 2, 4))[..., None, None, :]
     cos, sin = (jnp.transpose(w)[None, None, None, :, :, None] for w in (wave[0], wave[1]))
-    real = cos * vec[0] - sin * vec[1]
-    imag = cos * vec[1] + sin * vec[0]
-    both = jnp.stack([lanes_of(real, imag), lanes_of(-imag, real)]).astype(jnp.bfloat16)
+    real = (cos * vec[0] - sin * vec[1]).astype(jnp.bfloat16)
+    imag = (cos * vec[1] + sin * vec[0]).astype(jnp.bfloat16)
+    real, imag, behind = lax.optimization_barrier((real, imag, behind))
+    both = jnp.stack([lanes_of(real, imag), lanes_of(-imag, real)])
     both = both.reshape(modes // pairs, 2, pairs * vectors, local_k * LANES)
     both = jnp.pad(both, ((0, 0), (0, 0), (0, LANES - pairs * vectors), (0, 0)))
-    return both.reshape(modes // pairs, 2 * LANES, local_k * LANES)
-
-
-def ring_of(array, axis):
+    return both.reshape(modes // pairs, 2 * LANES, local_k * LANES), behind
+
+
+def ring_step(array, axis):
     size = lax.axis_size(axis)
-    held = [array]
-    for _ in range(size - 1):
-        held.append(lax.ppermute(held[-1], axis, [(i, (i + 1) % size) for i in range(size)]))
-    return held
+    return lax.ppermute(array, axis, [(i, (i + 1) % size) for i in range(size)])
+
+
+def from_each(array, axis):
+    size = lax.axis_size(axis)
+    return [array] + [
+        lax.ppermute(array, axis, [(i, (i + hop) % size) for i in range(size)]) for hop in range(1, size)
+    ]
 
 
 def shards(
@@ -340,22 +309,31 @@
     modes = frequencies.shape[1]
     vectors = g_wannier.shape[1]
     ka_size, pb_size = lax.axis_size("ka"), lax.axis_size("pb")
-    ka = lax.axis_index("ka")
+    ka, pb = lax.axis_index("ka"), lax.axis_index("pb")
     total_k = local_k * ka_size
     area = bands * bands
     pairs = max(n for n in range(1, LANES // vectors + 1) if modes // 2 % n == 0)
     count = modes // pairs
     mask_here = window_mask(band_window, bands)
     packed = jnp.concatenate([rotations, energies, mask_here.astype(jnp.bfloat16)], 1)
-    gathered = gather_rows(packed)
+    share = local_k // 2
+    mine = lax.dynamic_slice_in_dim(packed, pb % 2 * share, share, 0)
+    mine = jnp.concatenate(from_each(mine, "ka"), 0)
+    other = lax.ppermute(mine, "pb", [(i, i ^ 1) for i in range(pb_size)])
+    gathered = jnp.concatenate([mine, other], 0)
+    phases = phases_of(kpoint_coords, vectors).reshape(2, local_k, vectors)
     if ka_size == count:
-        parts = ring_of(g_wannier[0], "ka")
+        parts = [g_wannier[0], ring_step(g_wannier[0], "ka")]
         order = (ka - jnp.arange(count, dtype=jnp.int32)) % count
     else:
         whole = lax.all_gather(g_wannier, "ka", axis=2, tiled=True)[0]
         parts = jnp.split(whole, count, 1)
         order = jnp.arange(count, dtype=jnp.int32)
-    wanted = target_owner[0, :, 0] * local_k + target_row[0]
+    weights, parts[1] = weights_of(phases, mode_vectors[0], pairs, parts[1])
+    while len(parts) < count:
+        parts.append(ring_step(parts[-1], "ka"))
+    owner, row = target_owner[0, :, 0], target_row[0]
+    wanted = ((pb - row // share) % 2 * ka_size + (ka - owner) % ka_size) * share + row % share
     choose = (wanted[:, None] == jnp.arange(total_k, dtype=jnp.int32)[None, :]).astype(jnp.bfloat16)
     fetched = jnp.dot(choose, gathered, preferred_element_type=jnp.float32)
     size = 2 * area
@@ -363,9 +341,6 @@
     e_there = fetched[:, size : size + bands]
     mask_there = fetched[:, size + bands : size + 2 * bands]
 
-    weights = weights_of(
-        phases_of(kpoint_coords, vectors).reshape(2, local_k, vectors), mode_vectors[0], pairs
-    )
     early = early_sums(order, parts[:-1], weights, area)
     rot_here = rotations.reshape(local_k, 2, bands, bands)
     right = jnp.transpose(rot_here, (0, 3, 1, 2)).reshape(local_k, bands, 2 * bands)

time: 122 us -> 104 us (0.85)
  Pallas kernels: 67.5 us -> 46.6 us
  local copies, waits for them, and re-layouts: 15.3 us -> 10.8 us
  waiting for transfers between devices: 19.4 us -> 23.7 us
  starting transfers between devices: 4.26 us -> 7.77 us
    pallas_call x1 -> x0, Pallas kernels: 22.4 us -> none  [gather_rows(): pl.pallas_call(functools.partial(rows_kernel, sizes), in_specs=[pl.BlockS...]
    ppermute x3 -> x7, waiting for transfers between devices: 19.4 us -> 23.7 us  [the longest x3 22.2 us: ring_step(): return lax.ppermute(array, axis, [(i, (i + 1) % size) for i in range(size)])]
    another operation x4 -> x3, other arithmetic: 6.8 us -> 2.92 us  [the longest x2 2.8 us: weights_of(): both = jnp.stack([lanes_of(real, imag), lanes_of(-imag, real)])]
    ppermute x3 -> x7, starting transfers between devices: 4.26 us -> 7.77 us  [the longest x3 7.01 us: from_each(): lax.ppermute(array, axis, [(i, (i + hop) % size) for i in range(size)])]
    unnamed x50 -> x26, local copies, waits for them, and re-layouts: 7.79 us -> 4.79 us
    convert_element_type x0 -> x1, other arithmetic: none -> 2.96 us  [weights_of(): imag = (cos * vec[1] + sin * vec[0]).astype(jnp.bfloat16)]
    neg x0 -> x1, other arithmetic: none -> 2.25 us  [weights_of(): both = jnp.stack([lanes_of(real, imag), lanes_of(-imag, real)])]
    pad x1, local copies, waits for them, and re-layouts: 2.51 us -> 0.55 us  [weights_of(): both = jnp.pad(both, ((0, 0), (0, 0), (0, LANES - pairs * vectors), (0, 0)))]
  transfers between devices with their start and end apart: 3 -> 7, of which waited for: 2 -> 3; matrix products, arithmetic and copies ran while one was open for 19% -> 17% of each run, Pallas kernels for 30% -> 14%
where the time goes in v6:
time: 104 us; the launch traced here: 103 us
  Pallas kernels  46.6 us (45%)
  waiting for transfers between devices  23.7 us (23%)
  other arithmetic  13.1 us (13%)
  local copies, waits for them, and re-layouts  10.8 us (10%)
  starting transfers between devices  7.77 us (7%)
    pallas_call x1, Pallas kernels, pair_sums(): pl.pallas_call(functools.partial(pair_kernel, bands=bands), in_specs=[sme...  23.2 us
    ppermute x3, waiting for transfers between devices, ring_step(): return lax.ppermute(array, axis, [(i, (i + 1) % size) for i in range(size)])  22.2 us
    pallas_call x1, Pallas kernels, early_sums(): pl.pallas_call(functools.partial(early_kernel, area=area), in_specs=[pl.B...  14.5 us
    pallas_call x1, Pallas kernels, both_sums(): pl.pallas_call(functools.partial(sum_kernel, sizes, scales), in_specs=[pl...  8.84 us
    ppermute x3, starting transfers between devices, from_each(): lax.ppermute(array, axis, [(i, (i + hop) % size) for i in range(size)])  7.01 us
    unnamed x26, local copies, waits for them, and re-layouts  4.79 us
    convert_element_type x1, other arithmetic, weights_of(): imag = (cos * vec[1] + sin * vec[0]).astype(jnp.bfloat16)  2.96 us
    another operation x2, other arithmetic, weights_of(): both = jnp.stack([lanes_of(real, imag), lanes_of(-imag, real)])  2.8 us
  transfers between devices with their start and end apart: 7, of which 3 were waited for; matrix products, arithmetic and copies ran while one was open for 17% of the time, Pallas kernels for 14%

profile of v6, /device:TPU:0, one launch (start us, length us, event | category | flops | bytes accessed | tf_op | source)
XLA Modules:
  0.0 103.1 jit_solution(5076386979277011344)
XLA Ops:
  0.6 0.0 copy-start.6
  0.6 0.0 copy-start.7
  0.7 0.0 copy-start.8
  0.7 0.8 slice_bitcast_fusion.3
  1.4 0.1 fusion.8
  1.5 1.0 concatenate.32
  2.5 3.1 %collective-permute-start.3 = (bf16[8,3280]{1,0:T(8,128)(2,1)S(1)}, bf16[8,3280]{1,0:T(8,128)(2,1)S(1)}, u32[]{:S(2)}, u32[]{:S(2)}) collective-permute-start(bf16[8,3280]{1,0:T(8,128)(2,1)S(1)} %get-tuple-element.15), channel_id=1, source_target_pairs={{0,4},{4,8},{8,12},{12,0},{1,5},{5,9},{9,13},{13,1},{2,6},{6,10},{... | collective-permute-start | bytes 157448 | tf_op jit(solution)/shard_map/ppermute | solution.py:292
  5.6 2.6 %collective-permute-start.4 = (bf16[8,3280]{1,0:T(8,128)(2,1)S(1)}, bf16[8,3280]{1,0:T(8,128)(2,1)S(1)}, u32[]{:S(2)}, u32[]{:S(2)}) collective-permute-start(bf16[8,3280]{1,0:T(8,128)(2,1)S(1)} %get-tuple-element.15), channel_id=1, source_target_pairs={{0,8},{4,12},{8,0},{12,4},{1,9},{5,13},{9,1},{13,5},{2,10},{6,14},... | collective-permute-start | bytes 157448 | tf_op jit(solution)/shard_map/ppermute | solution.py:292
  8.2 1.3 %collective-permute-start.5 = (bf16[8,3280]{1,0:T(8,128)(2,1)S(1)}, bf16[8,3280]{1,0:T(8,128)(2,1)S(1)}, u32[]{:S(2)}, u32[]{:S(2)}) collective-permute-start(bf16[8,3280]{1,0:T(8,128)(2,1)S(1)} %get-tuple-element.15), channel_id=1, source_target_pairs={{0,12},{4,0},{8,4},{12,8},{1,13},{5,1},{9,5},{13,9},{2,14},{6,2},{... | collective-permute-start | bytes 157448 | tf_op jit(solution)/shard_map/ppermute | solution.py:292
  9.5 0.7 collective-permute-start
  10.2 0.8 divide_select_fusion.up_ref
  11.0 0.8 convert_bitcast_fusion
  11.8 0.8 slice_bitcast_fusion.6
  12.6 0.1 cosine_convert_fusion
  12.7 0.1 maximum_convert_fusion
  12.8 0.1 slice_bitcast_fusion.1
  12.9 0.1 copy.18
  13.0 0.1 copy.16
  13.0 0.7 broadcast_add_fusion
  13.7 0.7 fusion.12
  14.4 0.1 select_maximum_fusion
  14.5 0.1 select_maximum_fusion.1
  14.6 3.0 %add_convert_fusion = (bf16[2,2,15,8,16,60]{5,3,4,2,1,0:T(8,128)(2,1)}, bf16[2,2,15,8,16,60]{5,3,4,2,1,0:T(8,128)(2,1)}) fusion(f32[2,2,15,60]{3,2,1,0:T(8,128)S(1)} %copy.19, f32[8,16]{0,1:T(8,128)S(1)} %copy.18, f32[2,2,15,60]{3,2,1,0:T(8,128)S(1)} %copy.17, f32[8,16]{0,1:T(8,128)S(1)} %copy.16), kind=kLoop, calls=%fused_computation.3 | loop fusion | flops 3686400 | bytes 1873024 | tf_op jit(solution)/shard_map/convert_element_type | solution.py:276
  17.6 0.0 copy-done.8
  17.6 0.1 select_maximum_fusion.2
  17.6 0.0 copy-done.6
  17.6 0.5 reshape.195
  18.1 0.3 copy.20
  18.5 0.2 reshape.196.right_ref
  18.7 0.0 collective-permute-done.3
  18.7 0.0 collective-permute-done.4
  18.7 0.0 collective-permute-done.5
  18.7 0.1 collective-permute-start.6
  18.8 1.4 %collective-permute-done.6 = bf16[32,3280]{1,0:T(8,128)(2,1)S(1)} collective-permute-done((bf16[32,3280]{1,0:T(8,128)(2,1)S(1)}, bf16[32,3280]{1,0:T(8,128)(2,1)S(1)}, u32[]{:S(2)}, u32[]{:S(2)}) %collective-permute-start.6) | collective-permute-done | bytes 209952 | tf_op jit(solution)/shard_map/ppermute | solution.py:322
  20.3 0.2 fusion.6
  20.5 0.5 reshape.197
  21.0 8.6 %collective-permute-done.refs_2_ = bf16[8,48000]{1,0:T(8,128)(2,1)S(1)} collective-permute-done((bf16[8,48000]{1,0:T(8,128)(2,1)}, bf16[8,48000]{1,0:T(8,128)(2,1)S(1)}, u32[]{:S(2)}, u32[]{:S(2)}) %collective-permute-start) | collective-permute-done | bytes 768032 | tf_op jit(solution)/shard_map/ppermute | solution.py:286
  29.6 0.0 collective-permute-start.1
  29.6 0.2 copy.24
  29.8 0.3 neg.12
  30.2 0.2 copy.23
  30.4 0.9 maximum_bitcast_fusion
  31.2 0.2 reshape.198.left_ref
  31.4 0.1 fusion.23
  31.5 0.3 add_multiply_fusion
  31.9 2.3 %neg.11 = bf16[2,2,15,8,16,60]{5,3,4,2,1,0:T(8,128)(2,1)S(1)} negate(bf16[2,2,15,8,16,60]{5,3,4,2,1,0:T(8,128)(2,1)} %get-tuple-element.9) | non-fusion elementwise | flops 460800 | bytes 1843200 | tf_op jit(solution)/shard_map/neg | solution.py:278
  34.1 0.7 pad.34
  34.8 13.7 %collective-permute-done.1.refs_3_ = bf16[8,48000]{1,0:T(8,128)(2,1)S(1)} collective-permute-done((bf16[8,48000]{1,0:T(8,128)(2,1)S(1)}, bf16[8,48000]{1,0:T(8,128)(2,1)S(1)}, u32[]{:S(2)}, u32[]{:S(2)}) %collective-permute-start.1) | collective-permute-done | bytes 768032 | tf_op jit(solution)/shard_map/ppermute | solution.py:286
  48.5 0.0 collective-permute-start.2
  48.5 2.4 %fusion.5 = (bf16[1,2,2,15,8,16,128]{6,4,5,3,2,1,0:T(8,128)(2,1)S(1)}, bf16[1,2,2,15,8,16,128]{6,4,5,3,2,1,0:T(8,128)(2,1)S(1)}) fusion(bf16[2,2,15,8,16,60]{5,3,4,2,1,0:T(8,128)(2,1)S(1)} %copy-done.4, bf16[2,2,15,8,16,64]{5,3,4,2,1,0:T(8,128)(2,1)S(1)} %pad.34, bf16[2,2,15,8,16,60]{5,3,4,2,1,0:T(8,128)(2,1)S(1)} %neg.11), kind=kLoop, calls=%fused_computation.10 | loop fusion | flops 11796480 | bytes 6758400 | tf_op jit(solution)/shard_map/stack | solution.py:278
  50.9 0.4 pad_maximum_fusion
  51.3 0.0 copy-start.3
  51.3 0.5 pad.37
  51.9 0.6 copy-done.3
  52.4 14.5 %early.1.early_ref = bf16[8,1600,256]{2,1,0:T(8,128)(2,1)S(1)} custom-call(s32[4]{0:T(128)S(1)} %and_select_fusion.9.refs_0_.order_ref, bf16[8,48000]{1,0:T(8,128)(2,1)S(1)} %bitcast.55, bf16[8,48000]{1,0:T(8,128)(2,1)S(1)} %collective-permute-done.refs_2_, bf16[8,48000]{1,0:T(8,128)(2,1)S(1)} %collective-permute-done.1.refs_3_, ...), custom_call_target="tpu_custom_call" | custom-call | flops 5033164800 | bytes 10747904 | tf_op jit(solution)/shard_map/early/pallas_call | solution.py:94
  67.0 0.0 collective-permute-done.2.g_ref
  67.0 0.1 broadcast_in_dim.5.occ_ref
  67.1 0.1 broadcast_in_dim.4.keep_ref
  67.3 23.2 %pairs.1 = (f32[16,40,128]{2,1,0:T(8,128)S(1)}, f32[40,128]{1,0:T(8,128)S(1)}) custom-call(s32[4]{0:T(128)S(1)} %and_select_fusion.9.refs_0_.order_ref, bf16[8,48000]{1,0:T(8,128)(2,1)S(1)} %collective-permute-done.2.g_ref, bf16[4,256,2048]{2,1,0:T(8,128)(2,1)S(1)} %bitcast.53, bf16[8,1600,256]{2,1,0:T(8,128)(2,1)S(1)} %early.1.early_ref, ...), custom_call_target="tpu_custom_call" | custom-call | tf_op jit(solution)/shard_map/pairs/pallas_call | solution.py:175
  90.5 0.7 copy-done
  91.2 0.6 copy-done.2
  91.8 8.8 %sums.1 = (f32[16,40]{1,0:T(8,128)}, f32[1,60]{1,0:T(1,128)}) custom-call(f32[16,40,128]{2,1,0:T(8,128)} %copy-done, f32[16,40]{1,0:T(8,128)} %copy-done.1, f32[40,128]{1,0:T(8,128)} %copy-done.2), custom_call_target="tpu_custom_call" | custom-call | tf_op jit(solution)/shard_map/sums/pallas_call | solution.py:242
  100.7 1.3 %copy.31 = f32[16,40]{1,0:T(8,128)} copy(f32[16,40]{1,0:T(8,128)} %get-tuple-element.45) | data formatting | bytes 5120
  102.0 1.2 %copy.32 = f32[1,60]{1,0:T(1,128)} copy(f32[1,60]{1,0:T(1,128)} %get-tuple-element.46) | data formatting | bytes 480
  (26 shorter events, 0.2 us)
Async XLA Ops:
  0.6 17.0 %copy-start.6 = (bf16[16,3200]{1,0:T(8,128)(2,1)S(1)}, bf16[16,3200]{1,0:T(8,128)(2,1)}, u32[]{:S(2)}) copy-start(bf16[16,3200]{1,0:T(8,128)(2,1)} %param.13) | copy-start | bytes 307204
  0.6 17.5 %copy-start.7 = (bf16[16,40]{1,0:T(8,128)(2,1)S(1)}, bf16[16,40]{1,0:T(8,128)(2,1)}, u32[]{:S(2)}) copy-start(bf16[16,40]{1,0:T(8,128)(2,1)} %param.14) | copy-start | bytes 3844
  0.7 16.9 %copy-start.8 = (f32[1,60]{1,0:T(1,128)S(1)}, f32[1,60]{1,0:T(1,128)}, u32[]{:S(2)}) copy-start(f32[1,60]{1,0:T(1,128)} %param.12) | copy-start | bytes 724
  1.5 65.8 %copy-start.1 = (f32[16,40]{1,0:T(8,128)}, f32[16,40]{1,0:T(8,128)S(1)}, u32[]{:S(2)}) copy-start(f32[16,40]{1,0:T(8,128)S(1)} %get-tuple-element.34.mask_ref) | copy-start | bytes 7684
  2.5 16.2 %collective-permute-start.3 = (bf16[8,3280]{1,0:T(8,128)(2,1)S(1)}, bf16[8,3280]{1,0:T(8,128)(2,1)S(1)}, u32[]{:S(2)}, u32[]{:S(2)}) collective-permute-start(bf16[8,3280]{1,0:T(8,128)(2,1)S(1)} %get-tuple-element.15), channel_id=1, source_target_pairs={{0,4},{4,8},{8,12},{12,0},{1,5},{5,9},{9,13},{13,1},{2,6},{6,10},{... | collective-permute-start | bytes 157448 | tf_op jit(solution)/shard_map/ppermute | solution.py:292
  5.6 13.1 %collective-permute-start.4 = (bf16[8,3280]{1,0:T(8,128)(2,1)S(1)}, bf16[8,3280]{1,0:T(8,128)(2,1)S(1)}, u32[]{:S(2)}, u32[]{:S(2)}) collective-permute-start(bf16[8,3280]{1,0:T(8,128)(2,1)S(1)} %get-tuple-element.15), channel_id=1, source_target_pairs={{0,8},{4,12},{8,0},{12,4},{1,9},{5,13},{9,1},{13,5},{2,10},{6,14},... | collective-permute-start | bytes 157448 | tf_op jit(solution)/shard_map/ppermute | solution.py:292
  8.2 10.5 %collective-permute-start.5 = (bf16[8,3280]{1,0:T(8,128)(2,1)S(1)}, bf16[8,3280]{1,0:T(8,128)(2,1)S(1)}, u32[]{:S(2)}, u32[]{:S(2)}) collective-permute-start(bf16[8,3280]{1,0:T(8,128)(2,1)S(1)} %get-tuple-element.15), channel_id=1, source_target_pairs={{0,12},{4,0},{8,4},{12,8},{1,13},{5,1},{9,5},{13,9},{2,14},{6,2},{... | collective-permute-start | bytes 157448 | tf_op jit(solution)/shard_map/ppermute | solution.py:292
  9.5 20.1 %collective-permute-start = (bf16[8,48000]{1,0:T(8,128)(2,1)}, bf16[8,48000]{1,0:T(8,128)(2,1)S(1)}, u32[]{:S(2)}, u32[]{:S(2)}) collective-permute-start(bf16[8,48000]{1,0:T(8,128)(2,1)} %bitcast.54), channel_id=1, source_target_pairs={{0,4},{4,8},{8,12},{12,0},{1,5},{5,9},{9,13},{13,1},{2,6},{6,10},{... | collective-permute-start | bytes 2304008 | tf_op jit(solution)/shard_map/ppermute | solution.py:286
  18.7 1.5 %collective-permute-start.6 = (bf16[32,3280]{1,0:T(8,128)(2,1)S(1)}, bf16[32,3280]{1,0:T(8,128)(2,1)S(1)}, u32[]{:S(2)}, u32[]{:S(2)}) collective-permute-start(bf16[32,3280]{1,0:T(8,128)(2,1)S(1)} %pad_maximum_fusion.1), channel_id=1, source_target_pairs={{0,1},{1,0},{2,3},{3,2},{4,5},{5,4},{6,7},{7,6},{8,9},{9,8},{10,11... | collective-permute-start | bytes 629768 | tf_op jit(solution)/shard_map/ppermute | solution.py:322
  29.6 18.9 %collective-permute-start.1 = (bf16[8,48000]{1,0:T(8,128)(2,1)S(1)}, bf16[8,48000]{1,0:T(8,128)(2,1)S(1)}, u32[]{:S(2)}, u32[]{:S(2)}) collective-permute-start(bf16[8,48000]{1,0:T(8,128)(2,1)S(1)} %collective-permute-done.refs_2_), channel_id=1, source_target_pairs={{0,4},{4,8},{8,12},{12,0},{1,5},{5,9},{9,13},{13,1},{2,6},{6,10},{... | collective-permute-start | bytes 2304008 | tf_op jit(solution)/shard_map/ppermute | solution.py:286
  31.4 2.7 %copy-start.5 = (bf16[2,2,15,8,16,60]{5,3,4,2,1,0:T(8,128)(2,1)S(1)}, bf16[2,2,15,8,16,60]{5,3,4,2,1,0:T(8,128)(2,1)}, u32[]{:S(2)}) copy-start(bf16[2,2,15,8,16,60]{5,3,4,2,1,0:T(8,128)(2,1)} %get-tuple-element.8) | copy-start | bytes 2764804
  31.8 16.6 %copy-start.4 = (bf16[2,2,15,8,16,60]{5,3,4,2,1,0:T(8,128)(2,1)S(1)}, bf16[2,2,15,8,16,60]{5,3,4,2,1,0:T(8,128)(2,1)}, u32[]{:S(2)}) copy-start(bf16[2,2,15,8,16,60]{5,3,4,2,1,0:T(8,128)(2,1)} %get-tuple-element.9) | copy-start | bytes 2764804
  48.5 18.5 %collective-permute-start.2 = (bf16[8,48000]{1,0:T(8,128)(2,1)S(1)}, bf16[8,48000]{1,0:T(8,128)(2,1)S(1)}, u32[]{:S(2)}, u32[]{:S(2)}) collective-permute-start(bf16[8,48000]{1,0:T(8,128)(2,1)S(1)} %collective-permute-done.1.refs_3_), channel_id=1, source_target_pairs={{0,4},{4,8},{8,12},{12,0},{1,5},{5,9},{9,13},{13,1},{2,6},{6,10},{... | collective-permute-start | bytes 2304008 | tf_op jit(solution)/shard_map/ppermute | solution.py:286
  51.3 1.1 %copy-start.3 = (bf16[1,8,48000]{2,1,0:T(8,128)(2,1)S(1)}, bf16[1,8,48000]{2,1,0:T(8,128)(2,1)}, u32[]{:S(2)}) copy-start(bf16[1,8,48000]{2,1,0:T(8,128)(2,1)} %param.10) | copy-start | bytes 2304004
  90.5 0.7 copy-start
  91.2 0.6 copy-start.2

commit v7 on v6

--- a/solution.py
+++ b/solution.py
@@ -316,6 +316,9 @@
     count = modes // pairs
     mask_here = window_mask(band_window, bands)
     packed = jnp.concatenate([rotations, energies, mask_here.astype(jnp.bfloat16)], 1)
+    if ka_size == count:
+        behind = ring_step(g_wannier[0], "ka")
+        packed, behind = lax.optimization_barrier((packed, behind))
     share = local_k // 2
     mine = lax.dynamic_slice_in_dim(packed, pb % 2 * share, share, 0)
     mine = jnp.concatenate(from_each(mine, "ka"), 0)
@@ -323,7 +326,7 @@
     gathered = jnp.concatenate([mine, other], 0)
     phases = phases_of(kpoint_coords, vectors).reshape(2, local_k, vectors)
     if ka_size == count:
-        parts = [g_wannier[0], ring_step(g_wannier[0], "ka")]
+        parts = [g_wannier[0], behind]
         order = (ka - jnp.arange(count, dtype=jnp.int32)) % count
     else:
         whole = lax.all_gather(g_wannier, "ka", axis=2, tiled=True)[0]

time: 104 us -> 109 us (1.048)
  local copies, waits for them, and re-layouts: 10.8 us -> 16.8 us
  starting transfers between devices: 7.77 us -> 13.3 us
  waiting for transfers between devices: 23.7 us -> 18.3 us
  Pallas kernels: 46.6 us -> 45.1 us
    ppermute x3, starting transfers between devices: 0.68 us -> 9.35 us  [ring_step(): return lax.ppermute(array, axis, [(i, (i + 1) % size) for i in range(size)])]
    ppermute x3, waiting for transfers between devices: 22.2 us -> 16.9 us  [ring_step(): return lax.ppermute(array, axis, [(i, (i + 1) % size) for i in range(size)])]
    ppermute x3, starting transfers between devices: 7.01 us -> 3.87 us  [from_each(): lax.ppermute(array, axis, [(i, (i + hop) % size) for i in range(size)])]
    unnamed x26 -> x20, local copies, waits for them, and re-layouts: 4.79 us -> 7.1 us
    convert_element_type x1, other arithmetic: 2.96 us -> 1.09 us  [weights_of(): imag = (cos * vec[1] + sin * vec[0]).astype(jnp.bfloat16)]
    transpose x1, other arithmetic: 0.88 us -> 2.69 us  [shards(): left = jnp.transpose(left, (0, 3, 1, 2)).reshape(local_k, bands, 2 * bands)]
    pad x1, local copies, waits for them, and re-layouts: 0.55 us -> 2.28 us  [weights_of(): both = jnp.pad(both, ((0, 0), (0, 0), (0, LANES - pairs * vectors), (0, 0)))]
    neg x1, other arithmetic: 2.25 us -> 0.69 us  [weights_of(): both = jnp.stack([lanes_of(real, imag), lanes_of(-imag, real)])]
  transfers between devices with their start and end apart: 7 -> 7, of which waited for: 3 -> 3; matrix products, arithmetic and copies ran while one was open for 17% -> 22% of each run, Pallas kernels for 14% -> 13%
where the time goes in v7:
time: 109 us; the launch traced here: 108 us
  Pallas kernels  45.1 us (41%)
  waiting for transfers between devices  18.3 us (17%)
  local copies, waits for them, and re-layouts  16.8 us (15%)
  other arithmetic  13.5 us (12%)
  starting transfers between devices  13.3 us (12%)
    pallas_call x1, Pallas kernels, pair_sums(): pl.pallas_call(functools.partial(pair_kernel, bands=bands), in_specs=[sme...  23.2 us
    ppermute x3, waiting for transfers between devices, ring_step(): return lax.ppermute(array, axis, [(i, (i + 1) % size) for i in range(size)])  16.9 us
    pallas_call x1, Pallas kernels, early_sums(): pl.pallas_call(functools.partial(early_kernel, area=area), in_specs=[pl.B...  14.5 us
    ppermute x3, starting transfers between devices, ring_step(): return lax.ppermute(array, axis, [(i, (i + 1) % size) for i in range(size)])  9.35 us
    pallas_call x1, Pallas kernels, both_sums(): pl.pallas_call(functools.partial(sum_kernel, sizes, scales), in_specs=[pl...  7.32 us
    unnamed x20, local copies, waits for them, and re-layouts  7.1 us
    ppermute x3, starting transfers between devices, from_each(): lax.ppermute(array, axis, [(i, (i + hop) % size) for i in range(size)])  3.87 us
    another operation x2, other arithmetic, weights_of(): both = jnp.stack([lanes_of(real, imag), lanes_of(-imag, real)])  2.82 us
  transfers between devices with their start and end apart: 7, of which 3 were waited for; matrix products, arithmetic and copies ran while one was open for 22% of the time, Pallas kernels for 13%

profile of v7, /device:TPU:0, one launch (start us, length us, event | category | flops | bytes accessed | tf_op | source)
XLA Modules:
  0.0 108.1 jit_solution(14838411637645057940)
XLA Ops:
  0.6 3.1 %collective-permute-start = (bf16[8,48000]{1,0:T(8,128)(2,1)}, bf16[8,48000]{1,0:T(8,128)(2,1)S(1)}, u32[]{:S(2)}, u32[]{:S(2)}) collective-permute-start(bf16[8,48000]{1,0:T(8,128)(2,1)} %bitcast.54), channel_id=1, source_target_pairs={{0,4},{4,8},{8,12},{12,0},{1,5},{5,9},{9,13},{13,1},{2,6},{6,10},{... | collective-permute-start | bytes 2304008 | tf_op jit(solution)/shard_map/ppermute | solution.py:286
  3.7 0.8 convert_bitcast_fusion
  4.6 0.8 slice_bitcast_fusion.6
  5.4 0.1 cosine_convert_fusion
  5.5 0.1 maximum_convert_fusion
  5.6 0.1 slice_bitcast_fusion.1
  5.6 0.1 copy.18
  5.7 0.1 copy.16
  5.8 0.8 slice_bitcast_fusion.3
  6.6 1.4 %reshape.195 = bf16[16,2,40,40]{3,2,1,0:T(8,128)(2,1)S(1)} reshape(bf16[16,3200]{1,0:T(8,128)(2,1)} %param.13) | data formatting | bytes 204800 | tf_op jit(solution)/shard_map/reshape | solution.py:348
  7.9 0.7 convert_element_type.73.e_ref
  8.6 0.1 fusion.8
  8.7 1.0 concatenate.30
  9.7 0.3 copy.20
  10.0 0.2 reshape.196.right_ref
  10.2 0.7 broadcast_add_fusion
  10.9 0.1 select_maximum_fusion
  11.0 0.1 select_maximum_fusion.1
  11.1 0.7 select_maximum_fusion.2
  11.8 0.7 fusion.12
  12.5 0.8 divide_select_fusion.up_ref
  13.2 1.1 %add_convert_fusion = (bf16[2,2,15,8,16,60]{5,3,4,2,1,0:T(8,128)(2,1)S(1)}, bf16[2,2,15,8,16,60]{5,3,4,2,1,0:T(8,128)(2,1)S(1)}) fusion(f32[2,2,15,60]{3,2,1,0:T(8,128)S(1)} %copy.19, f32[8,16]{0,1:T(8,128)S(1)} %copy.18, f32[2,2,15,60]{3,2,1,0:T(8,128)S(1)} %copy.17, f32[8,16]{0,1:T(8,128)S(1)} %copy.16), kind=kLoop, calls=%fused_computation.3 | loop fusion | flops 3686400 | bytes 1873024 | tf_op jit(solution)/shard_map/convert_element_type | solution.py:276
  14.3 8.7 %collective-permute-done.refs_2_ = bf16[8,48000]{1,0:T(8,128)(2,1)S(1)} collective-permute-done((bf16[8,48000]{1,0:T(8,128)(2,1)}, bf16[8,48000]{1,0:T(8,128)(2,1)S(1)}, u32[]{:S(2)}, u32[]{:S(2)}) %collective-permute-start) | collective-permute-done | bytes 768032 | tf_op jit(solution)/shard_map/ppermute | solution.py:286
  23.1 0.1 collective-permute-start.3
  23.2 2.3 %collective-permute-start.4 = (bf16[8,3280]{1,0:T(8,128)(2,1)S(1)}, bf16[8,3280]{1,0:T(8,128)(2,1)S(1)}, u32[]{:S(2)}, u32[]{:S(2)}) collective-permute-start(bf16[8,3280]{1,0:T(8,128)(2,1)S(1)} %get-tuple-element.19), channel_id=1, source_target_pairs={{0,8},{4,12},{8,0},{12,4},{1,9},{5,13},{9,1},{13,5},{2,10},{6,14},... | collective-permute-start | bytes 157448 | tf_op jit(solution)/shard_map/ppermute | solution.py:292
  25.5 1.5 %collective-permute-start.5 = (bf16[8,3280]{1,0:T(8,128)(2,1)S(1)}, bf16[8,3280]{1,0:T(8,128)(2,1)S(1)}, u32[]{:S(2)}, u32[]{:S(2)}) collective-permute-start(bf16[8,3280]{1,0:T(8,128)(2,1)S(1)} %get-tuple-element.19), channel_id=1, source_target_pairs={{0,12},{4,0},{8,4},{12,8},{1,13},{5,1},{9,5},{13,9},{2,14},{6,2},{... | collective-permute-start | bytes 157448 | tf_op jit(solution)/shard_map/ppermute | solution.py:292
  27.0 0.6 collective-permute-start.1
  27.5 0.7 neg.11
  28.2 0.7 pad.34
  28.9 2.5 %fusion.5 = (bf16[1,2,2,15,8,16,128]{6,4,5,3,2,1,0:T(8,128)(2,1)S(1)}, bf16[1,2,2,15,8,16,128]{6,4,5,3,2,1,0:T(8,128)(2,1)S(1)}) fusion(bf16[2,2,15,8,16,60]{5,3,4,2,1,0:T(8,128)(2,1)S(1)} %get-tuple-element.12, bf16[2,2,15,8,16,64]{5,3,4,2,1,0:T(8,128)(2,1)S(1)} %pad.34, bf16[2,2,15,8,16,60]{5,3,4,2,1,0:T(8,128)(2,1)S(1)} %neg.11), kind=kLoop, calls=%fused_computation.10 | loop fusion | flops 11796480 | bytes 6758400 | tf_op jit(solution)/shard_map/stack | solution.py:278
  31.4 0.4 pad_maximum_fusion
  31.8 2.3 %pad.37 = bf16[4,2,128,2048]{3,2,1,0:T(8,128)(2,1)} pad(bf16[4,2,120,2048]{3,2,1,0:T(8,128)(2,1)S(1)} %bitcast.56, bf16[]{:T(256)} %constant.126.clone.1), padding=0_0x0_0x0_8x0_0 | pad | bytes 8126466 | tf_op jit(solution)/shard_map/jit(_pad)/pad | solution.py:280
  34.0 0.0 collective-permute-done.3
  34.0 0.0 collective-permute-done.4
  34.1 0.0 collective-permute-done.5
  34.1 0.1 collective-permute-start.6
  34.2 1.4 %collective-permute-done.6 = bf16[32,3280]{1,0:T(8,128)(2,1)S(1)} collective-permute-done((bf16[32,3280]{1,0:T(8,128)(2,1)S(1)}, bf16[32,3280]{1,0:T(8,128)(2,1)S(1)}, u32[]{:S(2)}, u32[]{:S(2)}) %collective-permute-start.6) | collective-permute-done | bytes 209952 | tf_op jit(solution)/shard_map/ppermute | solution.py:325
  35.6 0.2 fusion.7
  35.9 0.5 reshape.197
  36.4 0.2 copy.24
  36.6 1.1 neg.12
  37.7 0.9 copy.23
  38.6 0.1 fusion.23
  38.7 8.1 %collective-permute-done.1.refs_3_ = bf16[8,48000]{1,0:T(8,128)(2,1)S(1)} collective-permute-done((bf16[8,48000]{1,0:T(8,128)(2,1)S(1)}, bf16[8,48000]{1,0:T(8,128)(2,1)S(1)}, u32[]{:S(2)}, u32[]{:S(2)}) %collective-permute-start.1) | collective-permute-done | bytes 768032 | tf_op jit(solution)/shard_map/ppermute | solution.py:286
  46.8 5.7 %collective-permute-start.2 = (bf16[8,48000]{1,0:T(8,128)(2,1)S(1)}, bf16[8,48000]{1,0:T(8,128)(2,1)S(1)}, u32[]{:S(2)}, u32[]{:S(2)}) collective-permute-start(bf16[8,48000]{1,0:T(8,128)(2,1)S(1)} %collective-permute-done.1.refs_3_), channel_id=1, source_target_pairs={{0,4},{4,8},{8,12},{12,0},{1,5},{5,9},{9,13},{13,1},{2,6},{6,10},{... | collective-permute-start | bytes 2304008 | tf_op jit(solution)/shard_map/ppermute | solution.py:286
  52.5 2.7 %maximum_bitcast_fusion = bf16[16,40,2,40]{3,2,1,0:T(2,128)(2,1)} fusion(bf16[16,1,40,40]{2,1,3,0:T(2,128)(2,1)} %neg.12, bf16[16,1,40,40]{2,1,3,0:T(2,128)(2,1)} %copy.23), kind=kLoop, calls=%fused_computation.11 | loop fusion | flops 204800 | bytes 204800 | tf_op jit(solution)/shard_map/transpose | solution.py:351
  55.2 1.2 %reshape.198.left_ref = bf16[16,40,80]{2,1,0:T(8,128)(2,1)S(1)} reshape(bf16[16,40,2,40]{3,2,1,0:T(2,128)(2,1)} %maximum_bitcast_fusion) | data formatting | bytes 204800 | tf_op jit(solution)/shard_map/reshape | solution.py:351
  56.4 0.3 add_multiply_fusion
  56.7 0.0 copy-done.5
  56.7 0.0 copy-start
  56.7 2.2 %copy-done = bf16[4,2,128,2048]{3,2,1,0:T(8,128)(2,1)S(1)} copy-done((bf16[4,2,128,2048]{3,2,1,0:T(8,128)(2,1)S(1)}, bf16[4,2,128,2048]{3,2,1,0:T(8,128)(2,1)}, u32[]{:S(2)}) %copy-start) | copy-done | bytes 4194328
  58.9 14.5 %early.1.early_ref = bf16[8,1600,256]{2,1,0:T(8,128)(2,1)S(1)} custom-call(s32[4]{0:T(128)S(1)} %and_select_fusion.9.refs_0_.order_ref, bf16[8,48000]{1,0:T(8,128)(2,1)S(1)} %bitcast.55, bf16[8,48000]{1,0:T(8,128)(2,1)S(1)} %collective-permute-done.refs_2_, bf16[8,48000]{1,0:T(8,128)(2,1)S(1)} %collective-permute-done.1.refs_3_, ...), custom_call_target="tpu_custom_call" | custom-call | flops 5033164800 | bytes 10747904 | tf_op jit(solution)/shard_map/early/pallas_call | solution.py:94
  73.4 0.0 collective-permute-done.2.g_ref
  73.5 0.1 broadcast_in_dim.5.occ_ref
  73.6 0.1 broadcast_in_dim.4.keep_ref
  73.8 0.0 copy-done.3
  73.8 0.0 copy-done.1
  73.8 23.2 %pairs.1 = (f32[16,40,128]{2,1,0:T(8,128)S(1)}, f32[40,128]{1,0:T(8,128)S(1)}) custom-call(s32[4]{0:T(128)S(1)} %and_select_fusion.9.refs_0_.order_ref, bf16[8,48000]{1,0:T(8,128)(2,1)S(1)} %collective-permute-done.2.g_ref, bf16[4,256,2048]{2,1,0:T(8,128)(2,1)S(1)} %bitcast.53, bf16[8,1600,256]{2,1,0:T(8,128)(2,1)S(1)} %early.1.early_ref, ...), custom_call_target="tpu_custom_call" | custom-call | tf_op jit(solution)/shard_map/pairs/pallas_call | solution.py:175
  97.0 0.0 copy-start.2
  97.0 0.7 copy-done.2
  97.8 0.6 copy-done.4
  98.4 7.3 %sums.1 = (f32[16,40]{1,0:T(8,128)}, f32[1,60]{1,0:T(1,128)}) custom-call(f32[16,40,128]{2,1,0:T(8,128)} %copy-done.2, f32[16,40]{1,0:T(8,128)} %copy-done.3, f32[40,128]{1,0:T(8,128)} %copy-done.4), custom_call_target="tpu_custom_call" | custom-call | tf_op jit(solution)/shard_map/sums/pallas_call | solution.py:242
  105.7 1.3 %copy.31 = f32[16,40]{1,0:T(8,128)} copy(f32[16,40]{1,0:T(8,128)} %get-tuple-element.49) | data formatting | bytes 5120
  107.0 1.1 %copy.32 = f32[1,60]{1,0:T(1,128)} copy(f32[1,60]{1,0:T(1,128)} %get-tuple-element.50) | data formatting | bytes 480
  (20 shorter events, 0.2 us)
Async XLA Ops:
  0.6 22.5 %collective-permute-start = (bf16[8,48000]{1,0:T(8,128)(2,1)}, bf16[8,48000]{1,0:T(8,128)(2,1)S(1)}, u32[]{:S(2)}, u32[]{:S(2)}) collective-permute-start(bf16[8,48000]{1,0:T(8,128)(2,1)} %bitcast.54), channel_id=1, source_target_pairs={{0,4},{4,8},{8,12},{12,0},{1,5},{5,9},{9,13},{13,1},{2,6},{6,10},{... | collective-permute-start | bytes 2304008 | tf_op jit(solution)/shard_map/ppermute | solution.py:286
  8.7 65.0 %copy-start.3 = (f32[16,40]{1,0:T(8,128)}, f32[16,40]{1,0:T(8,128)S(1)}, u32[]{:S(2)}) copy-start(f32[16,40]{1,0:T(8,128)S(1)} %get-tuple-element.38.mask_ref) | copy-start | bytes 7684
  23.1 10.9 %collective-permute-start.3 = (bf16[8,3280]{1,0:T(8,128)(2,1)S(1)}, bf16[8,3280]{1,0:T(8,128)(2,1)S(1)}, u32[]{:S(2)}, u32[]{:S(2)}) collective-permute-start(bf16[8,3280]{1,0:T(8,128)(2,1)S(1)} %get-tuple-element.19), channel_id=1, source_target_pairs={{0,4},{4,8},{8,12},{12,0},{1,5},{5,9},{9,13},{13,1},{2,6},{6,10},{... | collective-permute-start | bytes 157448 | tf_op jit(solution)/shard_map/ppermute | solution.py:292
  23.2 10.9 %collective-permute-start.4 = (bf16[8,3280]{1,0:T(8,128)(2,1)S(1)}, bf16[8,3280]{1,0:T(8,128)(2,1)S(1)}, u32[]{:S(2)}, u32[]{:S(2)}) collective-permute-start(bf16[8,3280]{1,0:T(8,128)(2,1)S(1)} %get-tuple-element.19), channel_id=1, source_target_pairs={{0,8},{4,12},{8,0},{12,4},{1,9},{5,13},{9,1},{13,5},{2,10},{6,14},... | collective-permute-start | bytes 157448 | tf_op jit(solution)/shard_map/ppermute | solution.py:292
  25.5 8.6 %collective-permute-start.5 = (bf16[8,3280]{1,0:T(8,128)(2,1)S(1)}, bf16[8,3280]{1,0:T(8,128)(2,1)S(1)}, u32[]{:S(2)}, u32[]{:S(2)}) collective-permute-start(bf16[8,3280]{1,0:T(8,128)(2,1)S(1)} %get-tuple-element.19), channel_id=1, source_target_pairs={{0,12},{4,0},{8,4},{12,8},{1,13},{5,1},{9,5},{13,9},{2,14},{6,2},{... | collective-permute-start | bytes 157448 | tf_op jit(solution)/shard_map/ppermute | solution.py:292
  27.0 19.8 %collective-permute-start.1 = (bf16[8,48000]{1,0:T(8,128)(2,1)S(1)}, bf16[8,48000]{1,0:T(8,128)(2,1)S(1)}, u32[]{:S(2)}, u32[]{:S(2)}) collective-permute-start(bf16[8,48000]{1,0:T(8,128)(2,1)S(1)} %collective-permute-done.refs_2_), channel_id=1, source_target_pairs={{0,4},{4,8},{8,12},{12,0},{1,5},{5,9},{9,13},{13,1},{2,6},{6,10},{... | collective-permute-start | bytes 2304008 | tf_op jit(solution)/shard_map/ppermute | solution.py:286
  34.0 22.7 %copy-start.5 = (bf16[1,8,48000]{2,1,0:T(8,128)(2,1)S(1)}, bf16[1,8,48000]{2,1,0:T(8,128)(2,1)}, u32[]{:S(2)}) copy-start(bf16[1,8,48000]{2,1,0:T(8,128)(2,1)} %param.10) | copy-start | bytes 2304004
  34.1 1.5 %collective-permute-start.6 = (bf16[32,3280]{1,0:T(8,128)(2,1)S(1)}, bf16[32,3280]{1,0:T(8,128)(2,1)S(1)}, u32[]{:S(2)}, u32[]{:S(2)}) collective-permute-start(bf16[32,3280]{1,0:T(8,128)(2,1)S(1)} %pad_maximum_fusion.1), channel_id=1, source_target_pairs={{0,1},{1,0},{2,3},{3,2},{4,5},{5,4},{6,7},{7,6},{8,9},{9,8},{10,11... | collective-permute-start | bytes 629768 | tf_op jit(solution)/shard_map/ppermute | solution.py:325
  46.8 26.6 %collective-permute-start.2 = (bf16[8,48000]{1,0:T(8,128)(2,1)S(1)}, bf16[8,48000]{1,0:T(8,128)(2,1)S(1)}, u32[]{:S(2)}, u32[]{:S(2)}) collective-permute-start(bf16[8,48000]{1,0:T(8,128)(2,1)S(1)} %collective-permute-done.1.refs_3_), channel_id=1, source_target_pairs={{0,4},{4,8},{8,12},{12,0},{1,5},{5,9},{9,13},{13,1},{2,6},{6,10},{... | collective-permute-start | bytes 2304008 | tf_op jit(solution)/shard_map/ppermute | solution.py:286
  56.7 2.2 %copy-start = (bf16[4,2,128,2048]{3,2,1,0:T(8,128)(2,1)S(1)}, bf16[4,2,128,2048]{3,2,1,0:T(8,128)(2,1)}, u32[]{:S(2)}) copy-start(bf16[4,2,128,2048]{3,2,1,0:T(8,128)(2,1)} %pad.37) | copy-start | bytes 12582916
  58.9 14.8 %copy-start.1 = (bf16[4,2,128,2048]{3,2,1,0:T(8,128)(2,1)S(1)}, bf16[4,2,128,2048]{3,2,1,0:T(8,128)(2,1)}, u32[]{:S(2)}) copy-start(bf16[4,2,128,2048]{3,2,1,0:T(8,128)(2,1)} %pad.37) | copy-start | bytes 12582916
  97.0 0.7 copy-start.2
  97.8 0.6 copy-start.4
